TPU v7x, 32 devices: a whole 2x2x4 slice. The times are simulated.
32 devices in a mesh: row: 8 (over y, x, core), col: 4 (over z).
Axes of the slice: x: 2, y: 2, z: 4, core: 2. Of those that a mesh axis runs over, the one named last changes fastest.
Arguments:
- a_tile: bfloat16 [2048, 16384], P('row', 'col'), may hold values from -6 to 6
- b_tile: bfloat16 [16384, 26624], P('row', 'col'), may hold values from -0.046875 to 0.046875
- c_prior: bfloat16 [2048, 26624], P('row', 'col'), may hold values from -0.29882812 to 0.29882812
- sketch_matrix: bfloat16 [26624, 128], P('col'), may hold values from -0.0390625 to 0.0390625
- panel_ids: int32 [2], replicated, may hold values from 0 to 31
Outputs:
- c_out: bfloat16 [2048, 26624], P('row', 'col')
- sketch: float32 [2048, 128], P('row')
- predicted: float32 [2048, 128], P('row')
Inputs may be any that keep to these rules, and one draw needn't show every extreme that they name: `panel_ids`: the 2 ids may repeat.
All inputs are finite; a program needn't handle non-finite values.
Results may differ from a plain program's by a relative error of at most 0.0029.
Values may be sent and summed in bfloat16 or wider, within the bound.
No kernel may reach another device: no remote copies, remote signals or barrier semaphores. Data moves between devices by JAX's collectives and lax.ppermute only.
A program may use at most 128 MiB of HBM per device.

v0:
```python
import jax
import jax.numpy as jnp
from jax import lax
from jax.sharding import PartitionSpec as P

PANEL = 512
STEPS = 2


def broadcast(value, axis, source):
    kept = jnp.where(lax.axis_index(axis) == source, value, 0).astype(value.dtype)
    return lax.psum(kept, axis)


def locate_pieces(a_tile, b_tile, panel_ids, step):
    first_row = panel_ids[step] * PANEL
    a_width = a_tile.shape[1]
    b_height = b_tile.shape[0]
    a_owner = first_row // a_width
    b_owner = first_row // b_height
    a_piece = lax.dynamic_slice_in_dim(a_tile, first_row - a_owner * a_width, PANEL, 1)
    b_piece = lax.dynamic_slice_in_dim(b_tile, first_row - b_owner * b_height, PANEL, 0)
    return (a_piece, a_owner, b_piece, b_owner)


def spread_activations(a_piece, a_owner):
    return broadcast(a_piece, "col", a_owner)


def spread_weights(b_piece, b_owner):
    return broadcast(b_piece, "row", b_owner)


def panel_terms(a_panel, b_panel, sketch_matrix):
    product = jnp.dot(a_panel, b_panel, preferred_element_type=jnp.float32)
    local_sketch = jnp.dot(b_panel, sketch_matrix, preferred_element_type=jnp.float32)
    predicted_term = jnp.dot(
        a_panel.astype(jnp.float32), local_sketch, precision=lax.Precision.HIGHEST
    )
    return (product, predicted_term)


def per_device(a_tile, b_tile, c_prior, sketch_matrix, panel_ids):
    located = [locate_pieces(a_tile, b_tile, panel_ids, step) for step in range(STEPS)]
    a_panels = [spread_activations(entry[0], entry[1]) for entry in located]
    b_panels = [spread_weights(entry[2], entry[3]) for entry in located]
    running = c_prior.astype(jnp.float32)
    predicted_part = jnp.zeros((c_prior.shape[0], sketch_matrix.shape[1]), jnp.float32)
    for step in range(STEPS):
        product, predicted_term = panel_terms(a_panels[step], b_panels[step], sketch_matrix)
        running = running + product
        predicted_part = predicted_part + predicted_term
    c_out = running.astype(jnp.bfloat16)
    local_sketch = jnp.dot(c_out, sketch_matrix, preferred_element_type=jnp.float32)
    sketch, predicted = lax.psum((local_sketch, predicted_part), "col")
    return (c_out, sketch, predicted)


def solution(mesh):
    placed = (P("row", "col"), P("row", "col"), P("row", "col"), P("col", None), P())
    return jax.shard_map(
        per_device,
        mesh=mesh,
        in_specs=placed,
        out_specs=(P("row", "col"), P("row", None), P("row", None)),
        check_vma=False,
    )
```

profile of v0, /device:TPU:0, one launch (start us, length us, event | category | flops | bytes accessed | tf_op | source)
XLA Modules:
  0.0 308.6 jit_solution(11565316820246553004)
XLA Ops:
  7.2 0.0 copy-start
  7.2 0.0 all-reduce.9.cloned.1.call-start
  7.2 1.4 fusion.1
  10.0 10.4 %dynamic-slice_select_fusion = (bf16[512,6656]{1,0:T(8,128)(2,1)}, bf16[512,6656]{1,0:T(8,128)(2,1)}) fusion(bf16[2048,6656]{1,0:T(8,128)(2,1)} %param.6, s32[]{:T(128)S(6)} %select_n.68, pred[]{:T(512)S(6)} %eq.15, s32[]{:T(128)S(6)} %select_n.60, pred[]{:T(512)S(6)} %eq.13), kind=kLoop, calls=%fused_computation.3 | loop fusion | flops 6815744 | bytes 27262986 | tf_op jit(solution)/shard_map/jit(_where)/select_n | solution.py:11
  20.4 0.0 all-reduce.9.cloned.1.call-update
  20.4 0.0 all-reduce.11.cloned.1.call-start
  20.5 1.9 dynamic-slice_select_fusion.2
  22.5 0.0 all-reduce.11.cloned.1.call-update
  22.5 0.0 all-reduce.7.cloned.1.call-start
  22.5 184.9 %all-reduce.9.cloned.1.call-done = (bf16[512,6656]{1,0:T(8,128)(2,1)}, bf16[512,6656]{1,0:T(8,128)(2,1)}) async-done(((bf16[512,6656]{1,0:T(8,128)(2,1)}, bf16[512,6656]{1,0:T(8,128)(2,1)}), (bf16[512,6656]{1,0:T(8,128)(2,1)}, bf16[512,6656]{1,0:T(8,128)(2,1)})) %all-reduce.9.cloned.1.call-update) | async-done | bytes 13631504 | tf_op jit(solution)/shard_map/psum | solution.py:12
  207.4 0.0 copy-start.2
  207.4 0.0 copy-done
  207.4 5.0 %fusion.3 = f32[512,128]{1,0:T(8,128)S(1)} fusion(bf16[512,6656]{1,0:T(8,128)(2,1)} %get-tuple-element.5, bf16[6656,128]{1,0:T(8,128)(2,1)S(1)} %copy-done), kind=kOutput, calls=%fused_computation.10 | convolution fusion | flops 872415232 | bytes 8781824 | tf_op jit(solution)/shard_map/dot_general | solution.py:36
  212.4 0.0 copy-done.2
  212.4 1.9 fusion.5
  214.3 34.8 %all-reduce.11.cloned.1.call-done = (bf16[256,512]{1,0:T(8,128)(2,1)}, bf16[256,512]{1,0:T(8,128)(2,1)}) async-done(((bf16[256,512]{1,0:T(8,128)(2,1)}, bf16[256,512]{1,0:T(8,128)(2,1)}), (bf16[256,512]{1,0:T(8,128)(2,1)}, bf16[256,512]{1,0:T(8,128)(2,1)})) %all-reduce.11.cloned.1.call-update) | async-done | bytes 524304 | tf_op jit(solution)/shard_map/psum | solution.py:12
  249.1 0.0 slice-start
  249.1 1.5 fusion.4
  250.6 0.0 slice-start.1
  250.6 0.0 copy-start.3
  250.7 6.1 %convolution_add_fusion.1 = f32[256,6656]{1,0:T(8,128)S(1)} fusion(bf16[256,512]{1,0:T(8,128)(2,1)} %get-tuple-element.7, bf16[512,6656]{1,0:T(8,128)(2,1)} %get-tuple-element.5, bf16[256,6656]{1,0:T(8,128)(2,1)} %param.7), kind=kOutput, calls=%fused_computation.1 | convolution fusion | flops 1748238336 | bytes 17301504 | tf_op jit(solution)/shard_map/dot_general | solution.py:35
  256.7 0.0 slice-done
  256.7 0.0 slice-done.1
  256.7 0.0 copy-done.3
  256.8 1.9 fusion
  258.7 0.0 copy-start.1
  258.7 1.7 copy-done.1
  260.5 1.8 fusion.2
  262.2 1.0 convolution_add_fusion.2
  263.3 0.0 all-reduce.7.cloned.1.call-update
  263.3 35.6 %all-reduce.7.cloned.1.call-done = (f32[256,128]{1,0:T(8,128)}, f32[256,128]{1,0:T(8,128)}) async-done(((f32[256,128]{1,0:T(8,128)}, f32[256,128]{1,0:T(8,128)}), (f32[256,128]{1,0:T(8,128)}, f32[256,128]{1,0:T(8,128)})) %all-reduce.7.cloned.1.call-update) | async-done | bytes 262160 | tf_op jit(solution)/shard_map/psum | solution.py:55
  298.9 1.6 copy.14
  300.5 1.6 copy.15
  (1 shorter events, 0.0 us)
Async XLA Ops:
  7.2 200.2 %copy-start = (bf16[6656,128]{1,0:T(8,128)(2,1)S(1)}, bf16[6656,128]{1,0:T(8,128)(2,1)}, u32[]{:S(2)}) copy-start(bf16[6656,128]{1,0:T(8,128)(2,1)} %param.8) | copy-start | bytes 5111812
  7.2 200.2 %all-reduce.9.cloned.1.call-start = ((), (), s32[]{:S(2)}) async-start(), calls=%async_computation.1 | async-start | bytes 27262976 | tf_op jit(solution)/shard_map/psum | solution.py:12
  20.4 228.7 %all-reduce.11.cloned.1.call-start = ((), (), s32[]{:S(2)}) async-start(), calls=%async_computation.2 | async-start | bytes 1048576 | tf_op jit(solution)/shard_map/psum | solution.py:12
  22.5 276.5 %all-reduce.7.cloned.1.call-start = ((), (), s32[]{:S(2)}) async-start(), calls=%async_computation | async-start | bytes 524288 | tf_op jit(solution)/shard_map/psum | solution.py:55
  207.4 5.0 %copy-start.2 = (bf16[512,6656]{1,0:T(8,128)(2,1)S(1)}, bf16[512,6656]{1,0:T(8,128)(2,1)}, u32[]{:S(2)}) copy-start(bf16[512,6656]{1,0:T(8,128)(2,1)} %get-tuple-element.6) | copy-start | bytes 20447236
  249.1 7.6 %slice-start = ((s8[6815744]{0:T(1024)(128)(4,1)}), s8[4194304]{0:T(1024)(128)(4,1)S(1)}, s32[]{:S(2)}) async-start(s8[6815744]{0:T(1024)(128)(4,1)} %bitcast.16), calls=%async_computation.3 | async-start | bytes 8388608
  250.6 6.1 %slice-start.1 = ((s8[6815744]{0:T(1024)(128)(4,1)}), s8[2621440]{0:T(1024)(128)(4,1)S(1)}, s32[]{:S(2)}) async-start(s8[6815744]{0:T(1024)(128)(4,1)} %bitcast.16), calls=%async_computation.4 | async-start | bytes 5242880
  250.6 6.1 %copy-start.3 = (bf16[256,512]{1,0:T(8,128)(2,1)S(1)}, bf16[256,512]{1,0:T(8,128)(2,1)}, u32[]{:S(2)}) copy-start(bf16[256,512]{1,0:T(8,128)(2,1)} %get-tuple-element.8) | copy-start | bytes 786436
  258.7 1.8 copy-start.1
Sparse Core Ops, SparseCore 0:
  20.5 186.8 all-reduce.8
  210.5 38.5 all-reduce.10
  263.4 35.4 all-reduce.6
where the time goes:
time: 309 us
  waiting for transfers between devices  255 us (83%)
  matrix products  19.2 us (6%)
  between operations  15.3 us (5%)
  other arithmetic  12.3 us (4%)
  local copies, waits for them, and re-layouts  6.28 us (2%)
    psum x2, waiting for transfers between devices, broadcast(): return lax.psum(kept, axis)  220 us
    psum x1, waiting for transfers between devices, per_device(): sketch, predicted = lax.psum((local_sketch, predicted_part), 'col')  35.6 us
    select_n x2, other arithmetic, broadcast(): jnp.where(lax.axis_index(axis) == source, value, 0).astype(value.dtype)  12.3 us
    dot_general x2, matrix products, panel_terms(): product = jnp.dot(a_panel, b_panel, preferred_element_type=jnp.float32)  8 us
    dot_general x2, matrix products, panel_terms(): jnp.dot(b_panel, sketch_matrix, preferred_element_type=jnp.float32)  6.91 us
  transfers between devices with their start and end apart: 3, of which 3 were waited for; matrix products, arithmetic and copies ran while one was open for 3% of the time, Pallas kernels for 0%

commit v1 on v0

v1 whole, which is shorter than its diff:
```python
import functools

import jax
import jax.numpy as jnp
from jax import lax
from jax.experimental import pallas as pl
from jax.experimental.pallas import tpu as pltpu
from jax.sharding import PartitionSpec as P

PANEL = 512
STEPS = 2
CORES = 2
LANES = 128
WIDTHS = (256, 256)
C_MOST = 3
HEAD = 2
LAST_PIECE = 4
PARTS = 2

ANY = pl.BlockSpec(memory_space=pl.ANY)
SMEM = pl.BlockSpec(memory_space=pltpu.SMEM)
VMEM = pl.BlockSpec(memory_space=pltpu.VMEM)


def broadcast(value, axis, source):
    kept = jnp.where(lax.axis_index(axis) == source, value, 0).astype(value.dtype)
    return lax.psum(kept, axis)


def plain(a_tile, b_tile, c_prior, sketch_matrix, panel_ids):
    running = c_prior.astype(jnp.float32)
    predicted = jnp.zeros((c_prior.shape[0], sketch_matrix.shape[1]), jnp.float32)
    for step in range(STEPS):
        first = panel_ids[step] * PANEL
        a_owner, a_first = first // a_tile.shape[1], first % a_tile.shape[1]
        b_owner, b_first = first // b_tile.shape[0], first % b_tile.shape[0]
        a_panel = broadcast(lax.dynamic_slice_in_dim(a_tile, a_first, PANEL, 1), "col", a_owner)
        b_panel = broadcast(lax.dynamic_slice_in_dim(b_tile, b_first, PANEL, 0), "row", b_owner)
        running = running + jnp.dot(a_panel, b_panel, preferred_element_type=jnp.float32)
        part = jnp.dot(b_panel, sketch_matrix, preferred_element_type=jnp.float32)
        predicted = predicted + jnp.dot(
            a_panel.astype(jnp.float32), part, precision=lax.Precision.HIGHEST
        )
    c_out = running.astype(jnp.bfloat16)
    sketch = jnp.dot(c_out, sketch_matrix, preferred_element_type=jnp.float32)
    sketch, predicted = lax.psum((sketch, predicted), "col")
    return c_out, sketch, predicted


OWN, NEAR, ROW, DIST, A_OWNER, A_FIRST = (STEPS * i for i in range(6))
CORE = STEPS * 6


def aligned(x, m):
    return pl.multiple_of(x, m)


def copy(src, dst, sem):
    return pltpu.make_async_copy(src, dst, sem)


def place_of(chip, n_chips):
    shift = 1
    out = chip
    while shift < n_chips:
        out = out ^ (chip >> shift)
        shift += 1
    return out


def panel_chunk(b_ref, scal, s, core, half, chunk):
    start, width = chunk
    rows = pl.ds(aligned(scal[ROW + s], PANEL), PANEL)
    return b_ref.at[rows, pl.ds(aligned(core * half + start, LANES), width)]


def stage(b_ref, scal, half, chains, outs, bufs, load_sem, store_sem):
    mine = scal[CORE]
    outs = list(outs)
    spots = []
    for c, chunks in enumerate(chains):
        for i, chunk in enumerate(chunks):
            for which in range(2):
                out = outs.pop(0)
                for s in range(STEPS):
                    spots.append(((which, i, s), c, chunk, out))
    spots.sort(key=lambda spot: (spot[0][0], spot[0][1]))

    def each(act):
        for spot, c, chunk, out in spots:
            core = mine if spot[0] else 1 - mine
            s = spot[2]
            load = lambda: copy(
                panel_chunk(b_ref, scal, s, core, half, chunk),
                bufs[c].at[spot],
                load_sem[c].at[spot],
            )
            store = lambda: copy(bufs[c].at[spot], out.at[s], store_sem[c].at[spot])

            @pl.when(scal[OWN + s] == 1)
            def _():
                act(load, store)

    def start(load, store):
        load().start()

    def turn(load, store):
        load().wait()
        store().start()

    def finish(load, store):
        store().wait()

    each(start)
    each(turn)
    each(finish)


def prologue_kernel(n_row, half, chains, ids, b_ref, a_ref, scal, cand, *rest):
    n = 2 * sum(len(chunks) for chunks in chains)
    outs = rest[:n]
    a_buf, a_sem = rest[n : n + 2]
    bufs, load_sem, store_sem = (rest[n + 2 + i :: 3] for i in range(3))
    n_chips = n_row // CORES
    me = lax.axis_index("row")
    core = lax.rem(me, CORES)
    chip = lax.div(me, CORES)
    scal[CORE] = core
    for s in range(STEPS):
        first = ids[s] * PANEL
        owner = lax.div(first, b_ref.shape[0])
        owner_chip = lax.div(owner, CORES)
        ahead = place_of(chip, n_chips) - place_of(owner_chip, n_chips)
        ahead = jnp.where(core == 0, ahead, -ahead)
        scal[OWN + s] = (owner == me).astype(jnp.int32)
        scal[NEAR + s] = ((owner_chip == chip) & (owner != me)).astype(jnp.int32)
        scal[ROW + s] = lax.rem(first, b_ref.shape[0])
        scal[DIST + s] = jnp.where(ahead < 0, ahead + n_chips, ahead)
        scal[A_OWNER + s] = lax.div(first, a_ref.shape[1])
        scal[A_FIRST + s] = lax.rem(first, a_ref.shape[1])

    def a_load(s):
        cols = pl.ds(aligned(scal[A_FIRST + s], PANEL), PANEL)
        return copy(a_ref.at[:, cols], a_buf.at[:, pl.ds(s * PANEL, PANEL)], a_sem.at[s])

    for s in range(STEPS):
        a_load(s).start()
    stage(b_ref, scal, half, chains, outs, bufs, load_sem, store_sem)
    for s in range(STEPS):
        a_load(s).wait()
    out = copy(a_buf, cand, a_sem.at[0])
    out.start()
    out.wait()


def stage_kernel(half, chains, scal, b_ref, tok_in, *rest):
    n = 2 * sum(len(chunks) for chunks in chains)
    outs, rest = rest[:n], rest[n + 1 :]
    stage(b_ref, scal, half, chains, outs, *(rest[i::3] for i in range(3)))


def inject_kernel(first, done, scal, *refs):
    if done:
        return
    refs = list(refs)
    if not first:
        refs.pop(0)
    sib, own, tok_in, out, tok_out, buf, load_sem, store_sem = refs
    rows = PANEL // PARTS
    for act in ("load", "turn", "finish"):
        for flag, source in ((OWN, own), (NEAR, sib)):
            for s in range(STEPS):

                @pl.when(scal[flag + s] == 1)
                def _(source=source, s=s, act=act):
                    for p in range(PARTS):
                        part = pl.ds(p * rows, rows)
                        spot = (s, part)
                        load = lambda: copy(source.at[spot], buf.at[spot], load_sem.at[s, p])
                        store = lambda: copy(buf.at[spot], out.at[spot], store_sem.at[s, p])
                        if act == "load":
                            load().start()
                        elif act == "turn":
                            load().wait()
                            store().start()
                        else:
                            store().wait()


def pick_kernel(n_col, k, panels, scal, *refs):
    cand, out, tok_out, sem = refs[0], *refs[-3:]
    z = lax.axis_index("col")
    for i, s in enumerate(panels):
        away = z - scal[A_OWNER + s]
        away = jnp.where(away < 0, away + n_col, away)

        @pl.when(away == k)
        def _(i=i, s=s):
            cp = copy(
                cand.at[:, pl.ds(i * PANEL, PANEL)], out.at[:, pl.ds(s * PANEL, PANEL)], sem
            )
            cp.start()
            cp.wait()


def split3(x):
    hi = x.astype(jnp.bfloat16)
    rest = x - hi.astype(jnp.float32)
    mid = rest.astype(jnp.bfloat16)
    lo = (rest - mid.astype(jnp.float32)).astype(jnp.bfloat16)
    return hi, mid, lo


def fdot(a, b):
    return jnp.dot(a, b, preferred_element_type=jnp.float32)


def work_kernel(plan, ring, half, *refs):
    p_chunks, c_chunks, back, firsts, last = plan
    refs = list(refs)
    take = lambda n: [refs.pop(0) for _ in range(n)]
    scal, s_ref = take(2)
    chunks = sorted(set(p_chunks) | set(c_chunks))
    cands = {c: take(ring) for c in chunks}
    (tok_in,) = take(1)
    ps_in = None if firsts[0] else take(1)[0]
    if c_chunks or last:
        (a_ref,) = take(1)
    if c_chunks:
        c_ref, c_sib = take(2)
        sk_in, cout_in = (None, None) if firsts[1] else take(2)
        gots = take(len(back))
    tok_out, ps = take(2)
    if c_chunks:
        sk, cout = take(2)
        rets = take(len(c_chunks))
    b_buf, s_buf, c_buf, b_sem, s_sem, c_sem, o_sem, g_sem = take(8)
    mine = scal[CORE] * half
    theirs = (1 - scal[CORE]) * half
    rows = c_buf.shape[1] // CORES

    def load_b(i, s, which):
        width = chunks[i][1]
        return copy(
            cands[chunks[i]][which].at[s],
            b_buf.at[i, pl.ds(s * PANEL, PANEL), pl.ds(0, width)],
            b_sem.at[i, s],
        )

    def load_s(i):
        start, width = chunks[i]
        cols = pl.ds(aligned(mine + start, LANES), width)
        return copy(s_ref.at[cols, :], s_buf.at[i, pl.ds(0, width)], s_sem.at[i])

    def load_c(i):
        start, width = c_chunks[i]
        part = pl.ds(0, width)
        return (
            copy(
                c_ref.at[:, pl.ds(aligned(mine + start, LANES), width)],
                c_buf.at[i, pl.ds(0, rows), part],
                c_sem.at[i, 0],
            ),
            copy(
                c_sib.at[:, pl.ds(start, width)],
                c_buf.at[i, pl.ds(rows, rows), part],
                c_sem.at[i, 1],
            ),
        )

    def store_c(i):
        start, width = c_chunks[i]
        return copy(
            c_buf.at[i, pl.ds(0, rows), pl.ds(0, width)],
            cout.at[:, pl.ds(aligned(mine + start, LANES), width)],
            o_sem.at[i],
        )

    def store_got(i):
        start, width = back[i]
        return copy(
            gots[i], cout.at[:, pl.ds(aligned(theirs + start, LANES), width)], g_sem.at[i]
        )

    for i in range(len(chunks)):
        for s in range(STEPS):
            for which in range(ring):

                @pl.when(scal[DIST + s] == which)
                def _(i=i, s=s, which=which):
                    load_b(i, s, which).start()

        load_s(i).start()
    for i in range(len(c_chunks)):
        for cp in load_c(i):
            cp.start()
    for i in range(len(back)):
        store_got(i).start()
    if firsts[0]:
        ps[...] = jnp.zeros_like(ps)
    else:
        ps[...] = ps_in[...]
    if c_chunks:
        if firsts[1]:
            sk[...] = jnp.zeros_like(sk)
        else:
            sk[...] = sk_in[...]
    for i, chunk in enumerate(chunks):
        width = chunk[1]
        for s in range(STEPS):
            load_b(i, s, 0).wait()
        load_s(i).wait()
        b = b_buf[i, :, :width]
        sm = s_buf[i, :width, :]
        if chunk in c_chunks:
            k = c_chunks.index(chunk)
            for cp in load_c(k):
                cp.wait()
            c = c_buf[k, :, :width].astype(jnp.float32) + fdot(a_ref[...], b)
            c = c.astype(jnp.bfloat16)
            c_buf[k, :, :width] = c
            rets[k][...] = c[rows:]
            store_c(k).start()
            sk[...] += fdot(c, sm)
        if chunk in p_chunks:
            ps[...] += fdot(b, sm)
    if last:
        hi, mid, lo = split3(ps[...])
        a = a_ref[...]
        ps[: CORES * rows, :] = fdot(a, hi) + (fdot(a, mid) + fdot(a, lo))
    for i in range(len(c_chunks)):
        store_c(i).wait()
    for i in range(len(back)):
        store_got(i).wait()


def place_kernel(back, half, scal, *refs):
    gots, cout, sem = refs[: len(back)], refs[-2], refs[-1]
    theirs = (1 - scal[CORE]) * half
    copies = [
        copy(got, cout.at[:, pl.ds(aligned(theirs + start, LANES), width)], sem.at[i])
        for i, (got, (start, width)) in enumerate(zip(gots, back))
    ]
    for cp in copies:
        cp.start()
    for cp in copies:
        cp.wait()


def like(shape, dtype=jnp.bfloat16):
    return jax.ShapeDtypeStruct(shape, dtype)


def params(mb):
    return pltpu.CompilerParams(vmem_limit_bytes=mb * 2**20)


def call(kernel, **kw):
    cost = pl.CostEstimate(flops=1, bytes_accessed=1, transcendentals=0)
    return pl.pallas_call(kernel, cost_estimate=cost, **kw)


DMA = pltpu.SemaphoreType.DMA


def ring_form(n_row, n_col, a_tile, b_tile, c_prior, sketch_matrix, panel_ids):
    rows, wide = c_prior.shape
    half = wide // CORES
    sk_cols = sketch_matrix.shape[1]
    n_chips = n_row // CORES
    order = [i ^ (i >> 1) for i in range(n_chips)]
    place = [order.index(c) for c in range(n_chips)]
    follow = [order[(place[c] + 1) % n_chips] for c in range(n_chips)]
    before = [order[(place[c] - 1) % n_chips] for c in range(n_chips)]
    around = []
    for c in range(n_chips):
        around += [(CORES * c, CORES * follow[c]), (CORES * c + 1, CORES * before[c] + 1)]
    swap = [(d, d ^ 1) for d in range(n_row)]

    def spread(x):
        return lax.ppermute(x, "row", around)

    def exchange(x):
        return lax.ppermute(x, "row", swap)

    chains = [[] for _ in WIDTHS]
    at = turn = 0
    while at < half:
        width = WIDTHS[turn % len(WIDTHS)]
        if at + width > half:
            turn += 1
            continue
        chains[turn % len(WIDTHS)].append((at, width))
        at += width
        turn += 1
    n_chains = len(chains)
    heads = [chunks[:HEAD] for chunks in chains]
    tails = [chunks[HEAD:] for chunks in chains]

    def staged(parts):
        shapes, specs = [], []
        for chunks, width in zip(parts, WIDTHS):
            shapes += [like((STEPS, PANEL, width))] * (2 * len(chunks))
            specs += [ANY] * (2 * len(chunks))
        return tuple(shapes), tuple(specs)

    def unpack(arrays, parts):
        arrays = list(arrays)
        return [
            [(exchange(arrays.pop(0)), arrays.pop(0)) for _ in chunks] for chunks in parts
        ]

    def stage_scratch(parts):
        out = []
        for chunks, width in zip(parts, WIDTHS):
            n = len(chunks)
            out += [
                pltpu.VMEM((2, n, STEPS, PANEL, width), jnp.bfloat16),
                DMA((2, n, STEPS)),
                DMA((2, n, STEPS)),
            ]
        return out

    scal, cand, *staged_heads = call(
        functools.partial(prologue_kernel, n_row, half, heads),
        out_shape=(like((CORE + 1,), jnp.int32), like((rows, STEPS * PANEL))) + staged(heads)[0],
        in_specs=[SMEM, ANY, ANY],
        out_specs=(SMEM, ANY) + staged(heads)[1],
        scratch_shapes=[pltpu.VMEM((rows, STEPS * PANEL), jnp.bfloat16), DMA((STEPS,))]
        + stage_scratch(heads),
        compiler_params=params(62),
    )(panel_ids, b_tile, a_tile)

    feeds = unpack(staged_heads, heads)
    tok = jnp.zeros((8, LANES), jnp.float32)

    def inject(tok, c, t, recv, feed):
        first = recv is None
        args = [scal] + ([] if first else [recv]) + ([] if feed is None else list(feed)) + [tok]
        aliases = {} if first else {1: 0}
        return call(
            functools.partial(inject_kernel, first, feed is None),
            out_shape=(like((STEPS, PANEL, WIDTHS[c])), like(tok.shape, tok.dtype)),
            in_specs=[SMEM] + [ANY] * (len(args) - 1),
            out_specs=(ANY, ANY),
            scratch_shapes=[
                pltpu.VMEM((STEPS, PANEL, WIDTHS[c]), jnp.bfloat16),
                DMA((STEPS, PARTS)),
                DMA((STEPS, PARTS)),
            ],
            input_output_aliases=aliases,
            compiler_params=params(4),
        )(*args)

    sends = [[] for _ in chains]
    flying = [None] * n_chains
    for c in range(n_chains):
        sent, tok = inject(tok, c, 0, None, feeds[c][0])
        sends[c].append(sent)
        flying[c] = spread(sent)
    def pick(tok, k, panels, piece, mine):
        args = [scal, piece] + ([] if mine is None else [mine]) + [tok]
        return call(
            functools.partial(pick_kernel, n_col, k, panels),
            out_shape=(like(cand.shape), like(tok.shape, tok.dtype)),
            in_specs=[SMEM, ANY] + ([] if mine is None else [VMEM]) + [ANY],
            out_specs=(VMEM, ANY),
            scratch_shapes=[DMA],
            input_output_aliases={} if mine is None else {2: 0},
            compiler_params=params(4),
        )(*args)

    a_own, tok = pick(tok, 0, tuple(range(STEPS)), cand, None)
    c_other = exchange(
        lax.dynamic_slice_in_dim(c_prior, (1 - lax.axis_index("row") % CORES) * half, half, 1)
    )
    a_all = None
    pieces = []
    for k in sorted(range(1, n_col), key=lambda k: min(k, n_col - k)):
        if 2 * k == n_col:
            pieces += [(k, (s,)) for s in range(STEPS)]
        else:
            pieces.append((k, tuple(range(STEPS))))

    state = dict(ps=None, sk=None, cout=None, waiting=[])

    def work(tok, p_ids, c_ids, last=False):
        where = lambda cj: chains[cj[0]][cj[1]]
        p_chunks = [where(cj) for cj in p_ids]
        c_chunks = [where(cj) for cj in c_ids]
        ids = sorted(set(p_ids) | set(c_ids), key=where)
        n = len(ids)
        widest = max(where(cj)[1] for cj in ids)
        firsts = (state["ps"] is None, state["sk"] is None)
        back = []
        if c_ids:
            while len(state["waiting"]) > 2:
                back.append(state["waiting"].pop(0))
        args = [scal, sketch_matrix]
        specs = [SMEM, ANY]
        for c, j in ids:
            args += sends[c][j : j + n_chips]
            specs += [ANY] * n_chips
        aliases = {}
        args.append(tok)
        specs.append(ANY)
        outs = [like(tok.shape, tok.dtype), like((STEPS * PANEL, sk_cols), jnp.float32)]
        out_specs = [ANY, VMEM]
        if not firsts[0]:
            aliases[len(args)] = 1
            args.append(state["ps"])
            specs.append(VMEM)
        if c_ids or last:
            args.append(a_all)
            specs.append(VMEM)
        if c_ids:
            args += [c_prior, c_other]
            specs += [ANY, ANY]
            if not firsts[1]:
                aliases[len(args)] = 2
                aliases[len(args) + 1] = 3
                args += [state["sk"], state["cout"]]
                specs += [VMEM, ANY]
            args += [got for got, _ in back]
            specs += [VMEM] * len(back)
            outs += [like((CORES * rows, sk_cols), jnp.float32), like((rows, wide))]
            out_specs += [VMEM, ANY]
            outs += [like((rows, w)) for _, w in c_chunks]
            out_specs += [VMEM] * len(c_chunks)
        m = max(1, len(c_ids))
        plan = (p_chunks, c_chunks, [spot for _, spot in back], firsts, last)
        got = call(
            functools.partial(work_kernel, plan, n_chips, half),
            out_shape=tuple(outs),
            in_specs=specs,
            out_specs=tuple(out_specs),
            scratch_shapes=[
                pltpu.VMEM((n, STEPS * PANEL, widest), jnp.bfloat16),
                pltpu.VMEM((n, widest, sk_cols), jnp.bfloat16),
                pltpu.VMEM((m, CORES * rows, widest), jnp.bfloat16),
                DMA((n, STEPS)),
                DMA((n,)),
                DMA((m, CORES)),
                DMA((m,)),
                DMA((max(1, len(back)),)),
            ],
            input_output_aliases=aliases,
            compiler_params=params(16),
        )(*args)
        tok, state["ps"] = got[:2]
        if c_ids:
            state["sk"], state["cout"] = got[2:4]
            for ret, spot in zip(got[4:], c_chunks):
                state["waiting"].append((exchange(ret), spot))
        return tok

    p_todo, c_todo = [], []
    n_steps = [len(chunks) + n_chips - 2 for chunks in chains]
    for t in range(1, max(n_steps) + 1):
        if t == HEAD - 1:
            *staged_tails, tok = call(
                functools.partial(stage_kernel, half, tails),
                out_shape=staged(tails)[0] + (like(tok.shape, tok.dtype),),
                in_specs=[SMEM, ANY, ANY],
                out_specs=staged(tails)[1] + (ANY,),
                scratch_shapes=stage_scratch(tails),
                compiler_params=params(62),
            )(scal, b_tile, tok)
            feeds = [old + new for old, new in zip(feeds, unpack(staged_tails, tails))]
        for c in range(n_chains):
            if t > n_steps[c]:
                continue
            if t < len(chains[c]):
                sent, tok = inject(tok, c, t, flying[c], feeds[c][t])
            elif t < n_steps[c]:
                sent, tok = inject(tok, c, t, flying[c], None)
            else:
                sent = flying[c]
            sends[c].append(sent)
            if t < n_steps[c]:
                flying[c] = spread(sent)
            if t >= n_chips - 1:
                p_todo.append((c, t - n_chips + 1))
                c_todo.append((c, t - n_chips + 1))
            if c == n_chains - 1 and a_all is None:
                for k, panels in pieces[:1] if t < LAST_PIECE else pieces:
                    way = [(i, (i + k) % n_col) for i in range(n_col)]
                    piece = cand
                    if len(panels) == 1:
                        piece = cand[:, panels[0] * PANEL : (panels[0] + 1) * PANEL]
                    a_own, tok = pick(tok, k, panels, lax.ppermute(piece, "col", way), a_own)
                pieces = pieces[1:] if t < LAST_PIECE else []
                if not pieces:
                    a_all = jnp.concatenate([a_own, exchange(a_own)], 0)
            if t == max(n_steps) and all(len(sends[k]) > n_steps[k] for k in range(n_chains)):
                continue
            c_ids = c_todo[:C_MOST] if a_all is not None else []
            if c < n_chains - 1 and t <= min(n_steps):
                continue
            if p_todo or c_ids:
                tok = work(tok, p_todo, c_ids)
                p_todo, c_todo = [], c_todo[len(c_ids) :]
    tok = work(tok, p_todo, c_todo, True)

    back = state["waiting"]
    cout = call(
        functools.partial(place_kernel, [spot for _, spot in back], half),
        out_shape=like((rows, wide)),
        in_specs=[SMEM] + [VMEM] * len(back) + [ANY],
        out_specs=ANY,
        scratch_shapes=[DMA((len(back),))],
        input_output_aliases={len(back) + 1: 0},
        compiler_params=params(4),
    )(scal, *[got for got, _ in back], state["cout"])

    sk, ps = state["sk"], state["ps"]
    mine = jnp.concatenate([sk[:rows], ps[:rows]], 1)
    theirs = exchange(jnp.concatenate([sk[rows:], ps[rows : 2 * rows]], 1))
    total = mine + theirs
    z = lax.axis_index("col")
    share = rows // n_col
    shift = lambda k: [(i, (i + k) % n_col) for i in range(n_col)]
    cut = lambda i: lax.dynamic_slice_in_dim(total, (i % n_col) * share, share, 0)
    part = cut(z)
    for k in range(1, n_col):
        part = part + lax.ppermute(cut(z + k), "col", shift(k))
    full = jnp.zeros_like(total)
    full = lax.dynamic_update_slice_in_dim(full, part, z * share, 0)
    for k in range(1, n_col):
        full = lax.dynamic_update_slice_in_dim(
            full, lax.ppermute(part, "col", shift(k)), ((z - k) % n_col) * share, 0
        )
    return cout, full[:, :sk_cols], full[:, sk_cols:]


def solution(mesh):
    n_row, n_col = mesh.shape["row"], mesh.shape["col"]

    def per_device(a_tile, b_tile, c_prior, sketch_matrix, panel_ids):
        rows, wide = c_prior.shape
        chips = n_row // CORES
        fits = (
            n_row == CORES * chips
            and chips & (chips - 1) == 0
            and chips > 1
            and wide % (CORES * LANES) == 0
            and wide // CORES >= 4 * sum(WIDTHS)
            and (wide // CORES) % min(WIDTHS) == 0
            and b_tile.shape[0] % PANEL == 0
            and a_tile.shape[1] % PANEL == 0
            and CORES * rows <= STEPS * PANEL
            and rows % (8 * n_col) == 0
        )
        if not fits:
            return plain(a_tile, b_tile, c_prior, sketch_matrix, panel_ids)
        return ring_form(n_row, n_col, a_tile, b_tile, c_prior, sketch_matrix, panel_ids)

    placed = (P("row", "col"), P("row", "col"), P("row", "col"), P("col", None), P())
    return jax.shard_map(
        per_device,
        mesh=mesh,
        in_specs=placed,
        out_specs=(P("row", "col"), P("row", None), P("row", None)),
        check_vma=False,
    )
```

time: 309 us -> 162 us (0.52)
  waiting for transfers between devices: 255 us -> 44.5 us
  Pallas kernels: 0 us -> 73.1 us
  starting transfers between devices: 0.12 us -> 29.3 us
  matrix products: 19.2 us -> 0 us
  between operations: 15.3 us -> 1.56 us
  other arithmetic: 12.3 us -> 0.07 us
  local copies, waits for them, and re-layouts: 6.28 us -> 13.4 us
    psum x3 -> x0, waiting for transfers between devices: 255 us -> none  [the longest x2 220 us: broadcast(): return lax.psum(kept, axis)]
    pallas_call x0 -> x32, Pallas kernels: none -> 73.1 us  [the longest x17 31.7 us: inject(): call(functools.partial(inject_kernel, first, feed is None), out_shape=(li...]
    ppermute x0 -> x56, waiting for transfers between devices: none -> 44.5 us  [the longest x17 27.1 us: spread(): return lax.ppermute(x, 'row', around)]
    ppermute x0 -> x56, starting transfers between devices: none -> 29.3 us  [the longest x29 7.62 us: exchange(): return lax.ppermute(x, 'row', swap)]
    dot_general x7 -> x0, matrix products: 19.2 us -> none  [the longest x2 8 us: panel_terms(): product = jnp.dot(a_panel, b_panel, preferred_element_type=jnp.float32)]
    select_n x2 -> x0, other arithmetic: 12.3 us -> none  [broadcast(): jnp.where(lax.axis_index(axis) == source, value, 0).astype(value.dtype)]
    unnamed x14 -> x69, local copies, waits for them, and re-layouts: 4.9 us -> 12.4 us
  transfers between devices with their start and end apart: 3 -> 56, of which waited for: 3 -> 24; matrix products, arithmetic and copies ran while one was open for 3% -> 0% of each run, Pallas kernels for 0% -> 40%
where the time goes in v1:
time: 162 us
  Pallas kernels  73.1 us (45%)
  waiting for transfers between devices  44.5 us (27%)
  starting transfers between devices  29.3 us (18%)
  local copies, waits for them, and re-layouts  13.4 us (8%)
    pallas_call x17, Pallas kernels, inject(): call(functools.partial(inject_kernel, first, feed is None), out_shape=(li...  31.7 us
    ppermute x17, waiting for transfers between devices, spread(): return lax.ppermute(x, 'row', around)  27.1 us
    pallas_call x7, Pallas kernels, work(): call(functools.partial(work_kernel, plan, n_chips, half), out_shape=tuple...  26.8 us
    unnamed x69, local copies, waits for them, and re-layouts  12.4 us
    ppermute x29, starting transfers between devices, exchange(): return lax.ppermute(x, 'row', swap)  7.62 us
    ppermute x4, starting transfers between devices, ring_form(): a_own, tok = pick(tok, k, panels, lax.ppermute(piece, 'col', way), a_own)  7.19 us
    ppermute x17, starting transfers between devices, spread(): return lax.ppermute(x, 'row', around)  6.63 us
    pallas_call x1, Pallas kernels, ring_form(): call(functools.partial(stage_kernel, half, tails), out_shape=staged(tails...  5.74 us
  transfers between devices with their start and end apart: 56, of which 24 were waited for; matrix products, arithmetic and copies ran while one was open for 0% of the time, Pallas kernels for 40%

profile of v1, /device:TPU:0, one launch (start us, length us, event | category | flops | bytes accessed | tf_op | source)
XLA Modules:
  0.0 161.9 jit_solution(3803189623267961342)
XLA Ops:
  0.6 4.7 %shard_map.76 = (s32[13]{0:T(128)}, bf16[256,1024]{1,0:T(8,128)(2,1)}, bf16[2,512,256]{2,1,0:T(8,128)(2,1)}, bf16[2,512,256]{2,1,0:T(8,128)(2,1)}, bf16[2,512,25...) custom-call(s32[2]{0:T(128)} %ids.1, ...), custom_call_target="tpu_custom_call" | custom-call | flops 1 | bytes 1 | tf_op jit(solution)/shard_map/pallas_call | solution.py:424
  9.4 2.1 %shard_map.77 = (bf16[2,512,256]{2,1,0:T(8,128)(2,1)}, f32[8,128]{1,0:T(8,128)S(1)}) custom-call(s32[13]{0:T(128)S(1)} %copy-done.21, bf16[2,512,256]{2,1,0:T(8,128)(2,1)S(1)} %collective-permute-done.refs_0_, bf16[2,512,256]{2,1,0:T(8,128)(2,1)S(1)} %copy-done.20, f32[8,128]{1,0:T(8,128)S(1)} %broadcast_in_dim.6.refs_2_), custom_call_target="tpu_custom_call" | custom-call | flops 1 | bytes 1 | tf_op jit(solution)/shard_map/pallas_call | solution.py:441
  13.0 2.1 %shard_map.78 = (bf16[2,512,256]{2,1,0:T(8,128)(2,1)}, f32[8,128]{1,0:T(8,128)S(1)}) custom-call(s32[13]{0:T(128)S(1)} %copy-done.21, bf16[2,512,256]{2,1,0:T(8,128)(2,1)S(1)} %collective-permute-done.3.refs_0_, bf16[2,512,256]{2,1,0:T(8,128)(2,1)S(1)} %copy-done.19, f32[8,128]{1,0:T(8,128)S(1)} %get-tuple-element.123.refs_2_), custom_call_target="tpu_custom_call" | custom-call | flops 1 | bytes 1 | tf_op jit(solution)/shard_map/pallas_call | solution.py:441
  15.5 2.6 %collective-permute-start.6 = (bf16[256,1024]{1,0:T(8,128)(2,1)}, bf16[256,1024]{1,0:T(8,128)(2,1)}, u32[]{:S(2)}, u32[]{:S(2)}) collective-permute-start(bf16[256,1024]{1,0:T(8,128)(2,1)} %get-tuple-element.120.refs_0_), channel_id=1, source_target_pairs={{0,1},{1,2},{2,3},{3,0},{4,5},{5,6},{6,7},{7,4},{8,9},{9,10},{10,1... | collective-permute-start | bytes 1572872 | tf_op jit(solution)/shard_map/ppermute | solution.py:591
  21.9 5.7 %shard_map.80 = (bf16[2,512,256]{2,1,0:T(8,128)(2,1)}, bf16[2,512,256]{2,1,0:T(8,128)(2,1)}, bf16[2,512,256]{2,1,0:T(8,128)(2,1)}, bf16[2,512,256]{2,1,0:T(8,128...) custom-call(s32[13]{0:T(128)} %get-tuple-element.114.scal.refs_0_, ...), custom_call_target="tpu_custom_call" | custom-call | flops 1 | bytes 1 | tf_op jit(solution)/shard_map/pallas_call | solution.py:561
  29.7 2.7 %shard_map.81 = (bf16[2,512,256]{2,1,0:T(8,128)(2,1)}, f32[8,128]{1,0:T(8,128)S(1)}) custom-call(s32[13]{0:T(128)S(1)} %copy-done.23, bf16[2,512,256]{2,1,0:T(8,128)(2,1)} %collective-permute-done.1.refs_0_, bf16[2,512,256]{2,1,0:T(8,128)(2,1)} %collective-permute-done.2.refs_1_, ...), custom_call_target="tpu_custom_call", output_to_operand_aliasing={{0}: (1, {})} | custom-call | flops 1 | bytes 1 | tf_op jit(solution)/shard_map/pallas_call | solution.py:441
  34.1 2.7 %shard_map.82 = (bf16[2,512,256]{2,1,0:T(8,128)(2,1)}, f32[8,128]{1,0:T(8,128)S(1)}) custom-call(s32[13]{0:T(128)S(1)} %copy-done.23, bf16[2,512,256]{2,1,0:T(8,128)(2,1)} %collective-permute-done.7.refs_0_, bf16[2,512,256]{2,1,0:T(8,128)(2,1)} %collective-permute-done.8.refs_1_, ...), custom_call_target="tpu_custom_call", output_to_operand_aliasing={{0}: (1, {})} | custom-call | flops 1 | bytes 1 | tf_op jit(solution)/shard_map/pallas_call | solution.py:441
  36.9 1.9 %collective-permute-start.11 = (bf16[256,1024]{1,0:T(8,128)(2,1)}, bf16[256,1024]{1,0:T(8,128)(2,1)}, u32[]{:S(2)}, u32[]{:S(2)}) collective-permute-start(bf16[256,1024]{1,0:T(8,128)(2,1)} %get-tuple-element.120.refs_0_), channel_id=1, source_target_pairs={{0,3},{1,0},{2,1},{3,2},{4,7},{5,4},{6,5},{7,6},{8,11},{9,8},{10,9... | collective-permute-start | bytes 1572872 | tf_op jit(solution)/shard_map/ppermute | solution.py:591
  42.9 2.7 %shard_map.84 = (bf16[2,512,256]{2,1,0:T(8,128)(2,1)}, f32[8,128]{1,0:T(8,128)S(1)}) custom-call(s32[13]{0:T(128)S(1)} %copy-done.23, bf16[2,512,256]{2,1,0:T(8,128)(2,1)} %collective-permute-done.4.refs_0_, bf16[2,512,256]{2,1,0:T(8,128)(2,1)} %collective-permute-done.5.refs_1_, ...), custom_call_target="tpu_custom_call", output_to_operand_aliasing={{0}: (1, {})} | custom-call | flops 1 | bytes 1 | tf_op jit(solution)/shard_map/pallas_call | solution.py:441
  46.0 1.5 collective-permute-done.12.refs_0_
  47.5 2.7 %shard_map.85 = (bf16[2,512,256]{2,1,0:T(8,128)(2,1)}, f32[8,128]{1,0:T(8,128)S(1)}) custom-call(s32[13]{0:T(128)S(1)} %copy-done.23, bf16[2,512,256]{2,1,0:T(8,128)(2,1)} %collective-permute-done.12.refs_0_, bf16[2,512,256]{2,1,0:T(8,128)(2,1)} %collective-permute-done.13.refs_1_, ...), custom_call_target="tpu_custom_call", output_to_operand_aliasing={{0}: (1, {})} | custom-call | flops 1 | bytes 1 | tf_op jit(solution)/shard_map/pallas_call | solution.py:441
  51.1 2.6 %collective-permute-start.18 = (bf16[256,512]{1,0:T(8,128)(2,1)S(1)}, bf16[256,512]{1,0:T(8,128)(2,1)S(1)}, u32[]{:S(2)}, u32[]{:S(2)}) collective-permute-start(bf16[256,512]{1,0:T(8,128)(2,1)S(1)} %get-tuple-element.230), channel_id=1, source_target_pairs={{0,2},{1,3},{2,0},{3,1},{4,6},{5,7},{6,4},{7,5},{8,10},{9,11},{10,... | collective-permute-start | bytes 786440 | tf_op jit(solution)/shard_map/ppermute | solution.py:591
  53.8 1.3 collective-permute-done.9.refs_0_
  55.7 2.0 %shard_map.87 = (bf16[2,512,256]{2,1,0:T(8,128)(2,1)S(1)}, f32[8,128]{1,0:T(8,128)S(1)}) custom-call(s32[13]{0:T(128)S(1)} %copy-done.23, bf16[2,512,256]{2,1,0:T(8,128)(2,1)S(1)} %collective-permute-done.9.refs_0_, bf16[2,512,256]{2,1,0:T(8,128)(2,1)S(1)} %collective-permute-done.10.refs_1_, ...), custom_call_target="tpu_custom_call", output_to_operand_aliasing={{0}: (1, {})} | custom-call | flops 1 | bytes 1 | tf_op jit(solution)/shard_map/pallas_call | solution.py:441
  58.3 2.4 %collective-permute-done.16.refs_0_ = bf16[2,512,256]{2,1,0:T(8,128)(2,1)S(1)} collective-permute-done((bf16[2,512,256]{2,1,0:T(8,128)(2,1)}, bf16[2,512,256]{2,1,0:T(8,128)(2,1)S(1)}, u32[]{:S(2)}, u32[]{:S(2)}) %collective-permute-start.16) | collective-permute-done | bytes 524320 | tf_op jit(solution)/shard_map/ppermute | solution.py:381
  60.7 2.0 %shard_map.88 = (bf16[2,512,256]{2,1,0:T(8,128)(2,1)S(1)}, f32[8,128]{1,0:T(8,128)S(1)}) custom-call(s32[13]{0:T(128)S(1)} %copy-done.23, bf16[2,512,256]{2,1,0:T(8,128)(2,1)S(1)} %collective-permute-done.16.refs_0_, bf16[2,512,256]{2,1,0:T(8,128)(2,1)S(1)} %collective-permute-done.17.refs_1_, ...), custom_call_target="tpu_custom_call", output_to_operand_aliasing={{0}: (1, {})} | custom-call | flops 1 | bytes 1 | tf_op jit(solution)/shard_map/pallas_call | solution.py:441
  62.8 2.9 %collective-permute-done.18.refs_0_ = bf16[256,512]{1,0:T(8,128)(2,1)S(1)} collective-permute-done((bf16[256,512]{1,0:T(8,128)(2,1)S(1)}, bf16[256,512]{1,0:T(8,128)(2,1)S(1)}, u32[]{:S(2)}, u32[]{:S(2)}) %collective-permute-start.18) | collective-permute-done | bytes 262176 | tf_op jit(solution)/shard_map/ppermute | solution.py:591
  65.6 1.7 %collective-permute-start.21 = (bf16[2,512,256]{2,1,0:T(8,128)(2,1)S(1)}, bf16[2,512,256]{2,1,0:T(8,128)(2,1)S(1)}, u32[]{:S(2)}, u32[]{:S(2)}) collective-permute-start(bf16[2,512,256]{2,1,0:T(8,128)(2,1)S(1)} %get-tuple-element.154.refs_9_.refs_16_.refs_4_.refs_11_.refs_6_), channel_id=1, source_target_pairs={{0,8},{4,20},{8,24},{12,4},{16,0},{20,28},{24,16},{28,12},{1,9},{5... | collective-permute-start | bytes 1572872 | tf_op jit(solution)/shard_map/ppermute | solution.py:381
  68.0 2.5 %shard_map.90 = (f32[8,128]{1,0:T(8,128)S(1)}, f32[1024,128]{1,0:T(8,128)S(1)}) custom-call(s32[13]{0:T(128)S(1)} %copy-done.23, bf16[6656,128]{1,0:T(8,128)(2,1)S(1)} %copy-done.1, bf16[2,512,256]{2,1,0:T(8,128)(2,1)} %get-tuple-element.117.refs_2_, bf16[2,512,256]{2,1,0:T(8,128)(2,1)} %get-tuple-element.127.refs_3_.refs_10_, ...), custom_call_target="tpu_custom_call" | custom-call | flops 1 | bytes 1 | tf_op jit(solution)/shard_map/pallas_call | solution.py:532
  70.5 2.0 %shard_map.91 = (bf16[2,512,256]{2,1,0:T(8,128)(2,1)S(1)}, f32[8,128]{1,0:T(8,128)S(1)}) custom-call(s32[13]{0:T(128)S(1)} %copy-done.23, bf16[2,512,256]{2,1,0:T(8,128)(2,1)S(1)} %collective-permute-done.14.refs_0_, bf16[2,512,256]{2,1,0:T(8,128)(2,1)S(1)} %collective-permute-done.15.refs_1_, ...), custom_call_target="tpu_custom_call", output_to_operand_aliasing={{0}: (1, {})} | custom-call | flops 1 | bytes 1 | tf_op jit(solution)/shard_map/pallas_call | solution.py:441
  72.6 2.9 %collective-permute-done.21.refs_0_ = bf16[2,512,256]{2,1,0:T(8,128)(2,1)S(1)} collective-permute-done((bf16[2,512,256]{2,1,0:T(8,128)(2,1)S(1)}, bf16[2,512,256]{2,1,0:T(8,128)(2,1)S(1)}, u32[]{:S(2)}, u32[]{:S(2)}) %collective-permute-start.21) | collective-permute-done | bytes 524320 | tf_op jit(solution)/shard_map/ppermute | solution.py:381
  75.5 2.0 %shard_map.92 = (bf16[2,512,256]{2,1,0:T(8,128)(2,1)S(1)}, f32[8,128]{1,0:T(8,128)S(1)}) custom-call(s32[13]{0:T(128)S(1)} %copy-done.23, bf16[2,512,256]{2,1,0:T(8,128)(2,1)S(1)} %collective-permute-done.21.refs_0_, bf16[2,512,256]{2,1,0:T(8,128)(2,1)S(1)} %collective-permute-done.22.refs_1_, ...), custom_call_target="tpu_custom_call", output_to_operand_aliasing={{0}: (1, {})} | custom-call | flops 1 | bytes 1 | tf_op jit(solution)/shard_map/pallas_call | solution.py:441
  77.6 2.0 %collective-permute-done.23.refs_0_ = bf16[256,512]{1,0:T(8,128)(2,1)S(1)} collective-permute-done((bf16[256,512]{1,0:T(8,128)(2,1)S(1)}, bf16[256,512]{1,0:T(8,128)(2,1)S(1)}, u32[]{:S(2)}, u32[]{:S(2)}) %collective-permute-start.23) | collective-permute-done | bytes 262176 | tf_op jit(solution)/shard_map/ppermute | solution.py:591
  80.7 1.9 %collective-permute-start.19 = (bf16[2,512,256]{2,1,0:T(8,128)(2,1)S(1)}, bf16[2,512,256]{2,1,0:T(8,128)(2,1)S(1)}, u32[]{:S(2)}, u32[]{:S(2)}) collective-permute-start(bf16[2,512,256]{2,1,0:T(8,128)(2,1)S(1)} %get-tuple-element.159.refs_13_.refs_8_.refs_3_.refs_2_), channel_id=1, source_target_pairs={{0,8},{4,20},{8,24},{12,4},{16,0},{20,28},{24,16},{28,12},{1,9},{5... | collective-permute-start | bytes 1572872 | tf_op jit(solution)/shard_map/ppermute | solution.py:381
  85.0 4.7 %shard_map.94 = (f32[8,128]{1,0:T(8,128)S(1)}, f32[1024,128]{1,0:T(8,128)S(1)}, f32[512,128]{1,0:T(8,128)S(1)}, bf16[256,6656]{1,0:T(8,128)(2,1)}, bf16[256,256]...) custom-call(s32[13]{0:T(128)S(1)} %copy-done.23, ...), custom_call_target="tpu_custom_call", output_to_operand_aliasing={{1}: (19, {})} | custom-call | flops 1 | bytes 1 | tf_op jit(solution)/shard_map/pallas_call | solution.py:532
  90.8 2.0 %shard_map.95 = (bf16[2,512,256]{2,1,0:T(8,128)(2,1)S(1)}, f32[8,128]{1,0:T(8,128)S(1)}) custom-call(s32[13]{0:T(128)S(1)} %copy-done.23, bf16[2,512,256]{2,1,0:T(8,128)(2,1)S(1)} %collective-permute-done.19.refs_0_, bf16[2,512,256]{2,1,0:T(8,128)(2,1)S(1)} %collective-permute-done.20.refs_1_, ...), custom_call_target="tpu_custom_call", output_to_operand_aliasing={{0}: (1, {})} | custom-call | flops 1 | bytes 1 | tf_op jit(solution)/shard_map/pallas_call | solution.py:441
  93.0 3.4 %collective-permute-done.28.refs_0_ = bf16[2,512,256]{2,1,0:T(8,128)(2,1)S(1)} collective-permute-done((bf16[2,512,256]{2,1,0:T(8,128)(2,1)S(1)}, bf16[2,512,256]{2,1,0:T(8,128)(2,1)S(1)}, u32[]{:S(2)}, u32[]{:S(2)}) %collective-permute-start.28) | collective-permute-done | bytes 524320 | tf_op jit(solution)/shard_map/ppermute | solution.py:381
  96.4 2.0 %shard_map.96 = (bf16[2,512,256]{2,1,0:T(8,128)(2,1)S(1)}, f32[8,128]{1,0:T(8,128)S(1)}) custom-call(s32[13]{0:T(128)S(1)} %copy-done.23, bf16[2,512,256]{2,1,0:T(8,128)(2,1)S(1)} %collective-permute-done.28.refs_0_, bf16[2,512,256]{2,1,0:T(8,128)(2,1)S(1)} %collective-permute-done.29.refs_1_, ...), custom_call_target="tpu_custom_call", output_to_operand_aliasing={{0}: (1, {})} | custom-call | flops 1 | bytes 1 | tf_op jit(solution)/shard_map/pallas_call | solution.py:441
  98.5 5.0 %shard_map.97 = (f32[8,128]{1,0:T(8,128)S(1)}, f32[1024,128]{1,0:T(8,128)S(1)}, f32[512,128]{1,0:T(8,128)S(1)}, bf16[256,6656]{1,0:T(8,128)(2,1)}, bf16[256,256]...) custom-call(s32[13]{0:T(128)S(1)} %copy-done.23, ...), custom_call_target="tpu_custom_call", output_to_operand_aliasing={{1}: (15, {}), {2}: (19, {}), {3}: (20, {})} | custom-call | flops 1 | bytes 1 | tf_op jit(solution)/shard_map/pallas_call | solution.py:532
  103.5 2.0 %shard_map.98 = (bf16[2,512,256]{2,1,0:T(8,128)(2,1)S(1)}, f32[8,128]{1,0:T(8,128)S(1)}) custom-call(s32[13]{0:T(128)S(1)} %copy-done.23, bf16[2,512,256]{2,1,0:T(8,128)(2,1)S(1)} %collective-permute-done.26.refs_0_, bf16[2,512,256]{2,1,0:T(8,128)(2,1)S(1)} %collective-permute-done.27.refs_1_, ...), custom_call_target="tpu_custom_call", output_to_operand_aliasing={{0}: (1, {})} | custom-call | flops 1 | bytes 1 | tf_op jit(solution)/shard_map/pallas_call | solution.py:441
  109.3 3.7 %shard_map.100 = (f32[8,128]{1,0:T(8,128)S(1)}, f32[1024,128]{1,0:T(8,128)S(1)}, f32[512,128]{1,0:T(8,128)S(1)}, bf16[256,6656]{1,0:T(8,128)(2,1)}, bf16[256,256...) custom-call(s32[13]{0:T(128)S(1)} %copy-done.23, ...), custom_call_target="tpu_custom_call", output_to_operand_aliasing={{1}: (11, {}), {2}: (15, {}), {3}: (16, {})} | custom-call | flops 1 | bytes 1 | tf_op jit(solution)/shard_map/pallas_call | solution.py:532
  113.0 2.0 %collective-permute-done.31.refs_0_ = bf16[2,512,256]{2,1,0:T(8,128)(2,1)S(1)} collective-permute-done((bf16[2,512,256]{2,1,0:T(8,128)(2,1)S(1)}, bf16[2,512,256]{2,1,0:T(8,128)(2,1)S(1)}, u32[]{:S(2)}, u32[]{:S(2)}) %collective-permute-start.31) | collective-permute-done | bytes 524320 | tf_op jit(solution)/shard_map/ppermute | solution.py:381
  116.3 4.4 %collective-permute-done.37.refs_0_ = bf16[2,512,256]{2,1,0:T(8,128)(2,1)S(1)} collective-permute-done((bf16[2,512,256]{2,1,0:T(8,128)(2,1)S(1)}, bf16[2,512,256]{2,1,0:T(8,128)(2,1)S(1)}, u32[]{:S(2)}, u32[]{:S(2)}) %collective-permute-start.37) | collective-permute-done | bytes 524320 | tf_op jit(solution)/shard_map/ppermute | solution.py:381
  121.3 3.7 %shard_map.103 = (f32[8,128]{1,0:T(8,128)S(1)}, f32[1024,128]{1,0:T(8,128)S(1)}, f32[512,128]{1,0:T(8,128)S(1)}, bf16[256,6656]{1,0:T(8,128)(2,1)}, bf16[256,256...) custom-call(s32[13]{0:T(128)S(1)} %copy-done.23, ...), custom_call_target="tpu_custom_call", output_to_operand_aliasing={{1}: (11, {}), {2}: (15, {}), {3}: (16, {})} | custom-call | flops 1 | bytes 1 | tf_op jit(solution)/shard_map/pallas_call | solution.py:532
  128.5 3.3 %collective-permute-done.40.refs_9_ = bf16[2,512,256]{2,1,0:T(8,128)(2,1)S(1)} collective-permute-done((bf16[2,512,256]{2,1,0:T(8,128)(2,1)S(1)}, bf16[2,512,256]{2,1,0:T(8,128)(2,1)S(1)}, u32[]{:S(2)}, u32[]{:S(2)}) %collective-permute-start.40) | collective-permute-done | bytes 524320 | tf_op jit(solution)/shard_map/ppermute | solution.py:381
  131.8 3.7 %shard_map.105 = (f32[8,128]{1,0:T(8,128)S(1)}, f32[1024,128]{1,0:T(8,128)S(1)}, f32[512,128]{1,0:T(8,128)S(1)}, bf16[256,6656]{1,0:T(8,128)(2,1)}, bf16[256,256...) custom-call(s32[13]{0:T(128)S(1)} %copy-done.23, ...), custom_call_target="tpu_custom_call", output_to_operand_aliasing={{1}: (11, {}), {2}: (15, {}), {3}: (16, {})} | custom-call | flops 1 | bytes 1 | tf_op jit(solution)/shard_map/pallas_call | solution.py:532
  135.6 1.9 %collective-permute-done.45.refs_5_ = bf16[2,512,256]{2,1,0:T(8,128)(2,1)S(1)} collective-permute-done((bf16[2,512,256]{2,1,0:T(8,128)(2,1)S(1)}, bf16[2,512,256]{2,1,0:T(8,128)(2,1)S(1)}, u32[]{:S(2)}, u32[]{:S(2)}) %collective-permute-start.45) | collective-permute-done | bytes 524320 | tf_op jit(solution)/shard_map/ppermute | solution.py:381
  137.5 3.4 %shard_map.106 = (f32[8,128]{1,0:T(8,128)}, f32[1024,128]{1,0:T(8,128)S(1)}, f32[512,128]{1,0:T(8,128)S(1)}, bf16[256,6656]{1,0:T(8,128)(2,1)}, bf16[256,256]{1,0:T(8,128)(2,1)S(1)}) custom-call(s32[13]{0:T(128)S(1)} %copy-done.23, bf16[6656,128]{1,0:T(8,128)(2,1)S(1)} %copy-done.1, ...), custom_call_target="tpu_custom_call", output_to_operand_aliasing={{1}: (7, {}), {2}: (11, {}), {3}: (12, {})} | custom-call | flops 1 | bytes 1 | tf_op jit(solution)/shard_map/pallas_call | solution.py:532
  141.7 1.5 collective-permute-done.49
  143.3 1.7 %collective-permute-start.51 = (f32[64,256]{1,0:T(8,128)S(1)}, f32[64,256]{1,0:T(8,128)S(1)}, u32[]{:S(2)}, u32[]{:S(2)}) collective-permute-start(f32[64,256]{1,0:T(8,128)S(1)} %get-tuple-element.235), channel_id=1, source_target_pairs={{0,2},{1,3},{2,0},{3,1},{4,6},{5,7},{6,4},{7,5},{8,10},{9,11},{10,... | collective-permute-start | bytes 196616 | tf_op jit(solution)/shard_map/ppermute | solution.py:626
  145.0 2.1 %collective-permute-start.52 = (f32[64,256]{1,0:T(8,128)S(1)}, f32[64,256]{1,0:T(8,128)S(1)}, u32[]{:S(2)}, u32[]{:S(2)}) collective-permute-start(f32[64,256]{1,0:T(8,128)S(1)} %get-tuple-element.234), channel_id=1, source_target_pairs={{0,3},{1,0},{2,1},{3,2},{4,7},{5,4},{6,5},{7,6},{8,11},{9,8},{10,9... | collective-permute-start | bytes 196616 | tf_op jit(solution)/shard_map/ppermute | solution.py:626
  147.6 2.4 %collective-permute-done.50 = f32[64,256]{1,0:T(8,128)S(1)} collective-permute-done((f32[64,256]{1,0:T(8,128)S(1)}, f32[64,256]{1,0:T(8,128)S(1)}, u32[]{:S(2)}, u32[]{:S(2)}) %collective-permute-start.50) | collective-permute-done | bytes 65568 | tf_op jit(solution)/shard_map/ppermute | solution.py:626
  150.1 1.9 %collective-permute-done.51 = f32[64,256]{1,0:T(8,128)S(1)} collective-permute-done((f32[64,256]{1,0:T(8,128)S(1)}, f32[64,256]{1,0:T(8,128)S(1)}, u32[]{:S(2)}, u32[]{:S(2)}) %collective-permute-start.51) | collective-permute-done | bytes 65568 | tf_op jit(solution)/shard_map/ppermute | solution.py:626
  152.0 1.4 collective-permute-start.53
  153.4 1.3 shard_map.107
  156.0 1.3 collective-permute-start.55
  157.3 1.5 collective-permute-done.53
  158.8 2.3 %collective-permute-done.54 = f32[64,256]{1,0:T(8,128)S(1)} collective-permute-done((f32[64,256]{1,0:T(8,128)S(1)}, f32[64,256]{1,0:T(8,128)S(1)}, u32[]{:S(2)}, u32[]{:S(2)}) %collective-permute-start.54) | collective-permute-done | bytes 65568 | tf_op jit(solution)/shard_map/ppermute | solution.py:631
  (179 shorter events, 37.8 us)
Async XLA Ops:
  5.9 6.1 %collective-permute-start.3 = (bf16[2,512,256]{2,1,0:T(8,128)(2,1)}, bf16[2,512,256]{2,1,0:T(8,128)(2,1)S(1)}, u32[]{:S(2)}, u32[]{:S(2)}) collective-permute-start(bf16[2,512,256]{2,1,0:T(8,128)(2,1)} %get-tuple-element.121), channel_id=1, source_target_pairs={{0,4},{4,0},{8,12},{12,8},{16,20},{20,16},{24,28},{28,24},{1,5},{5... | collective-permute-start | bytes 1572872 | tf_op jit(solution)/shard_map/ppermute | solution.py:384
  6.0 21.7 %collective-permute-start.2 = (bf16[2,512,256]{2,1,0:T(8,128)(2,1)}, bf16[2,512,256]{2,1,0:T(8,128)(2,1)}, u32[]{:S(2)}, u32[]{:S(2)}) collective-permute-start(bf16[2,512,256]{2,1,0:T(8,128)(2,1)} %get-tuple-element.118), channel_id=1, source_target_pairs={{0,4},{4,0},{8,12},{12,8},{16,20},{20,16},{24,28},{28,24},{1,5},{5... | collective-permute-start | bytes 1572872 | tf_op jit(solution)/shard_map/ppermute | solution.py:384
  11.5 16.3 %collective-permute-start.1 = (bf16[2,512,256]{2,1,0:T(8,128)(2,1)}, bf16[2,512,256]{2,1,0:T(8,128)(2,1)}, u32[]{:S(2)}, u32[]{:S(2)}) collective-permute-start(bf16[2,512,256]{2,1,0:T(8,128)(2,1)} %get-tuple-element.117.refs_2_), channel_id=1, source_target_pairs={{0,8},{4,20},{8,24},{12,4},{16,0},{20,28},{24,16},{28,12},{1,9},{5... | collective-permute-start | bytes 1572872 | tf_op jit(solution)/shard_map/ppermute | solution.py:381
  11.6 20.8 %collective-permute-start.8 = (bf16[2,512,256]{2,1,0:T(8,128)(2,1)}, bf16[2,512,256]{2,1,0:T(8,128)(2,1)}, u32[]{:S(2)}, u32[]{:S(2)}) collective-permute-start(bf16[2,512,256]{2,1,0:T(8,128)(2,1)} %get-tuple-element.132), channel_id=1, source_target_pairs={{0,4},{4,0},{8,12},{12,8},{16,20},{20,16},{24,28},{28,24},{1,5},{5... | collective-permute-start | bytes 1572872 | tf_op jit(solution)/shard_map/ppermute | solution.py:384
  15.2 17.9 %collective-permute-start.7 = (bf16[2,512,256]{2,1,0:T(8,128)(2,1)}, bf16[2,512,256]{2,1,0:T(8,128)(2,1)}, u32[]{:S(2)}, u32[]{:S(2)}) collective-permute-start(bf16[2,512,256]{2,1,0:T(8,128)(2,1)} %get-tuple-element.131.refs_6_), channel_id=1, source_target_pairs={{0,8},{4,20},{8,24},{12,4},{16,0},{20,28},{24,16},{28,12},{1,9},{5... | collective-permute-start | bytes 1572872 | tf_op jit(solution)/shard_map/ppermute | solution.py:381
  15.5 21.4 %collective-permute-start.6 = (bf16[256,1024]{1,0:T(8,128)(2,1)}, bf16[256,1024]{1,0:T(8,128)(2,1)}, u32[]{:S(2)}, u32[]{:S(2)}) collective-permute-start(bf16[256,1024]{1,0:T(8,128)(2,1)} %get-tuple-element.120.refs_0_), channel_id=1, source_target_pairs={{0,1},{1,2},{2,3},{3,0},{4,5},{5,6},{6,7},{7,4},{8,9},{9,10},{10,1... | collective-permute-start | bytes 1572872 | tf_op jit(solution)/shard_map/ppermute | solution.py:591
  27.7 13.5 %collective-permute-start.5 = (bf16[2,512,256]{2,1,0:T(8,128)(2,1)}, bf16[2,512,256]{2,1,0:T(8,128)(2,1)}, u32[]{:S(2)}, u32[]{:S(2)}) collective-permute-start(bf16[2,512,256]{2,1,0:T(8,128)(2,1)} %get-tuple-element.128), channel_id=1, source_target_pairs={{0,4},{4,0},{8,12},{12,8},{16,20},{20,16},{24,28},{28,24},{1,5},{5... | collective-permute-start | bytes 1572872 | tf_op jit(solution)/shard_map/ppermute | solution.py:384
  32.3 9.5 %collective-permute-start.4 = (bf16[2,512,256]{2,1,0:T(8,128)(2,1)}, bf16[2,512,256]{2,1,0:T(8,128)(2,1)}, u32[]{:S(2)}, u32[]{:S(2)}) collective-permute-start(bf16[2,512,256]{2,1,0:T(8,128)(2,1)} %get-tuple-element.127.refs_3_.refs_10_), channel_id=1, source_target_pairs={{0,8},{4,20},{8,24},{12,4},{16,0},{20,28},{24,16},{28,12},{1,9},{5... | collective-permute-start | bytes 1572872 | tf_op jit(solution)/shard_map/ppermute | solution.py:381
  32.4 13.5 %collective-permute-start.13 = (bf16[2,512,256]{2,1,0:T(8,128)(2,1)}, bf16[2,512,256]{2,1,0:T(8,128)(2,1)}, u32[]{:S(2)}, u32[]{:S(2)}) collective-permute-start(bf16[2,512,256]{2,1,0:T(8,128)(2,1)} %get-tuple-element.142), channel_id=1, source_target_pairs={{0,4},{4,0},{8,12},{12,8},{16,20},{20,16},{24,28},{28,24},{1,5},{5... | collective-permute-start | bytes 1572872 | tf_op jit(solution)/shard_map/ppermute | solution.py:384
  36.8 10.7 %collective-permute-start.12 = (bf16[2,512,256]{2,1,0:T(8,128)(2,1)}, bf16[2,512,256]{2,1,0:T(8,128)(2,1)}, u32[]{:S(2)}, u32[]{:S(2)}) collective-permute-start(bf16[2,512,256]{2,1,0:T(8,128)(2,1)} %get-tuple-element.141.refs_7_.refs_14_.refs_2_), channel_id=1, source_target_pairs={{0,8},{4,20},{8,24},{12,4},{16,0},{20,28},{24,16},{28,12},{1,9},{5... | collective-permute-start | bytes 1572872 | tf_op jit(solution)/shard_map/ppermute | solution.py:381
  36.9 14.2 %collective-permute-start.11 = (bf16[256,1024]{1,0:T(8,128)(2,1)}, bf16[256,1024]{1,0:T(8,128)(2,1)}, u32[]{:S(2)}, u32[]{:S(2)}) collective-permute-start(bf16[256,1024]{1,0:T(8,128)(2,1)} %get-tuple-element.120.refs_0_), channel_id=1, source_target_pairs={{0,3},{1,0},{2,1},{3,2},{4,7},{5,4},{6,5},{7,6},{8,11},{9,8},{10,9... | collective-permute-start | bytes 1572872 | tf_op jit(solution)/shard_map/ppermute | solution.py:591
  41.2 9.9 %collective-permute-start.10 = (bf16[2,512,256]{2,1,0:T(8,128)(2,1)}, bf16[2,512,256]{2,1,0:T(8,128)(2,1)S(1)}, u32[]{:S(2)}, u32[]{:S(2)}) collective-permute-start(bf16[2,512,256]{2,1,0:T(8,128)(2,1)} %get-tuple-element.138), channel_id=1, source_target_pairs={{0,4},{4,0},{8,12},{12,8},{16,20},{20,16},{24,28},{28,24},{1,5},{5... | collective-permute-start | bytes 1572872 | tf_op jit(solution)/shard_map/ppermute | solution.py:384
  45.7 9.4 %collective-permute-start.9 = (bf16[2,512,256]{2,1,0:T(8,128)(2,1)}, bf16[2,512,256]{2,1,0:T(8,128)(2,1)S(1)}, u32[]{:S(2)}, u32[]{:S(2)}) collective-permute-start(bf16[2,512,256]{2,1,0:T(8,128)(2,1)} %get-tuple-element.137.refs_4_.refs_11_.refs_6_), channel_id=1, source_target_pairs={{0,8},{4,20},{8,24},{12,4},{16,0},{20,28},{24,16},{28,12},{1,9},{5... | collective-permute-start | bytes 1572872 | tf_op jit(solution)/shard_map/ppermute | solution.py:381
  45.9 38.6 %collective-permute-start.25 = (bf16[256,3328]{1,0:T(8,128)(2,1)S(1)}, bf16[256,3328]{1,0:T(8,128)(2,1)S(1)}, u32[]{:S(2)}, u32[]{:S(2)}) collective-permute-start(bf16[256,3328]{1,0:T(8,128)(2,1)S(1)} %constant_dynamic-slice_fusion.3), channel_id=1, source_target_pairs={{0,4},{4,0},{8,12},{12,8},{16,20},{20,16},{24,28},{28,24},{1,5},{5... | collective-permute-start | bytes 5111816 | tf_op jit(solution)/shard_map/ppermute | solution.py:384
  47.5 10.2 %collective-permute-start.17 = (bf16[2,512,256]{2,1,0:T(8,128)(2,1)S(1)}, bf16[2,512,256]{2,1,0:T(8,128)(2,1)S(1)}, u32[]{:S(2)}, u32[]{:S(2)}) collective-permute-start(bf16[2,512,256]{2,1,0:T(8,128)(2,1)S(1)} %copy-done.33), channel_id=1, source_target_pairs={{0,4},{4,0},{8,12},{12,8},{16,20},{20,16},{24,28},{28,24},{1,5},{5... | collective-permute-start | bytes 1572872 | tf_op jit(solution)/shard_map/ppermute | solution.py:384
  51.1 9.6 %collective-permute-start.16 = (bf16[2,512,256]{2,1,0:T(8,128)(2,1)}, bf16[2,512,256]{2,1,0:T(8,128)(2,1)S(1)}, u32[]{:S(2)}, u32[]{:S(2)}) collective-permute-start(bf16[2,512,256]{2,1,0:T(8,128)(2,1)} %get-tuple-element.150.refs_8_.refs_15_.refs_3_.refs_10_), channel_id=1, source_target_pairs={{0,8},{4,20},{8,24},{12,4},{16,0},{20,28},{24,16},{28,12},{1,9},{5... | collective-permute-start | bytes 1572872 | tf_op jit(solution)/shard_map/ppermute | solution.py:381
  51.1 14.5 %collective-permute-start.18 = (bf16[256,512]{1,0:T(8,128)(2,1)S(1)}, bf16[256,512]{1,0:T(8,128)(2,1)S(1)}, u32[]{:S(2)}, u32[]{:S(2)}) collective-permute-start(bf16[256,512]{1,0:T(8,128)(2,1)S(1)} %get-tuple-element.230), channel_id=1, source_target_pairs={{0,2},{1,3},{2,0},{3,1},{4,6},{5,7},{6,4},{7,5},{8,10},{9,11},{10,... | collective-permute-start | bytes 786440 | tf_op jit(solution)/shard_map/ppermute | solution.py:591
  55.1 12.3 %collective-permute-start.15 = (bf16[2,512,256]{2,1,0:T(8,128)(2,1)S(1)}, bf16[2,512,256]{2,1,0:T(8,128)(2,1)S(1)}, u32[]{:S(2)}, u32[]{:S(2)}) collective-permute-start(bf16[2,512,256]{2,1,0:T(8,128)(2,1)S(1)} %copy-done.32), channel_id=1, source_target_pairs={{0,4},{4,0},{8,12},{12,8},{16,20},{20,16},{24,28},{28,24},{1,5},{5... | collective-permute-start | bytes 1572872 | tf_op jit(solution)/shard_map/ppermute | solution.py:384
  57.8 14.8 %collective-permute-start.22 = (bf16[2,512,256]{2,1,0:T(8,128)(2,1)S(1)}, bf16[2,512,256]{2,1,0:T(8,128)(2,1)S(1)}, u32[]{:S(2)}, u32[]{:S(2)}) collective-permute-start(bf16[2,512,256]{2,1,0:T(8,128)(2,1)S(1)} %copy-done.31), channel_id=1, source_target_pairs={{0,4},{4,0},{8,12},{12,8},{16,20},{20,16},{24,28},{28,24},{1,5},{5... | collective-permute-start | bytes 1572872 | tf_op jit(solution)/shard_map/ppermute | solution.py:384
  60.7 9.8 %collective-permute-start.14 = (bf16[2,512,256]{2,1,0:T(8,128)(2,1)S(1)}, bf16[2,512,256]{2,1,0:T(8,128)(2,1)S(1)}, u32[]{:S(2)}, u32[]{:S(2)}) collective-permute-start(bf16[2,512,256]{2,1,0:T(8,128)(2,1)S(1)} %get-tuple-element.147.refs_5_.refs_12_.refs_7_.refs_2_), channel_id=1, source_target_pairs={{0,8},{4,20},{8,24},{12,4},{16,0},{20,28},{24,16},{28,12},{1,9},{5... | collective-permute-start | bytes 1572872 | tf_op jit(solution)/shard_map/ppermute | solution.py:381
  65.6 9.9 %collective-permute-start.21 = (bf16[2,512,256]{2,1,0:T(8,128)(2,1)S(1)}, bf16[2,512,256]{2,1,0:T(8,128)(2,1)S(1)}, u32[]{:S(2)}, u32[]{:S(2)}) collective-permute-start(bf16[2,512,256]{2,1,0:T(8,128)(2,1)S(1)} %get-tuple-element.154.refs_9_.refs_16_.refs_4_.refs_11_.refs_6_), channel_id=1, source_target_pairs={{0,8},{4,20},{8,24},{12,4},{16,0},{20,28},{24,16},{28,12},{1,9},{5... | collective-permute-start | bytes 1572872 | tf_op jit(solution)/shard_map/ppermute | solution.py:381
  67.4 12.2 %collective-permute-start.23 = (bf16[256,512]{1,0:T(8,128)(2,1)S(1)}, bf16[256,512]{1,0:T(8,128)(2,1)S(1)}, u32[]{:S(2)}, u32[]{:S(2)}) collective-permute-start(bf16[256,512]{1,0:T(8,128)(2,1)S(1)} %get-tuple-element.229), channel_id=1, source_target_pairs={{0,2},{1,3},{2,0},{3,1},{4,6},{5,7},{6,4},{7,5},{8,10},{9,11},{10,... | collective-permute-start | bytes 786440 | tf_op jit(solution)/shard_map/ppermute | solution.py:591
  80.2 9.4 %collective-permute-start.20 = (bf16[2,512,256]{2,1,0:T(8,128)(2,1)S(1)}, bf16[2,512,256]{2,1,0:T(8,128)(2,1)S(1)}, u32[]{:S(2)}, u32[]{:S(2)}) collective-permute-start(bf16[2,512,256]{2,1,0:T(8,128)(2,1)S(1)} %copy-done.30), channel_id=1, source_target_pairs={{0,4},{4,0},{8,12},{12,8},{16,20},{20,16},{24,28},{28,24},{1,5},{5... | collective-permute-start | bytes 1572872 | tf_op jit(solution)/shard_map/ppermute | solution.py:384
  80.7 10.1 %collective-permute-start.19 = (bf16[2,512,256]{2,1,0:T(8,128)(2,1)S(1)}, bf16[2,512,256]{2,1,0:T(8,128)(2,1)S(1)}, u32[]{:S(2)}, u32[]{:S(2)}) collective-permute-start(bf16[2,512,256]{2,1,0:T(8,128)(2,1)S(1)} %get-tuple-element.159.refs_13_.refs_8_.refs_3_.refs_2_), channel_id=1, source_target_pairs={{0,8},{4,20},{8,24},{12,4},{16,0},{20,28},{24,16},{28,12},{1,9},{5... | collective-permute-start | bytes 1572872 | tf_op jit(solution)/shard_map/ppermute | solution.py:381
  82.6 10.4 %collective-permute-start.29 = (bf16[2,512,256]{2,1,0:T(8,128)(2,1)S(1)}, bf16[2,512,256]{2,1,0:T(8,128)(2,1)S(1)}, u32[]{:S(2)}, u32[]{:S(2)}) collective-permute-start(bf16[2,512,256]{2,1,0:T(8,128)(2,1)S(1)} %copy-done.29), channel_id=1, source_target_pairs={{0,4},{4,0},{8,12},{12,8},{16,20},{20,16},{24,28},{28,24},{1,5},{5... | collective-permute-start | bytes 1572872 | tf_op jit(solution)/shard_map/ppermute | solution.py:384
  83.4 12.9 %collective-permute-start.28 = (bf16[2,512,256]{2,1,0:T(8,128)(2,1)S(1)}, bf16[2,512,256]{2,1,0:T(8,128)(2,1)S(1)}, u32[]{:S(2)}, u32[]{:S(2)}) collective-permute-start(bf16[2,512,256]{2,1,0:T(8,128)(2,1)S(1)} %get-tuple-element.165.refs_17_.refs_5_.refs_12_.refs_7_.refs_6_), channel_id=1, source_target_pairs={{0,8},{4,20},{8,24},{12,4},{16,0},{20,28},{24,16},{28,12},{1,9},{5... | collective-permute-start | bytes 1572872 | tf_op jit(solution)/shard_map/ppermute | solution.py:381
  84.5 19.0 %collective-permute-start.27 = (bf16[2,512,256]{2,1,0:T(8,128)(2,1)S(1)}, bf16[2,512,256]{2,1,0:T(8,128)(2,1)S(1)}, u32[]{:S(2)}, u32[]{:S(2)}) collective-permute-start(bf16[2,512,256]{2,1,0:T(8,128)(2,1)S(1)} %copy-done.28), channel_id=1, source_target_pairs={{0,4},{4,0},{8,12},{12,8},{16,20},{20,16},{24,28},{28,24},{1,5},{5... | collective-permute-start | bytes 1572872 | tf_op jit(solution)/shard_map/ppermute | solution.py:384
  92.8 10.7 %collective-permute-start.26 = (bf16[2,512,256]{2,1,0:T(8,128)(2,1)S(1)}, bf16[2,512,256]{2,1,0:T(8,128)(2,1)S(1)}, u32[]{:S(2)}, u32[]{:S(2)}) collective-permute-start(bf16[2,512,256]{2,1,0:T(8,128)(2,1)S(1)} %get-tuple-element.172.refs_9_.refs_4_.refs_3_.refs_2_), channel_id=1, source_target_pairs={{0,8},{4,20},{8,24},{12,4},{16,0},{20,28},{24,16},{28,12},{1,9},{5... | collective-permute-start | bytes 1572872 | tf_op jit(solution)/shard_map/ppermute | solution.py:381
  92.9 5.6 %collective-permute-start.30 = (bf16[256,256]{1,0:T(8,128)(2,1)S(1)}, bf16[256,256]{1,0:T(8,128)(2,1)S(1)}, u32[]{:S(2)}, u32[]{:S(2)}) collective-permute-start(bf16[256,256]{1,0:T(8,128)(2,1)S(1)} %get-tuple-element.183), channel_id=1, source_target_pairs={{0,4},{4,0},{8,12},{12,8},{16,20},{20,16},{24,28},{28,24},{1,5},{5... | collective-permute-start | bytes 393224 | tf_op jit(solution)/shard_map/ppermute | solution.py:384
  98.4 9.2 %collective-permute-start.32 = (bf16[2,512,256]{2,1,0:T(8,128)(2,1)S(1)}, bf16[2,512,256]{2,1,0:T(8,128)(2,1)S(1)}, u32[]{:S(2)}, u32[]{:S(2)}) collective-permute-start(bf16[2,512,256]{2,1,0:T(8,128)(2,1)S(1)} %get-tuple-element.178.refs_13_.refs_8_.refs_7_.refs_6_), channel_id=1, source_target_pairs={{0,8},{4,20},{8,24},{12,4},{16,0},{20,28},{24,16},{28,12},{1,9},{5... | collective-permute-start | bytes 1572872 | tf_op jit(solution)/shard_map/ppermute | solution.py:381
  105.6 9.4 %collective-permute-start.31 = (bf16[2,512,256]{2,1,0:T(8,128)(2,1)S(1)}, bf16[2,512,256]{2,1,0:T(8,128)(2,1)S(1)}, u32[]{:S(2)}, u32[]{:S(2)}) collective-permute-start(bf16[2,512,256]{2,1,0:T(8,128)(2,1)S(1)} %get-tuple-element.185.refs_5_.refs_4_.refs_3_.refs_2_), channel_id=1, source_target_pairs={{0,8},{4,20},{8,24},{12,4},{16,0},{20,28},{24,16},{28,12},{1,9},{5... | collective-permute-start | bytes 1572872 | tf_op jit(solution)/shard_map/ppermute | solution.py:381
  105.8 3.4 %collective-permute-start.33 = (bf16[256,256]{1,0:T(8,128)(2,1)S(1)}, bf16[256,256]{1,0:T(8,128)(2,1)S(1)}, u32[]{:S(2)}, u32[]{:S(2)}) collective-permute-start(bf16[256,256]{1,0:T(8,128)(2,1)S(1)} %get-tuple-element.192), channel_id=1, source_target_pairs={{0,4},{4,0},{8,12},{12,8},{16,20},{20,16},{24,28},{28,24},{1,5},{5... | collective-permute-start | bytes 393224 | tf_op jit(solution)/shard_map/ppermute | solution.py:384
  108.3 12.3 %collective-permute-start.37 = (bf16[2,512,256]{2,1,0:T(8,128)(2,1)S(1)}, bf16[2,512,256]{2,1,0:T(8,128)(2,1)S(1)}, u32[]{:S(2)}, u32[]{:S(2)}) collective-permute-start(bf16[2,512,256]{2,1,0:T(8,128)(2,1)S(1)} %get-tuple-element.187.refs_9_.refs_8_.refs_7_), channel_id=1, source_target_pairs={{0,8},{4,20},{8,24},{12,4},{16,0},{20,28},{24,16},{28,12},{1,9},{5... | collective-permute-start | bytes 1572872 | tf_op jit(solution)/shard_map/ppermute | solution.py:381
  115.6 10.6 %collective-permute-start.36 = (bf16[2,512,256]{2,1,0:T(8,128)(2,1)S(1)}, bf16[2,512,256]{2,1,0:T(8,128)(2,1)S(1)}, u32[]{:S(2)}, u32[]{:S(2)}) collective-permute-start(bf16[2,512,256]{2,1,0:T(8,128)(2,1)S(1)} %get-tuple-element.196.refs_5_.refs_4_.refs_3_), channel_id=1, source_target_pairs={{0,8},{4,20},{8,24},{12,4},{16,0},{20,28},{24,16},{28,12},{1,9},{5... | collective-permute-start | bytes 1572872 | tf_op jit(solution)/shard_map/ppermute | solution.py:381
  115.7 5.6 %collective-permute-start.38 = (bf16[256,256]{1,0:T(8,128)(2,1)S(1)}, bf16[256,256]{1,0:T(8,128)(2,1)S(1)}, u32[]{:S(2)}, u32[]{:S(2)}) collective-permute-start(bf16[256,256]{1,0:T(8,128)(2,1)S(1)} %get-tuple-element.203), channel_id=1, source_target_pairs={{0,4},{4,0},{8,12},{12,8},{16,20},{20,16},{24,28},{28,24},{1,5},{5... | collective-permute-start | bytes 393224 | tf_op jit(solution)/shard_map/ppermute | solution.py:384
  115.8 5.6 %collective-permute-start.39 = (bf16[256,256]{1,0:T(8,128)(2,1)S(1)}, bf16[256,256]{1,0:T(8,128)(2,1)S(1)}, u32[]{:S(2)}, u32[]{:S(2)}) collective-permute-start(bf16[256,256]{1,0:T(8,128)(2,1)S(1)} %get-tuple-element.204), channel_id=1, source_target_pairs={{0,4},{4,0},{8,12},{12,8},{16,20},{20,16},{24,28},{28,24},{1,5},{5... | collective-permute-start | bytes 393224 | tf_op jit(solution)/shard_map/ppermute | solution.py:384
  121.2 10.6 %collective-permute-start.40 = (bf16[2,512,256]{2,1,0:T(8,128)(2,1)S(1)}, bf16[2,512,256]{2,1,0:T(8,128)(2,1)S(1)}, u32[]{:S(2)}, u32[]{:S(2)}) collective-permute-start(bf16[2,512,256]{2,1,0:T(8,128)(2,1)S(1)} %get-tuple-element.198.refs_9_.refs_8_), channel_id=1, source_target_pairs={{0,8},{4,20},{8,24},{12,4},{16,0},{20,28},{24,16},{28,12},{1,9},{5... | collective-permute-start | bytes 1572872 | tf_op jit(solution)/shard_map/ppermute | solution.py:381
  126.8 10.6 %collective-permute-start.45 = (bf16[2,512,256]{2,1,0:T(8,128)(2,1)S(1)}, bf16[2,512,256]{2,1,0:T(8,128)(2,1)S(1)}, u32[]{:S(2)}, u32[]{:S(2)}) collective-permute-start(bf16[2,512,256]{2,1,0:T(8,128)(2,1)S(1)} %get-tuple-element.206.refs_5_.refs_4_), channel_id=1, source_target_pairs={{0,8},{4,20},{8,24},{12,4},{16,0},{20,28},{24,16},{28,12},{1,9},{5... | collective-permute-start | bytes 1572872 | tf_op jit(solution)/shard_map/ppermute | solution.py:381
  127.5 8.1 %collective-permute-start.46 = (bf16[256,256]{1,0:T(8,128)(2,1)S(1)}, bf16[256,256]{1,0:T(8,128)(2,1)S(1)}, u32[]{:S(2)}, u32[]{:S(2)}) collective-permute-start(bf16[256,256]{1,0:T(8,128)(2,1)S(1)} %get-tuple-element.219), channel_id=1, source_target_pairs={{0,4},{4,0},{8,12},{12,8},{16,20},{20,16},{24,28},{28,24},{1,5},{5... | collective-permute-start | bytes 393224 | tf_op jit(solution)/shard_map/ppermute | solution.py:384
  128.3 7.3 %collective-permute-start.47 = (bf16[256,256]{1,0:T(8,128)(2,1)S(1)}, bf16[256,256]{1,0:T(8,128)(2,1)S(1)}, u32[]{:S(2)}, u32[]{:S(2)}) collective-permute-start(bf16[256,256]{1,0:T(8,128)(2,1)S(1)} %get-tuple-element.220), channel_id=1, source_target_pairs={{0,4},{4,0},{8,12},{12,8},{16,20},{20,16},{24,28},{28,24},{1,5},{5... | collective-permute-start | bytes 393224 | tf_op jit(solution)/shard_map/ppermute | solution.py:384
  143.2 6.8 %collective-permute-start.50 = (f32[64,256]{1,0:T(8,128)S(1)}, f32[64,256]{1,0:T(8,128)S(1)}, u32[]{:S(2)}, u32[]{:S(2)}) collective-permute-start(f32[64,256]{1,0:T(8,128)S(1)} %get-tuple-element.233), channel_id=1, source_target_pairs={{0,1},{1,2},{2,3},{3,0},{4,5},{5,6},{6,7},{7,4},{8,9},{9,10},{10,1... | collective-permute-start | bytes 196616 | tf_op jit(solution)/shard_map/ppermute | solution.py:626
  143.3 8.6 %collective-permute-start.51 = (f32[64,256]{1,0:T(8,128)S(1)}, f32[64,256]{1,0:T(8,128)S(1)}, u32[]{:S(2)}, u32[]{:S(2)}) collective-permute-start(f32[64,256]{1,0:T(8,128)S(1)} %get-tuple-element.235), channel_id=1, source_target_pairs={{0,2},{1,3},{2,0},{3,1},{4,6},{5,7},{6,4},{7,5},{8,10},{9,11},{10,... | collective-permute-start | bytes 196616 | tf_op jit(solution)/shard_map/ppermute | solution.py:626
  145.0 6.9 %collective-permute-start.52 = (f32[64,256]{1,0:T(8,128)S(1)}, f32[64,256]{1,0:T(8,128)S(1)}, u32[]{:S(2)}, u32[]{:S(2)}) collective-permute-start(f32[64,256]{1,0:T(8,128)S(1)} %get-tuple-element.234), channel_id=1, source_target_pairs={{0,3},{1,0},{2,1},{3,2},{4,7},{5,4},{6,5},{7,6},{8,11},{9,8},{10,9... | collective-permute-start | bytes 196616 | tf_op jit(solution)/shard_map/ppermute | solution.py:626
  147.1 6.3 %collective-permute-start.43 = (bf16[256,256]{1,0:T(8,128)(2,1)}, bf16[256,256]{1,0:T(8,128)(2,1)S(1)}, u32[]{:S(2)}, u32[]{:S(2)}) collective-permute-start(bf16[256,256]{1,0:T(8,128)(2,1)} %copy-done.26), channel_id=1, source_target_pairs={{0,4},{4,0},{8,12},{12,8},{16,20},{20,16},{24,28},{28,24},{1,5},{5... | collective-permute-start | bytes 393224 | tf_op jit(solution)/shard_map/ppermute | solution.py:384
  147.1 6.3 %collective-permute-start.44 = (bf16[256,256]{1,0:T(8,128)(2,1)S(1)}, bf16[256,256]{1,0:T(8,128)(2,1)S(1)}, u32[]{:S(2)}, u32[]{:S(2)}) collective-permute-start(bf16[256,256]{1,0:T(8,128)(2,1)S(1)} %get-tuple-element.214), channel_id=1, source_target_pairs={{0,4},{4,0},{8,12},{12,8},{16,20},{20,16},{24,28},{28,24},{1,5},{5... | collective-permute-start | bytes 393224 | tf_op jit(solution)/shard_map/ppermute | solution.py:384
  152.0 6.9 %collective-permute-start.53 = (f32[64,256]{1,0:T(8,128)S(1)}, f32[64,256]{1,0:T(8,128)S(1)}, u32[]{:S(2)}, u32[]{:S(2)}) collective-permute-start(f32[64,256]{1,0:T(8,128)S(1)} %get-tuple-element.226), channel_id=1, source_target_pairs={{0,1},{1,2},{2,3},{3,0},{4,5},{5,6},{6,7},{7,4},{8,9},{9,10},{10,1... | collective-permute-start | bytes 196616 | tf_op jit(solution)/shard_map/ppermute | solution.py:631
  154.7 6.4 %collective-permute-start.54 = (f32[64,256]{1,0:T(8,128)S(1)}, f32[64,256]{1,0:T(8,128)S(1)}, u32[]{:S(2)}, u32[]{:S(2)}) collective-permute-start(f32[64,256]{1,0:T(8,128)S(1)} %get-tuple-element.226), channel_id=1, source_target_pairs={{0,2},{1,3},{2,0},{3,1},{4,6},{5,7},{6,4},{7,5},{8,10},{9,11},{10,... | collective-permute-start | bytes 196616 | tf_op jit(solution)/shard_map/ppermute | solution.py:631
  156.0 5.2 %collective-permute-start.55 = (f32[64,256]{1,0:T(8,128)S(1)}, f32[64,256]{1,0:T(8,128)S(1)}, u32[]{:S(2)}, u32[]{:S(2)}) collective-permute-start(f32[64,256]{1,0:T(8,128)S(1)} %get-tuple-element.226), channel_id=1, source_target_pairs={{0,3},{1,0},{2,1},{3,2},{4,7},{5,4},{6,5},{7,6},{8,11},{9,8},{10,9... | collective-permute-start | bytes 196616 | tf_op jit(solution)/shard_map/ppermute | solution.py:631
  (42 other events, 230.3 us)

commit v2 on v1

--- a/solution.py
+++ b/solution.py
@@ -13,8 +13,7 @@
 LANES = 128
 WIDTHS = (256, 256)
 C_MOST = 3
-HEAD = 2
-LAST_PIECE = 4
+HOPS = (1, 0), (2, 1), (4, 0)
 PARTS = 2
 
 ANY = pl.BlockSpec(memory_space=pl.ANY)
@@ -47,8 +46,8 @@
     return c_out, sketch, predicted
 
 
-OWN, NEAR, ROW, DIST, A_OWNER, A_FIRST = (STEPS * i for i in range(6))
-CORE = STEPS * 6
+OWN, NEAR, ROW, DIST, A_OWNER = (STEPS * i for i in range(5))
+CORE = STEPS * 5
 
 
 def aligned(x, m):
@@ -74,53 +73,9 @@
     return b_ref.at[rows, pl.ds(aligned(core * half + start, LANES), width)]
 
 
-def stage(b_ref, scal, half, chains, outs, bufs, load_sem, store_sem):
-    mine = scal[CORE]
-    outs = list(outs)
-    spots = []
-    for c, chunks in enumerate(chains):
-        for i, chunk in enumerate(chunks):
-            for which in range(2):
-                out = outs.pop(0)
-                for s in range(STEPS):
-                    spots.append(((which, i, s), c, chunk, out))
-    spots.sort(key=lambda spot: (spot[0][0], spot[0][1]))
-
-    def each(act):
-        for spot, c, chunk, out in spots:
-            core = mine if spot[0] else 1 - mine
-            s = spot[2]
-            load = lambda: copy(
-                panel_chunk(b_ref, scal, s, core, half, chunk),
-                bufs[c].at[spot],
-                load_sem[c].at[spot],
-            )
-            store = lambda: copy(bufs[c].at[spot], out.at[s], store_sem[c].at[spot])
-
-            @pl.when(scal[OWN + s] == 1)
-            def _():
-                act(load, store)
-
-    def start(load, store):
-        load().start()
-
-    def turn(load, store):
-        load().wait()
-        store().start()
-
-    def finish(load, store):
-        store().wait()
-
-    each(start)
-    each(turn)
-    each(finish)
-
-
-def prologue_kernel(n_row, half, chains, ids, b_ref, a_ref, scal, cand, *rest):
-    n = 2 * sum(len(chunks) for chunks in chains)
-    outs = rest[:n]
-    a_buf, a_sem = rest[n : n + 2]
-    bufs, load_sem, store_sem = (rest[n + 2 + i :: 3] for i in range(3))
+def prologue_kernel(n_row, half, chunks, ids, b_ref, a_ref, scal, cand, tok_out, *rest):
+    n = len(chunks)
+    outs, (a_buf, bufs, a_sem, load_sem, store_sem) = rest[:n], rest[n:]
     n_chips = n_row // CORES
     me = lax.axis_index("row")
     core = lax.rem(me, CORES)
@@ -137,46 +92,113 @@
         scal[ROW + s] = lax.rem(first, b_ref.shape[0])
         scal[DIST + s] = jnp.where(ahead < 0, ahead + n_chips, ahead)
         scal[A_OWNER + s] = lax.div(first, a_ref.shape[1])
-        scal[A_FIRST + s] = lax.rem(first, a_ref.shape[1])
 
     def a_load(s):
-        cols = pl.ds(aligned(scal[A_FIRST + s], PANEL), PANEL)
+        first = lax.rem(ids[s] * PANEL, a_ref.shape[1])
+        cols = pl.ds(aligned(first, PANEL), PANEL)
         return copy(a_ref.at[:, cols], a_buf.at[:, pl.ds(s * PANEL, PANEL)], a_sem.at[s])
+
+    def each(act):
+        for i, chunk in enumerate(chunks):
+            for s in range(STEPS):
+                load = lambda: copy(
+                    panel_chunk(b_ref, scal, s, 1 - core, half, chunk),
+                    bufs.at[i, s, :, pl.ds(0, chunk[1])],
+                    load_sem.at[i, s],
+                )
+                store = lambda: copy(
+                    bufs.at[i, s, :, pl.ds(0, chunk[1])], outs[i].at[s], store_sem.at[i, s]
+                )
+
+                @pl.when(scal[OWN + s] == 1)
+                def _():
+                    act(load, store)
+
+    owner = scal[OWN] + scal[OWN + 1] > 0
+
+    @pl.when(owner)
+    def _():
+        each(lambda load, store: load().start())
 
     for s in range(STEPS):
         a_load(s).start()
-    stage(b_ref, scal, half, chains, outs, bufs, load_sem, store_sem)
+
+    @pl.when(owner)
+    def _():
+        def turn(load, store):
+            load().wait()
+            store().start()
+
+        each(turn)
+
     for s in range(STEPS):
         a_load(s).wait()
     out = copy(a_buf, cand, a_sem.at[0])
     out.start()
+
+    @pl.when(owner)
+    def _():
+        each(lambda load, store: store().wait())
+
     out.wait()
 
 
-def stage_kernel(half, chains, scal, b_ref, tok_in, *rest):
-    n = 2 * sum(len(chunks) for chunks in chains)
-    outs, rest = rest[:n], rest[n + 1 :]
-    stage(b_ref, scal, half, chains, outs, *(rest[i::3] for i in range(3)))
-
-
-def inject_kernel(first, done, scal, *refs):
-    if done:
-        return
+def take_panels(n_col, hop, scal, came, held, buf, sem, act):
+    z = lax.axis_index("col")
+    mid = n_col // 2
+    for s in range(STEPS):
+        owner = scal[A_OWNER + s]
+        outer = jnp.where(lax.rem(z + 1, n_col) < 2, 1, 0)
+        apart = jnp.where(lax.div(z, mid) == lax.div(owner, mid), 0, 1)
+        other = jnp.where(owner == z, 0, 1)
+        take = ((1 - outer) * (1 - apart) * other, (1 - outer) * apart, outer * other)[hop]
+
+        @pl.when(take == 1)
+        def _(s=s):
+            cols = pl.ds(s * PANEL, PANEL)
+            load = lambda: copy(came.at[:, cols], buf.at[:, cols], sem.at[0, s])
+            store = lambda: copy(buf.at[:, cols], held.at[:, cols], sem.at[1, s])
+            if act == "load":
+                load().start()
+            elif act == "turn":
+                load().wait()
+                store().start()
+            else:
+                store().wait()
+
+
+def inject_kernel(n_col, half, chunk, first, hop, scal, *refs):
     refs = list(refs)
+    take = lambda n: [refs.pop(0) for _ in range(n)]
     if not first:
-        refs.pop(0)
-    sib, own, tok_in, out, tok_out, buf, load_sem, store_sem = refs
+        take(1)
+    if chunk is not None:
+        b_ref, sib = take(2)
+    if hop is not None:
+        came, held_in = take(2)
+    tok_in, out, tok_out = take(3)
+    if hop is not None:
+        (held,) = take(1)
+    buf, load_sem, store_sem, a_buf, a_sem = refs
     rows = PANEL // PARTS
     for act in ("load", "turn", "finish"):
-        for flag, source in ((OWN, own), (NEAR, sib)):
+        if hop is not None:
+            take_panels(n_col, hop, scal, came, held, a_buf, a_sem, act)
+        if chunk is None:
+            continue
+        for flag in (OWN, NEAR):
             for s in range(STEPS):
 
                 @pl.when(scal[flag + s] == 1)
-                def _(source=source, s=s, act=act):
+                def _(flag=flag, s=s, act=act):
+                    if flag == OWN:
+                        source = panel_chunk(b_ref, scal, s, scal[CORE], half, chunk)
+                    else:
+                        source = sib.at[s]
                     for p in range(PARTS):
                         part = pl.ds(p * rows, rows)
                         spot = (s, part)
-                        load = lambda: copy(source.at[spot], buf.at[spot], load_sem.at[s, p])
+                        load = lambda: copy(source.at[part], buf.at[spot], load_sem.at[s, p])
                         store = lambda: copy(buf.at[spot], out.at[spot], store_sem.at[s, p])
                         if act == "load":
                             load().start()
@@ -187,20 +209,12 @@
                             store().wait()
 
 
-def pick_kernel(n_col, k, panels, scal, *refs):
-    cand, out, tok_out, sem = refs[0], *refs[-3:]
-    z = lax.axis_index("col")
-    for i, s in enumerate(panels):
-        away = z - scal[A_OWNER + s]
-        away = jnp.where(away < 0, away + n_col, away)
-
-        @pl.when(away == k)
-        def _(i=i, s=s):
-            cp = copy(
-                cand.at[:, pl.ds(i * PANEL, PANEL)], out.at[:, pl.ds(s * PANEL, PANEL)], sem
-            )
-            cp.start()
-            cp.wait()
+def share_kernel(half, scal, c_ref, tok_in, out, tok_out, buf, sem):
+    cols = pl.ds(aligned((1 - scal[CORE]) * half, LANES), half)
+    for one, two in ((c_ref.at[:, cols], buf), (buf, out)):
+        cp = copy(one, two, sem)
+        cp.start()
+        cp.wait()
 
 
 def split3(x):
@@ -225,7 +239,7 @@
     (tok_in,) = take(1)
     ps_in = None if firsts[0] else take(1)[0]
     if c_chunks or last:
-        (a_ref,) = take(1)
+        a_refs = take(2)
     if c_chunks:
         c_ref, c_sib = take(2)
         sk_in, cout_in = (None, None) if firsts[1] else take(2)
@@ -234,6 +248,7 @@
     if c_chunks:
         sk, cout = take(2)
         rets = take(len(c_chunks))
+    totals = take(2) if last else []
     b_buf, s_buf, c_buf, b_sem, s_sem, c_sem, o_sem, g_sem = take(8)
     mine = scal[CORE] * half
     theirs = (1 - scal[CORE]) * half
@@ -316,18 +331,25 @@
             k = c_chunks.index(chunk)
             for cp in load_c(k):
                 cp.wait()
-            c = c_buf[k, :, :width].astype(jnp.float32) + fdot(a_ref[...], b)
-            c = c.astype(jnp.bfloat16)
-            c_buf[k, :, :width] = c
-            rets[k][...] = c[rows:]
-            store_c(k).start()
-            sk[...] += fdot(c, sm)
+            for h, a_ref in enumerate(a_refs):
+                part = slice(h * rows, (h + 1) * rows)
+                c = c_buf[k, part, :width].astype(jnp.float32) + fdot(a_ref[...], b)
+                c = c.astype(jnp.bfloat16)
+                if h == 0:
+                    c_buf[k, part, :width] = c
+                    store_c(k).start()
+                else:
+                    rets[k][...] = c
+                sk[part, :] += fdot(c, sm)
         if chunk in p_chunks:
             ps[...] += fdot(b, sm)
     if last:
         hi, mid, lo = split3(ps[...])
-        a = a_ref[...]
-        ps[: CORES * rows, :] = fdot(a, hi) + (fdot(a, mid) + fdot(a, lo))
+        cols = sk.shape[1]
+        for h, (a_ref, total) in enumerate(zip(a_refs, totals)):
+            a = a_ref[...]
+            total[:, :cols] = sk[h * rows : (h + 1) * rows, :]
+            total[:, cols:] = fdot(a, hi) + (fdot(a, mid) + fdot(a, lo))
     for i in range(len(c_chunks)):
         store_c(i).wait()
     for i in range(len(back)):
@@ -394,97 +416,87 @@
         at += width
         turn += 1
     n_chains = len(chains)
-    heads = [chunks[:HEAD] for chunks in chains]
-    tails = [chunks[HEAD:] for chunks in chains]
-
-    def staged(parts):
-        shapes, specs = [], []
-        for chunks, width in zip(parts, WIDTHS):
-            shapes += [like((STEPS, PANEL, width))] * (2 * len(chunks))
-            specs += [ANY] * (2 * len(chunks))
-        return tuple(shapes), tuple(specs)
-
-    def unpack(arrays, parts):
-        arrays = list(arrays)
-        return [
-            [(exchange(arrays.pop(0)), arrays.pop(0)) for _ in chunks] for chunks in parts
-        ]
-
-    def stage_scratch(parts):
-        out = []
-        for chunks, width in zip(parts, WIDTHS):
-            n = len(chunks)
-            out += [
-                pltpu.VMEM((2, n, STEPS, PANEL, width), jnp.bfloat16),
-                DMA((2, n, STEPS)),
-                DMA((2, n, STEPS)),
-            ]
-        return out
-
-    scal, cand, *staged_heads = call(
-        functools.partial(prologue_kernel, n_row, half, heads),
-        out_shape=(like((CORE + 1,), jnp.int32), like((rows, STEPS * PANEL))) + staged(heads)[0],
+    order_of = sorted(
+        ((j, c) for c in range(n_chains) for j in range(len(chains[c])))
+    )
+    flat = [chains[c][j] for j, c in order_of]
+    widest = max(WIDTHS)
+    scal, cand, tok, *others = call(
+        functools.partial(prologue_kernel, n_row, half, flat),
+        out_shape=(
+            like((CORE + 1,), jnp.int32),
+            like((rows, STEPS * PANEL)),
+            like((8, LANES)),
+        )
+        + tuple(like((STEPS, PANEL, width)) for _, width in flat),
         in_specs=[SMEM, ANY, ANY],
-        out_specs=(SMEM, ANY) + staged(heads)[1],
-        scratch_shapes=[pltpu.VMEM((rows, STEPS * PANEL), jnp.bfloat16), DMA((STEPS,))]
-        + stage_scratch(heads),
+        out_specs=(SMEM,) + (ANY,) * (2 + len(flat)),
+        scratch_shapes=[
+            pltpu.VMEM((rows, STEPS * PANEL), jnp.bfloat16),
+            pltpu.VMEM((len(flat), STEPS, PANEL, widest), jnp.bfloat16),
+            DMA((STEPS,)),
+            DMA((len(flat), STEPS)),
+            DMA((len(flat), STEPS)),
+        ],
         compiler_params=params(62),
     )(panel_ids, b_tile, a_tile)
-
-    feeds = unpack(staged_heads, heads)
-    tok = jnp.zeros((8, LANES), jnp.float32)
-
-    def inject(tok, c, t, recv, feed):
+    sibs = {(c, j): exchange(other) for (j, c), other in zip(order_of, others)}
+
+    mid = n_col // 2
+    hops = [[(i, i + 1) for i in range(mid - 1)] + [(i, i - 1) for i in range(mid + 1, n_col)]]
+    hops.append([(mid - 1, mid), (mid, mid - 1)])
+    hops.append([(j, i) for i, j in hops[0]])
+
+    def inject(tok, c, t, recv, hop=None, cand=None):
+        chunk = chains[c][t] if t < len(chains[c]) else None
         first = recv is None
-        args = [scal] + ([] if first else [recv]) + ([] if feed is None else list(feed)) + [tok]
+        args = [scal] + ([] if first else [recv])
         aliases = {} if first else {1: 0}
+        if chunk is not None:
+            args += [b_tile, sibs[c, t]]
+        outs = [like((STEPS, PANEL, WIDTHS[c])), like(tok.shape, tok.dtype)]
+        if hop is not None:
+            aliases[len(args) + 1] = 2
+            args += [lax.ppermute(cand, "col", hops[hop]), cand]
+            outs.append(like(cand.shape))
+        args.append(tok)
         return call(
-            functools.partial(inject_kernel, first, feed is None),
-            out_shape=(like((STEPS, PANEL, WIDTHS[c])), like(tok.shape, tok.dtype)),
+            functools.partial(inject_kernel, n_col, half, chunk, first, hop),
+            out_shape=tuple(outs),
             in_specs=[SMEM] + [ANY] * (len(args) - 1),
-            out_specs=(ANY, ANY),
+            out_specs=(ANY,) * len(outs),
             scratch_shapes=[
                 pltpu.VMEM((STEPS, PANEL, WIDTHS[c]), jnp.bfloat16),
                 DMA((STEPS, PARTS)),
                 DMA((STEPS, PARTS)),
+                pltpu.VMEM((rows, STEPS * PANEL), jnp.bfloat16),
+                DMA((2, STEPS)),
             ],
             input_output_aliases=aliases,
-            compiler_params=params(4),
+            compiler_params=params(40),
         )(*args)
 
     sends = [[] for _ in chains]
     flying = [None] * n_chains
     for c in range(n_chains):
-        sent, tok = inject(tok, c, 0, None, feeds[c][0])
+        sent, tok = inject(tok, c, 0, None)
         sends[c].append(sent)
         flying[c] = spread(sent)
-    def pick(tok, k, panels, piece, mine):
-        args = [scal, piece] + ([] if mine is None else [mine]) + [tok]
-        return call(
-            functools.partial(pick_kernel, n_col, k, panels),
-            out_shape=(like(cand.shape), like(tok.shape, tok.dtype)),
-            in_specs=[SMEM, ANY] + ([] if mine is None else [VMEM]) + [ANY],
-            out_specs=(VMEM, ANY),
-            scratch_shapes=[DMA],
-            input_output_aliases={} if mine is None else {2: 0},
-            compiler_params=params(4),
-        )(*args)
-
-    a_own, tok = pick(tok, 0, tuple(range(STEPS)), cand, None)
-    c_other = exchange(
-        lax.dynamic_slice_in_dim(c_prior, (1 - lax.axis_index("row") % CORES) * half, half, 1)
-    )
-    a_all = None
-    pieces = []
-    for k in sorted(range(1, n_col), key=lambda k: min(k, n_col - k)):
-        if 2 * k == n_col:
-            pieces += [(k, (s,)) for s in range(STEPS)]
-        else:
-            pieces.append((k, tuple(range(STEPS))))
+
+    c_other, tok = call(
+        functools.partial(share_kernel, half),
+        out_shape=(like((rows, half)), like(tok.shape, tok.dtype)),
+        in_specs=[SMEM, ANY, ANY],
+        out_specs=(ANY, ANY),
+        scratch_shapes=[pltpu.VMEM((rows, half), jnp.bfloat16), DMA],
+        compiler_params=params(4),
+    )(scal, c_prior, tok)
+    c_other = exchange(c_other)
 
     state = dict(ps=None, sk=None, cout=None, waiting=[])
 
-    def work(tok, p_ids, c_ids, last=False):
+    def work(tok, c_ids, last=False):
+        p_ids = c_ids
         where = lambda cj: chains[cj[0]][cj[1]]
         p_chunks = [where(cj) for cj in p_ids]
         c_chunks = [where(cj) for cj in c_ids]
@@ -511,8 +523,8 @@
             args.append(state["ps"])
             specs.append(VMEM)
         if c_ids or last:
-            args.append(a_all)
-            specs.append(VMEM)
+            args += a_all
+            specs += [VMEM, VMEM]
         if c_ids:
             args += [c_prior, c_other]
             specs += [ANY, ANY]
@@ -527,6 +539,9 @@
             out_specs += [VMEM, ANY]
             outs += [like((rows, w)) for _, w in c_chunks]
             out_specs += [VMEM] * len(c_chunks)
+        if last:
+            outs += [like((rows, 2 * sk_cols), jnp.float32)] * 2
+            out_specs += [VMEM] * 2
         m = max(1, len(c_ids))
         plan = (p_chunks, c_chunks, [spot for _, spot in back], firsts, last)
         got = call(
@@ -550,57 +565,39 @@
         tok, state["ps"] = got[:2]
         if c_ids:
             state["sk"], state["cout"] = got[2:4]
+            state["totals"] = got[4 + len(c_chunks) :]
             for ret, spot in zip(got[4:], c_chunks):
                 state["waiting"].append((exchange(ret), spot))
         return tok
 
-    p_todo, c_todo = [], []
+    c_todo = []
     n_steps = [len(chunks) + n_chips - 2 for chunks in chains]
     for t in range(1, max(n_steps) + 1):
-        if t == HEAD - 1:
-            *staged_tails, tok = call(
-                functools.partial(stage_kernel, half, tails),
-                out_shape=staged(tails)[0] + (like(tok.shape, tok.dtype),),
-                in_specs=[SMEM, ANY, ANY],
-                out_specs=staged(tails)[1] + (ANY,),
-                scratch_shapes=stage_scratch(tails),
-                compiler_params=params(62),
-            )(scal, b_tile, tok)
-            feeds = [old + new for old, new in zip(feeds, unpack(staged_tails, tails))]
         for c in range(n_chains):
             if t > n_steps[c]:
                 continue
-            if t < len(chains[c]):
-                sent, tok = inject(tok, c, t, flying[c], feeds[c][t])
+            if (t, c) in HOPS:
+                sent, tok, cand = inject(tok, c, t, flying[c], HOPS.index((t, c)), cand)
+                if (t, c) == HOPS[-1]:
+                    a_all = cand, exchange(cand)
             elif t < n_steps[c]:
-                sent, tok = inject(tok, c, t, flying[c], None)
+                sent, tok = inject(tok, c, t, flying[c])
             else:
                 sent = flying[c]
             sends[c].append(sent)
             if t < n_steps[c]:
                 flying[c] = spread(sent)
             if t >= n_chips - 1:
-                p_todo.append((c, t - n_chips + 1))
                 c_todo.append((c, t - n_chips + 1))
-            if c == n_chains - 1 and a_all is None:
-                for k, panels in pieces[:1] if t < LAST_PIECE else pieces:
-                    way = [(i, (i + k) % n_col) for i in range(n_col)]
-                    piece = cand
-                    if len(panels) == 1:
-                        piece = cand[:, panels[0] * PANEL : (panels[0] + 1) * PANEL]
-                    a_own, tok = pick(tok, k, panels, lax.ppermute(piece, "col", way), a_own)
-                pieces = pieces[1:] if t < LAST_PIECE else []
-                if not pieces:
-                    a_all = jnp.concatenate([a_own, exchange(a_own)], 0)
             if t == max(n_steps) and all(len(sends[k]) > n_steps[k] for k in range(n_chains)):
                 continue
-            c_ids = c_todo[:C_MOST] if a_all is not None else []
+            c_ids = c_todo[:C_MOST] if t >= HOPS[-1][0] else []
             if c < n_chains - 1 and t <= min(n_steps):
                 continue
-            if p_todo or c_ids:
-                tok = work(tok, p_todo, c_ids)
-                p_todo, c_todo = [], c_todo[len(c_ids) :]
-    tok = work(tok, p_todo, c_todo, True)
+            if c_ids:
+                tok = work(tok, c_ids)
+                c_todo = c_todo[len(c_ids) :]
+    tok = work(tok, c_todo, True)
 
     back = state["waiting"]
     cout = call(
@@ -613,10 +610,8 @@
         compiler_params=params(4),
     )(scal, *[got for got, _ in back], state["cout"])
 
-    sk, ps = state["sk"], state["ps"]
-    mine = jnp.concatenate([sk[:rows], ps[:rows]], 1)
-    theirs = exchange(jnp.concatenate([sk[rows:], ps[rows : 2 * rows]], 1))
-    total = mine + theirs
+    mine, theirs = state["totals"]
+    total = mine + exchange(theirs)
     z = lax.axis_index("col")
     share = rows // n_col
     shift = lambda k: [(i, (i + k) % n_col) for i in range(n_col)]
@@ -650,6 +645,7 @@
             and a_tile.shape[1] % PANEL == 0
             and CORES * rows <= STEPS * PANEL
             and rows % (8 * n_col) == 0
+            and n_col == 4
         )
         if not fits:
             return plain(a_tile, b_tile, c_prior, sketch_matrix, panel_ids)

time: 162 us -> 147 us (0.907)
  starting transfers between devices: 29.3 us -> 61.3 us
  Pallas kernels: 73.1 us -> 41.8 us
  local copies, waits for them, and re-layouts: 13.4 us -> 2.27 us
  waiting for transfers between devices: 44.5 us -> 39.9 us
    ppermute x17, starting transfers between devices: 6.63 us -> 40.3 us  [spread(): return lax.ppermute(x, 'row', around)]
    pallas_call x24 -> x19, Pallas kernels: 45 us -> 16.8 us  [the longest x17 12.3 us: inject(): call(functools.partial(inject_kernel, n_col, half, chunk, first, hop), ou...]
    unnamed x69 -> x32, local copies, waits for them, and re-layouts: 12.4 us -> 1.49 us
    ppermute x17, waiting for transfers between devices: 27.1 us -> 16.4 us  [spread(): return lax.ppermute(x, 'row', around)]
    ppermute x4 -> x3, waiting for transfers between devices: 5.7 us -> 12.7 us  [inject(): args += [lax.ppermute(cand, 'col', hops[hop]), cand]]
    pallas_call x7 -> x6, Pallas kernels: 26.8 us -> 23.6 us  [work(): call(functools.partial(work_kernel, plan, n_chips, half), out_shape=tuple...]
    ppermute x4 -> x3, starting transfers between devices: 7.19 us -> 6.89 us  [inject(): args += [lax.ppermute(cand, 'col', hops[hop]), cand]]
  transfers between devices with their start and end apart: 56 -> 55, of which waited for: 24 -> 20; matrix products, arithmetic and copies ran while one was open for 0% -> 0% of each run, Pallas kernels for 40% -> 24%
where the time goes in v2:
time: 147 us; the launch traced here: 146 us
  starting transfers between devices  61.3 us (42%)
  Pallas kernels  41.8 us (28%)
  waiting for transfers between devices  39.9 us (27%)
  local copies, waits for them, and re-layouts  2.27 us (2%)
    ppermute x17, starting transfers between devices, spread(): return lax.ppermute(x, 'row', around)  40.3 us
    pallas_call x6, Pallas kernels, work(): call(functools.partial(work_kernel, plan, n_chips, half), out_shape=tuple...  23.6 us
    ppermute x17, waiting for transfers between devices, spread(): return lax.ppermute(x, 'row', around)  16.4 us
    ppermute x3, waiting for transfers between devices, inject(): args += [lax.ppermute(cand, 'col', hops[hop]), cand]  12.7 us
    pallas_call x17, Pallas kernels, inject(): call(functools.partial(inject_kernel, n_col, half, chunk, first, hop), ou...  12.3 us
    ppermute x3, starting transfers between devices, inject(): args += [lax.ppermute(cand, 'col', hops[hop]), cand]  6.89 us
    ppermute x29, starting transfers between devices, exchange(): return lax.ppermute(x, 'row', swap)  6.1 us
    ppermute x3, waiting for transfers between devices, ring_form(): lax.ppermute(part, 'col', shift(k))  4.19 us
  transfers between devices with their start and end apart: 55, of which 20 were waited for; matrix products, arithmetic and copies ran while one was open for 0% of the time, Pallas kernels for 24%

profile of v2, /device:TPU:0, one launch (start us, length us, event | category | flops | bytes accessed | tf_op | source)
XLA Modules:
  0.0 146.5 jit_solution(2766284302817278258)
XLA Ops:
  0.6 3.5 %shard_map.76 = (s32[11]{0:T(128)}, bf16[256,1024]{1,0:T(8,128)(2,1)}, bf16[8,128]{1,0:T(8,128)(2,1)}, bf16[2,512,256]{2,1,0:T(8,128)(2,1)}, bf16[2,512,256]{2,1...) custom-call(s32[2]{0:T(128)} %ids.1, ...), custom_call_target="tpu_custom_call" | custom-call | flops 1 | bytes 1 | tf_op jit(solution)/shard_map/pallas_call | solution.py:424
  4.8 4.9 %collective-permute-start.3 = (bf16[256,1024]{1,0:T(8,128)(2,1)}, bf16[256,1024]{1,0:T(8,128)(2,1)S(1)}, u32[]{:S(2)}, u32[]{:S(2)}) collective-permute-start(bf16[256,1024]{1,0:T(8,128)(2,1)} %get-tuple-element.99.refs_4_), channel_id=1, source_target_pairs={{0,1},{3,2},{4,5},{7,6},{8,9},{11,10},{12,13},{15,14},{16,17},{19,... | collective-permute-start | bytes 1572872 | tf_op jit(solution)/shard_map/ppermute | solution.py:460
  11.9 3.5 %collective-permute-start.1 = (bf16[2,512,256]{2,1,0:T(8,128)(2,1)S(1)}, bf16[2,512,256]{2,1,0:T(8,128)(2,1)S(1)}, u32[]{:S(2)}, u32[]{:S(2)}) collective-permute-start(bf16[2,512,256]{2,1,0:T(8,128)(2,1)S(1)} %get-tuple-element.97.refs_2_), channel_id=1, source_target_pairs={{0,8},{4,20},{8,24},{12,4},{16,0},{20,28},{24,16},{28,12},{1,9},{5... | collective-permute-start | bytes 1572872 | tf_op jit(solution)/shard_map/ppermute | solution.py:403
  16.2 3.2 %collective-permute-start.7 = (bf16[2,512,256]{2,1,0:T(8,128)(2,1)S(1)}, bf16[2,512,256]{2,1,0:T(8,128)(2,1)S(1)}, u32[]{:S(2)}, u32[]{:S(2)}) collective-permute-start(bf16[2,512,256]{2,1,0:T(8,128)(2,1)S(1)} %get-tuple-element.106.refs_6_), channel_id=1, source_target_pairs={{0,8},{4,20},{8,24},{12,4},{16,0},{20,28},{24,16},{28,12},{1,9},{5... | collective-permute-start | bytes 1572872 | tf_op jit(solution)/shard_map/ppermute | solution.py:403
  19.4 2.0 %collective-permute-done.3.refs_3_ = bf16[256,1024]{1,0:T(8,128)(2,1)S(1)} collective-permute-done((bf16[256,1024]{1,0:T(8,128)(2,1)}, bf16[256,1024]{1,0:T(8,128)(2,1)S(1)}, u32[]{:S(2)}, u32[]{:S(2)}) %collective-permute-start.3) | collective-permute-done | bytes 524320 | tf_op jit(solution)/shard_map/ppermute | solution.py:460
  21.4 1.0 shard_map.79
  23.2 3.7 %collective-permute-start.5 = (bf16[2,512,256]{2,1,0:T(8,128)(2,1)S(1)}, bf16[2,512,256]{2,1,0:T(8,128)(2,1)S(1)}, u32[]{:S(2)}, u32[]{:S(2)}) collective-permute-start(bf16[2,512,256]{2,1,0:T(8,128)(2,1)S(1)} %get-tuple-element.104.refs_3_.refs_10_), channel_id=1, source_target_pairs={{0,8},{4,20},{8,24},{12,4},{16,0},{20,28},{24,16},{28,12},{1,9},{5... | collective-permute-start | bytes 1572872 | tf_op jit(solution)/shard_map/ppermute | solution.py:403
  28.4 3.2 %collective-permute-start.11 = (bf16[2,512,256]{2,1,0:T(8,128)(2,1)S(1)}, bf16[2,512,256]{2,1,0:T(8,128)(2,1)S(1)}, u32[]{:S(2)}, u32[]{:S(2)}) collective-permute-start(bf16[2,512,256]{2,1,0:T(8,128)(2,1)S(1)} %get-tuple-element.112.refs_7_.refs_2_), channel_id=1, source_target_pairs={{0,8},{4,20},{8,24},{12,4},{16,0},{20,28},{24,16},{28,12},{1,9},{5... | collective-permute-start | bytes 1572872 | tf_op jit(solution)/shard_map/ppermute | solution.py:403
  32.4 1.3 collective-permute-done.5.refs_0_
  35.3 2.5 %collective-permute-start.9 = (bf16[2,512,256]{2,1,0:T(8,128)(2,1)S(1)}, bf16[2,512,256]{2,1,0:T(8,128)(2,1)S(1)}, u32[]{:S(2)}, u32[]{:S(2)}) collective-permute-start(bf16[2,512,256]{2,1,0:T(8,128)(2,1)S(1)} %get-tuple-element.110.refs_4_.refs_11_.refs_6_), channel_id=1, source_target_pairs={{0,8},{4,20},{8,24},{12,4},{16,0},{20,28},{24,16},{28,12},{1,9},{5... | collective-permute-start | bytes 1572872 | tf_op jit(solution)/shard_map/ppermute | solution.py:403
  37.8 1.5 %collective-permute-done.11.refs_0_ = bf16[2,512,256]{2,1,0:T(8,128)(2,1)S(1)} collective-permute-done((bf16[2,512,256]{2,1,0:T(8,128)(2,1)S(1)}, bf16[2,512,256]{2,1,0:T(8,128)(2,1)S(1)}, u32[]{:S(2)}, u32[]{:S(2)}) %collective-permute-start.11) | collective-permute-done | bytes 524320 | tf_op jit(solution)/shard_map/ppermute | solution.py:403
  41.0 2.5 %collective-permute-start.17 = (bf16[2,512,256]{2,1,0:T(8,128)(2,1)S(1)}, bf16[2,512,256]{2,1,0:T(8,128)(2,1)S(1)}, u32[]{:S(2)}, u32[]{:S(2)}) collective-permute-start(bf16[2,512,256]{2,1,0:T(8,128)(2,1)S(1)} %get-tuple-element.120.refs_8_.refs_3_.refs_10_), channel_id=1, source_target_pairs={{0,8},{4,20},{8,24},{12,4},{16,0},{20,28},{24,16},{28,12},{1,9},{5... | collective-permute-start | bytes 1572872 | tf_op jit(solution)/shard_map/ppermute | solution.py:403
  43.5 1.5 collective-permute-done.9.refs_0_
  44.9 1.3 collective-permute-start.16
  47.0 3.2 %collective-permute-start.14 = (bf16[2,512,256]{2,1,0:T(8,128)(2,1)S(1)}, bf16[2,512,256]{2,1,0:T(8,128)(2,1)S(1)}, u32[]{:S(2)}, u32[]{:S(2)}) collective-permute-start(bf16[2,512,256]{2,1,0:T(8,128)(2,1)S(1)} %get-tuple-element.117.refs_5_.refs_12_.refs_7_.refs_2_), channel_id=1, source_target_pairs={{0,8},{4,20},{8,24},{12,4},{16,0},{20,28},{24,16},{28,12},{1,9},{5... | collective-permute-start | bytes 1572872 | tf_op jit(solution)/shard_map/ppermute | solution.py:403
  50.5 0.9 collective-permute-start.22
  52.1 2.5 %collective-permute-start.21 = (bf16[2,512,256]{2,1,0:T(8,128)(2,1)S(1)}, bf16[2,512,256]{2,1,0:T(8,128)(2,1)S(1)}, u32[]{:S(2)}, u32[]{:S(2)}) collective-permute-start(bf16[2,512,256]{2,1,0:T(8,128)(2,1)S(1)} %get-tuple-element.126.refs_9_.refs_4_.refs_11_.refs_6_), channel_id=1, source_target_pairs={{0,8},{4,20},{8,24},{12,4},{16,0},{20,28},{24,16},{28,12},{1,9},{5... | collective-permute-start | bytes 1572872 | tf_op jit(solution)/shard_map/ppermute | solution.py:403
  54.6 10.6 %collective-permute-done.16.refs_3_ = bf16[256,1024]{1,0:T(8,128)(2,1)S(1)} collective-permute-done((bf16[256,1024]{1,0:T(8,128)(2,1)S(1)}, bf16[256,1024]{1,0:T(8,128)(2,1)S(1)}, u32[]{:S(2)}, u32[]{:S(2)}) %collective-permute-start.16) | collective-permute-done | bytes 524320 | tf_op jit(solution)/shard_map/ppermute | solution.py:460
  66.7 1.7 %collective-permute-start.19 = (bf16[2,512,256]{2,1,0:T(8,128)(2,1)S(1)}, bf16[2,512,256]{2,1,0:T(8,128)(2,1)S(1)}, u32[]{:S(2)}, u32[]{:S(2)}) collective-permute-start(bf16[2,512,256]{2,1,0:T(8,128)(2,1)S(1)} %get-tuple-element.124.refs_13_.refs_8_.refs_3_.refs_2_), channel_id=1, source_target_pairs={{0,8},{4,20},{8,24},{12,4},{16,0},{20,28},{24,16},{28,12},{1,9},{5... | collective-permute-start | bytes 1572872 | tf_op jit(solution)/shard_map/ppermute | solution.py:403
  69.2 1.3 collective-permute-start.27
  70.4 4.9 %shard_map.88 = (bf16[8,128]{1,0:T(8,128)(2,1)S(1)}, f32[1024,128]{1,0:T(8,128)S(1)}, f32[512,128]{1,0:T(8,128)S(1)}, bf16[256,6656]{1,0:T(8,128)(2,1)}, bf16[25...) custom-call(s32[11]{0:T(128)S(1)} %copy-done.3, ...), custom_call_target="tpu_custom_call" | custom-call | flops 1 | bytes 1 | tf_op jit(solution)/shard_map/pallas_call | solution.py:547
  76.6 2.4 %collective-permute-start.25 = (bf16[2,512,256]{2,1,0:T(8,128)(2,1)S(1)}, bf16[2,512,256]{2,1,0:T(8,128)(2,1)S(1)}, u32[]{:S(2)}, u32[]{:S(2)}) collective-permute-start(bf16[2,512,256]{2,1,0:T(8,128)(2,1)S(1)} %get-tuple-element.133.refs_9_.refs_4_.refs_3_.refs_2_), channel_id=1, source_target_pairs={{0,8},{4,20},{8,24},{12,4},{16,0},{20,28},{24,16},{28,12},{1,9},{5... | collective-permute-start | bytes 1572872 | tf_op jit(solution)/shard_map/ppermute | solution.py:403
  79.0 2.5 %collective-permute-done.27.refs_0_ = bf16[2,512,256]{2,1,0:T(8,128)(2,1)S(1)} collective-permute-done((bf16[2,512,256]{2,1,0:T(8,128)(2,1)S(1)}, bf16[2,512,256]{2,1,0:T(8,128)(2,1)S(1)}, u32[]{:S(2)}, u32[]{:S(2)}) %collective-permute-start.27) | collective-permute-done | bytes 524320 | tf_op jit(solution)/shard_map/ppermute | solution.py:403
  82.2 2.4 %collective-permute-start.31 = (bf16[2,512,256]{2,1,0:T(8,128)(2,1)S(1)}, bf16[2,512,256]{2,1,0:T(8,128)(2,1)S(1)}, u32[]{:S(2)}, u32[]{:S(2)}) collective-permute-start(bf16[2,512,256]{2,1,0:T(8,128)(2,1)S(1)} %get-tuple-element.138.refs_13_.refs_8_.refs_7_.refs_6_), channel_id=1, source_target_pairs={{0,8},{4,20},{8,24},{12,4},{16,0},{20,28},{24,16},{28,12},{1,9},{5... | collective-permute-start | bytes 1572872 | tf_op jit(solution)/shard_map/ppermute | solution.py:403
  84.6 5.3 %shard_map.91 = (bf16[8,128]{1,0:T(8,128)(2,1)S(1)}, f32[1024,128]{1,0:T(8,128)S(1)}, f32[512,128]{1,0:T(8,128)S(1)}, bf16[256,6656]{1,0:T(8,128)(2,1)}, bf16[25...) custom-call(s32[11]{0:T(128)S(1)} %copy-done.3, ...), custom_call_target="tpu_custom_call", output_to_operand_aliasing={{1}: (15, {}), {2}: (20, {}), {3}: (21, {})} | custom-call | flops 1 | bytes 1 | tf_op jit(solution)/shard_map/pallas_call | solution.py:547
  90.7 1.9 %collective-permute-start.30 = (bf16[2,512,256]{2,1,0:T(8,128)(2,1)S(1)}, bf16[2,512,256]{2,1,0:T(8,128)(2,1)S(1)}, u32[]{:S(2)}, u32[]{:S(2)}) collective-permute-start(bf16[2,512,256]{2,1,0:T(8,128)(2,1)S(1)} %get-tuple-element.145.refs_5_.refs_4_.refs_3_.refs_2_), channel_id=1, source_target_pairs={{0,8},{4,20},{8,24},{12,4},{16,0},{20,28},{24,16},{28,12},{1,9},{5... | collective-permute-start | bytes 1572872 | tf_op jit(solution)/shard_map/ppermute | solution.py:403
  93.8 1.3 collective-permute-start.36
  95.1 3.4 %shard_map.94 = (bf16[8,128]{1,0:T(8,128)(2,1)S(1)}, f32[1024,128]{1,0:T(8,128)S(1)}, f32[512,128]{1,0:T(8,128)S(1)}, bf16[256,6656]{1,0:T(8,128)(2,1)}, bf16[25...) custom-call(s32[11]{0:T(128)S(1)} %copy-done.3, ...), custom_call_target="tpu_custom_call", output_to_operand_aliasing={{1}: (11, {}), {2}: (16, {}), {3}: (17, {})} | custom-call | flops 1 | bytes 1 | tf_op jit(solution)/shard_map/pallas_call | solution.py:547
  98.6 1.5 %collective-permute-done.30.refs_0_ = bf16[2,512,256]{2,1,0:T(8,128)(2,1)S(1)} collective-permute-done((bf16[2,512,256]{2,1,0:T(8,128)(2,1)S(1)}, bf16[2,512,256]{2,1,0:T(8,128)(2,1)S(1)}, u32[]{:S(2)}, u32[]{:S(2)}) %collective-permute-start.30) | collective-permute-done | bytes 524320 | tf_op jit(solution)/shard_map/ppermute | solution.py:403
  100.7 1.8 %collective-permute-start.35 = (bf16[2,512,256]{2,1,0:T(8,128)(2,1)S(1)}, bf16[2,512,256]{2,1,0:T(8,128)(2,1)S(1)}, u32[]{:S(2)}, u32[]{:S(2)}) collective-permute-start(bf16[2,512,256]{2,1,0:T(8,128)(2,1)S(1)} %get-tuple-element.156.refs_5_.refs_4_.refs_3_), channel_id=1, source_target_pairs={{0,8},{4,20},{8,24},{12,4},{16,0},{20,28},{24,16},{28,12},{1,9},{5... | collective-permute-start | bytes 1572872 | tf_op jit(solution)/shard_map/ppermute | solution.py:403
  103.0 2.7 %collective-permute-done.36.refs_0_ = bf16[2,512,256]{2,1,0:T(8,128)(2,1)S(1)} collective-permute-done((bf16[2,512,256]{2,1,0:T(8,128)(2,1)S(1)}, bf16[2,512,256]{2,1,0:T(8,128)(2,1)S(1)}, u32[]{:S(2)}, u32[]{:S(2)}) %collective-permute-start.36) | collective-permute-done | bytes 524320 | tf_op jit(solution)/shard_map/ppermute | solution.py:403
  106.4 1.8 %collective-permute-start.39 = (bf16[2,512,256]{2,1,0:T(8,128)(2,1)S(1)}, bf16[2,512,256]{2,1,0:T(8,128)(2,1)S(1)}, u32[]{:S(2)}, u32[]{:S(2)}) collective-permute-start(bf16[2,512,256]{2,1,0:T(8,128)(2,1)S(1)} %get-tuple-element.158.refs_9_.refs_8_), channel_id=1, source_target_pairs={{0,8},{4,20},{8,24},{12,4},{16,0},{20,28},{24,16},{28,12},{1,9},{5... | collective-permute-start | bytes 1572872 | tf_op jit(solution)/shard_map/ppermute | solution.py:403
  108.1 3.4 %shard_map.97 = (bf16[8,128]{1,0:T(8,128)(2,1)S(1)}, f32[1024,128]{1,0:T(8,128)S(1)}, f32[512,128]{1,0:T(8,128)S(1)}, bf16[256,6656]{1,0:T(8,128)(2,1)}, bf16[25...) custom-call(s32[11]{0:T(128)S(1)} %copy-done.3, ...), custom_call_target="tpu_custom_call", output_to_operand_aliasing={{1}: (11, {}), {2}: (16, {}), {3}: (17, {})} | custom-call | flops 1 | bytes 1 | tf_op jit(solution)/shard_map/pallas_call | solution.py:547
  112.2 1.5 %collective-permute-start.44 = (bf16[2,512,256]{2,1,0:T(8,128)(2,1)S(1)}, bf16[2,512,256]{2,1,0:T(8,128)(2,1)S(1)}, u32[]{:S(2)}, u32[]{:S(2)}) collective-permute-start(bf16[2,512,256]{2,1,0:T(8,128)(2,1)S(1)} %get-tuple-element.166.refs_5_.refs_4_), channel_id=1, source_target_pairs={{0,8},{4,20},{8,24},{12,4},{16,0},{20,28},{24,16},{28,12},{1,9},{5... | collective-permute-start | bytes 1572872 | tf_op jit(solution)/shard_map/ppermute | solution.py:403
  115.3 1.7 %collective-permute-done.39.refs_9_ = bf16[2,512,256]{2,1,0:T(8,128)(2,1)S(1)} collective-permute-done((bf16[2,512,256]{2,1,0:T(8,128)(2,1)S(1)}, bf16[2,512,256]{2,1,0:T(8,128)(2,1)S(1)}, u32[]{:S(2)}, u32[]{:S(2)}) %collective-permute-start.39) | collective-permute-done | bytes 524320 | tf_op jit(solution)/shard_map/ppermute | solution.py:403
  116.9 3.4 %shard_map.99 = (bf16[8,128]{1,0:T(8,128)(2,1)S(1)}, f32[1024,128]{1,0:T(8,128)S(1)}, f32[512,128]{1,0:T(8,128)S(1)}, bf16[256,6656]{1,0:T(8,128)(2,1)}, bf16[25...) custom-call(s32[11]{0:T(128)S(1)} %copy-done.3, ...), custom_call_target="tpu_custom_call", output_to_operand_aliasing={{1}: (11, {}), {2}: (16, {}), {3}: (17, {})} | custom-call | flops 1 | bytes 1 | tf_op jit(solution)/shard_map/pallas_call | solution.py:547
  120.4 2.2 %collective-permute-done.44.refs_5_ = bf16[2,512,256]{2,1,0:T(8,128)(2,1)S(1)} collective-permute-done((bf16[2,512,256]{2,1,0:T(8,128)(2,1)S(1)}, bf16[2,512,256]{2,1,0:T(8,128)(2,1)S(1)}, u32[]{:S(2)}, u32[]{:S(2)}) %collective-permute-start.44) | collective-permute-done | bytes 524320 | tf_op jit(solution)/shard_map/ppermute | solution.py:403
  122.6 3.2 %shard_map.100 = (bf16[8,128]{1,0:T(8,128)(2,1)}, f32[1024,128]{1,0:T(8,128)S(1)}, f32[512,128]{1,0:T(8,128)S(1)}, bf16[256,6656]{1,0:T(8,128)(2,1)}, bf16[256,2...) custom-call(s32[11]{0:T(128)S(1)} %copy-done.3, ...), custom_call_target="tpu_custom_call", output_to_operand_aliasing={{1}: (7, {}), {2}: (12, {}), {3}: (13, {})} | custom-call | flops 1 | bytes 1 | tf_op jit(solution)/shard_map/pallas_call | solution.py:547
  125.9 1.5 %collective-permute-done.48 = f32[256,256]{1,0:T(8,128)S(1)} collective-permute-done((f32[256,256]{1,0:T(8,128)S(1)}, f32[256,256]{1,0:T(8,128)S(1)}, u32[]{:S(2)}, u32[]{:S(2)}) %collective-permute-start.48) | collective-permute-done | bytes 262176 | tf_op jit(solution)/shard_map/ppermute | solution.py:406
  127.5 3.0 %collective-permute-start.50 = (f32[64,256]{1,0:T(8,128)S(1)}, f32[64,256]{1,0:T(8,128)S(1)}, u32[]{:S(2)}, u32[]{:S(2)}) collective-permute-start(f32[64,256]{1,0:T(8,128)S(1)} %get-tuple-element.191), channel_id=1, source_target_pairs={{0,2},{1,3},{2,0},{3,1},{4,6},{5,7},{6,4},{7,5},{8,10},{9,11},{10,... | collective-permute-start | bytes 196616 | tf_op jit(solution)/shard_map/ppermute | solution.py:621
  130.5 1.0 collective-permute-start.51
  132.0 2.3 %collective-permute-done.49 = f32[64,256]{1,0:T(8,128)S(1)} collective-permute-done((f32[64,256]{1,0:T(8,128)S(1)}, f32[64,256]{1,0:T(8,128)S(1)}, u32[]{:S(2)}, u32[]{:S(2)}) %collective-permute-start.49) | collective-permute-done | bytes 65568 | tf_op jit(solution)/shard_map/ppermute | solution.py:621
  134.3 1.9 %collective-permute-done.50 = f32[64,256]{1,0:T(8,128)S(1)} collective-permute-done((f32[64,256]{1,0:T(8,128)S(1)}, f32[64,256]{1,0:T(8,128)S(1)}, u32[]{:S(2)}, u32[]{:S(2)}) %collective-permute-start.50) | collective-permute-done | bytes 65568 | tf_op jit(solution)/shard_map/ppermute | solution.py:621
  136.2 1.4 collective-permute-start.52
  137.6 1.3 shard_map.101
  139.0 2.0 %collective-permute-start.53 = (f32[64,256]{1,0:T(8,128)S(1)}, f32[64,256]{1,0:T(8,128)S(1)}, u32[]{:S(2)}, u32[]{:S(2)}) collective-permute-start(f32[64,256]{1,0:T(8,128)S(1)} %get-tuple-element.186), channel_id=1, source_target_pairs={{0,2},{1,3},{2,0},{3,1},{4,6},{5,7},{6,4},{7,5},{8,10},{9,11},{10,... | collective-permute-start | bytes 196616 | tf_op jit(solution)/shard_map/ppermute | solution.py:626
  141.5 1.6 %collective-permute-done.52 = f32[64,256]{1,0:T(8,128)S(1)} collective-permute-done((f32[64,256]{1,0:T(8,128)S(1)}, f32[64,256]{1,0:T(8,128)S(1)}, u32[]{:S(2)}, u32[]{:S(2)}) %collective-permute-start.52) | collective-permute-done | bytes 65568 | tf_op jit(solution)/shard_map/ppermute | solution.py:626
  143.2 2.2 %collective-permute-done.53 = f32[64,256]{1,0:T(8,128)S(1)} collective-permute-done((f32[64,256]{1,0:T(8,128)S(1)}, f32[64,256]{1,0:T(8,128)S(1)}, u32[]{:S(2)}, u32[]{:S(2)}) %collective-permute-start.53) | collective-permute-done | bytes 65568 | tf_op jit(solution)/shard_map/ppermute | solution.py:626
  (128 shorter events, 24.2 us)
Async XLA Ops:
  4.2 5.6 %collective-permute-start = (bf16[2,512,256]{2,1,0:T(8,128)(2,1)}, bf16[2,512,256]{2,1,0:T(8,128)(2,1)S(1)}, u32[]{:S(2)}, u32[]{:S(2)}) collective-permute-start(bf16[2,512,256]{2,1,0:T(8,128)(2,1)} %get-tuple-element.95), channel_id=1, source_target_pairs={{0,4},{4,0},{8,12},{12,8},{16,20},{20,16},{24,28},{28,24},{1,5},{5... | collective-permute-start | bytes 1572872 | tf_op jit(solution)/shard_map/ppermute | solution.py:406
  4.7 10.7 %collective-permute-start.4 = (bf16[2,512,256]{2,1,0:T(8,128)(2,1)}, bf16[2,512,256]{2,1,0:T(8,128)(2,1)S(1)}, u32[]{:S(2)}, u32[]{:S(2)}) collective-permute-start(bf16[2,512,256]{2,1,0:T(8,128)(2,1)} %get-tuple-element.100), channel_id=1, source_target_pairs={{0,4},{4,0},{8,12},{12,8},{16,20},{20,16},{24,28},{28,24},{1,5},{5... | collective-permute-start | bytes 1572872 | tf_op jit(solution)/shard_map/ppermute | solution.py:406
  4.8 16.6 %collective-permute-start.3 = (bf16[256,1024]{1,0:T(8,128)(2,1)}, bf16[256,1024]{1,0:T(8,128)(2,1)S(1)}, u32[]{:S(2)}, u32[]{:S(2)}) collective-permute-start(bf16[256,1024]{1,0:T(8,128)(2,1)} %get-tuple-element.99.refs_4_), channel_id=1, source_target_pairs={{0,1},{3,2},{4,5},{7,6},{8,9},{11,10},{12,13},{15,14},{16,17},{19,... | collective-permute-start | bytes 1572872 | tf_op jit(solution)/shard_map/ppermute | solution.py:460
  9.7 12.7 %collective-permute-start.2 = (bf16[2,512,256]{2,1,0:T(8,128)(2,1)}, bf16[2,512,256]{2,1,0:T(8,128)(2,1)S(1)}, u32[]{:S(2)}, u32[]{:S(2)}) collective-permute-start(bf16[2,512,256]{2,1,0:T(8,128)(2,1)} %get-tuple-element.98), channel_id=1, source_target_pairs={{0,4},{4,0},{8,12},{12,8},{16,20},{20,16},{24,28},{28,24},{1,5},{5... | collective-permute-start | bytes 1572872 | tf_op jit(solution)/shard_map/ppermute | solution.py:406
  11.9 10.5 %collective-permute-start.1 = (bf16[2,512,256]{2,1,0:T(8,128)(2,1)S(1)}, bf16[2,512,256]{2,1,0:T(8,128)(2,1)S(1)}, u32[]{:S(2)}, u32[]{:S(2)}) collective-permute-start(bf16[2,512,256]{2,1,0:T(8,128)(2,1)S(1)} %get-tuple-element.97.refs_2_), channel_id=1, source_target_pairs={{0,8},{4,20},{8,24},{12,4},{16,0},{20,28},{24,16},{28,12},{1,9},{5... | collective-permute-start | bytes 1572872 | tf_op jit(solution)/shard_map/ppermute | solution.py:403
  15.4 11.6 %collective-permute-start.8 = (bf16[2,512,256]{2,1,0:T(8,128)(2,1)S(1)}, bf16[2,512,256]{2,1,0:T(8,128)(2,1)S(1)}, u32[]{:S(2)}, u32[]{:S(2)}) collective-permute-start(bf16[2,512,256]{2,1,0:T(8,128)(2,1)S(1)} %copy-done.15), channel_id=1, source_target_pairs={{0,4},{4,0},{8,12},{12,8},{16,20},{20,16},{24,28},{28,24},{1,5},{5... | collective-permute-start | bytes 1572872 | tf_op jit(solution)/shard_map/ppermute | solution.py:406
  16.2 11.5 %collective-permute-start.7 = (bf16[2,512,256]{2,1,0:T(8,128)(2,1)S(1)}, bf16[2,512,256]{2,1,0:T(8,128)(2,1)S(1)}, u32[]{:S(2)}, u32[]{:S(2)}) collective-permute-start(bf16[2,512,256]{2,1,0:T(8,128)(2,1)S(1)} %get-tuple-element.106.refs_6_), channel_id=1, source_target_pairs={{0,8},{4,20},{8,24},{12,4},{16,0},{20,28},{24,16},{28,12},{1,9},{5... | collective-permute-start | bytes 1572872 | tf_op jit(solution)/shard_map/ppermute | solution.py:403
  21.4 10.9 %collective-permute-start.6 = (bf16[2,512,256]{2,1,0:T(8,128)(2,1)S(1)}, bf16[2,512,256]{2,1,0:T(8,128)(2,1)S(1)}, u32[]{:S(2)}, u32[]{:S(2)}) collective-permute-start(bf16[2,512,256]{2,1,0:T(8,128)(2,1)S(1)} %copy-done.14), channel_id=1, source_target_pairs={{0,4},{4,0},{8,12},{12,8},{16,20},{20,16},{24,28},{28,24},{1,5},{5... | collective-permute-start | bytes 1572872 | tf_op jit(solution)/shard_map/ppermute | solution.py:406
  23.2 10.4 %collective-permute-start.5 = (bf16[2,512,256]{2,1,0:T(8,128)(2,1)S(1)}, bf16[2,512,256]{2,1,0:T(8,128)(2,1)S(1)}, u32[]{:S(2)}, u32[]{:S(2)}) collective-permute-start(bf16[2,512,256]{2,1,0:T(8,128)(2,1)S(1)} %get-tuple-element.104.refs_3_.refs_10_), channel_id=1, source_target_pairs={{0,8},{4,20},{8,24},{12,4},{16,0},{20,28},{24,16},{28,12},{1,9},{5... | collective-permute-start | bytes 1572872 | tf_op jit(solution)/shard_map/ppermute | solution.py:403
  27.0 8.3 %collective-permute-start.12 = (bf16[2,512,256]{2,1,0:T(8,128)(2,1)S(1)}, bf16[2,512,256]{2,1,0:T(8,128)(2,1)S(1)}, u32[]{:S(2)}, u32[]{:S(2)}) collective-permute-start(bf16[2,512,256]{2,1,0:T(8,128)(2,1)S(1)} %copy-done.13), channel_id=1, source_target_pairs={{0,4},{4,0},{8,12},{12,8},{16,20},{20,16},{24,28},{28,24},{1,5},{5... | collective-permute-start | bytes 1572872 | tf_op jit(solution)/shard_map/ppermute | solution.py:406
  28.4 10.9 %collective-permute-start.11 = (bf16[2,512,256]{2,1,0:T(8,128)(2,1)S(1)}, bf16[2,512,256]{2,1,0:T(8,128)(2,1)S(1)}, u32[]{:S(2)}, u32[]{:S(2)}) collective-permute-start(bf16[2,512,256]{2,1,0:T(8,128)(2,1)S(1)} %get-tuple-element.112.refs_7_.refs_2_), channel_id=1, source_target_pairs={{0,8},{4,20},{8,24},{12,4},{16,0},{20,28},{24,16},{28,12},{1,9},{5... | collective-permute-start | bytes 1572872 | tf_op jit(solution)/shard_map/ppermute | solution.py:403
  31.6 8.5 %collective-permute-start.13 = (bf16[256,1024]{1,0:T(8,128)(2,1)S(1)}, bf16[256,1024]{1,0:T(8,128)(2,1)S(1)}, u32[]{:S(2)}, u32[]{:S(2)}) collective-permute-start(bf16[256,1024]{1,0:T(8,128)(2,1)S(1)} %get-tuple-element.114.refs_4_), channel_id=1, source_target_pairs={{1,2},{2,1},{5,6},{6,5},{9,10},{10,9},{13,14},{14,13},{17,18},{18,... | collective-permute-start | bytes 1572872 | tf_op jit(solution)/shard_map/ppermute | solution.py:460
  32.3 36.8 %collective-permute-start.24 = (bf16[256,3328]{1,0:T(8,128)(2,1)S(1)}, bf16[256,3328]{1,0:T(8,128)(2,1)S(1)}, u32[]{:S(2)}, u32[]{:S(2)}) collective-permute-start(bf16[256,3328]{1,0:T(8,128)(2,1)S(1)} %get-tuple-element.131), channel_id=1, source_target_pairs={{0,4},{4,0},{8,12},{12,8},{16,20},{20,16},{24,28},{28,24},{1,5},{5... | collective-permute-start | bytes 5111816 | tf_op jit(solution)/shard_map/ppermute | solution.py:406
  33.7 9.8 %collective-permute-start.10 = (bf16[2,512,256]{2,1,0:T(8,128)(2,1)S(1)}, bf16[2,512,256]{2,1,0:T(8,128)(2,1)S(1)}, u32[]{:S(2)}, u32[]{:S(2)}) collective-permute-start(bf16[2,512,256]{2,1,0:T(8,128)(2,1)S(1)} %copy-done.12), channel_id=1, source_target_pairs={{0,4},{4,0},{8,12},{12,8},{16,20},{20,16},{24,28},{28,24},{1,5},{5... | collective-permute-start | bytes 1572872 | tf_op jit(solution)/shard_map/ppermute | solution.py:406
  35.3 9.6 %collective-permute-start.9 = (bf16[2,512,256]{2,1,0:T(8,128)(2,1)S(1)}, bf16[2,512,256]{2,1,0:T(8,128)(2,1)S(1)}, u32[]{:S(2)}, u32[]{:S(2)}) collective-permute-start(bf16[2,512,256]{2,1,0:T(8,128)(2,1)S(1)} %get-tuple-element.110.refs_4_.refs_11_.refs_6_), channel_id=1, source_target_pairs={{0,8},{4,20},{8,24},{12,4},{16,0},{20,28},{24,16},{28,12},{1,9},{5... | collective-permute-start | bytes 1572872 | tf_op jit(solution)/shard_map/ppermute | solution.py:403
  39.3 7.7 %collective-permute-start.18 = (bf16[2,512,256]{2,1,0:T(8,128)(2,1)S(1)}, bf16[2,512,256]{2,1,0:T(8,128)(2,1)S(1)}, u32[]{:S(2)}, u32[]{:S(2)}) collective-permute-start(bf16[2,512,256]{2,1,0:T(8,128)(2,1)S(1)} %copy-done.11), channel_id=1, source_target_pairs={{0,4},{4,0},{8,12},{12,8},{16,20},{20,16},{24,28},{28,24},{1,5},{5... | collective-permute-start | bytes 1572872 | tf_op jit(solution)/shard_map/ppermute | solution.py:406
  41.0 9.5 %collective-permute-start.17 = (bf16[2,512,256]{2,1,0:T(8,128)(2,1)S(1)}, bf16[2,512,256]{2,1,0:T(8,128)(2,1)S(1)}, u32[]{:S(2)}, u32[]{:S(2)}) collective-permute-start(bf16[2,512,256]{2,1,0:T(8,128)(2,1)S(1)} %get-tuple-element.120.refs_8_.refs_3_.refs_10_), channel_id=1, source_target_pairs={{0,8},{4,20},{8,24},{12,4},{16,0},{20,28},{24,16},{28,12},{1,9},{5... | collective-permute-start | bytes 1572872 | tf_op jit(solution)/shard_map/ppermute | solution.py:403
  43.5 8.7 %collective-permute-start.15 = (bf16[2,512,256]{2,1,0:T(8,128)(2,1)S(1)}, bf16[2,512,256]{2,1,0:T(8,128)(2,1)S(1)}, u32[]{:S(2)}, u32[]{:S(2)}) collective-permute-start(bf16[2,512,256]{2,1,0:T(8,128)(2,1)S(1)} %copy-done.10), channel_id=1, source_target_pairs={{0,4},{4,0},{8,12},{12,8},{16,20},{20,16},{24,28},{28,24},{1,5},{5... | collective-permute-start | bytes 1572872 | tf_op jit(solution)/shard_map/ppermute | solution.py:406
  44.9 20.3 %collective-permute-start.16 = (bf16[256,1024]{1,0:T(8,128)(2,1)S(1)}, bf16[256,1024]{1,0:T(8,128)(2,1)S(1)}, u32[]{:S(2)}, u32[]{:S(2)}) collective-permute-start(bf16[256,1024]{1,0:T(8,128)(2,1)S(1)} %get-tuple-element.119.refs_4_), channel_id=1, source_target_pairs={{1,0},{2,3},{5,4},{6,7},{9,8},{10,11},{13,12},{14,15},{17,16},{18,... | collective-permute-start | bytes 1572872 | tf_op jit(solution)/shard_map/ppermute | solution.py:460
  47.0 18.3 %collective-permute-start.14 = (bf16[2,512,256]{2,1,0:T(8,128)(2,1)S(1)}, bf16[2,512,256]{2,1,0:T(8,128)(2,1)S(1)}, u32[]{:S(2)}, u32[]{:S(2)}) collective-permute-start(bf16[2,512,256]{2,1,0:T(8,128)(2,1)S(1)} %get-tuple-element.117.refs_5_.refs_12_.refs_7_.refs_2_), channel_id=1, source_target_pairs={{0,8},{4,20},{8,24},{12,4},{16,0},{20,28},{24,16},{28,12},{1,9},{5... | collective-permute-start | bytes 1572872 | tf_op jit(solution)/shard_map/ppermute | solution.py:403
  50.5 16.2 %collective-permute-start.22 = (bf16[2,512,256]{2,1,0:T(8,128)(2,1)S(1)}, bf16[2,512,256]{2,1,0:T(8,128)(2,1)S(1)}, u32[]{:S(2)}, u32[]{:S(2)}) collective-permute-start(bf16[2,512,256]{2,1,0:T(8,128)(2,1)S(1)} %copy-done.9), channel_id=1, source_target_pairs={{0,4},{4,0},{8,12},{12,8},{16,20},{20,16},{24,28},{28,24},{1,5},{5... | collective-permute-start | bytes 1572872 | tf_op jit(solution)/shard_map/ppermute | solution.py:406
  52.1 16.2 %collective-permute-start.21 = (bf16[2,512,256]{2,1,0:T(8,128)(2,1)S(1)}, bf16[2,512,256]{2,1,0:T(8,128)(2,1)S(1)}, u32[]{:S(2)}, u32[]{:S(2)}) collective-permute-start(bf16[2,512,256]{2,1,0:T(8,128)(2,1)S(1)} %get-tuple-element.126.refs_9_.refs_4_.refs_11_.refs_6_), channel_id=1, source_target_pairs={{0,8},{4,20},{8,24},{12,4},{16,0},{20,28},{24,16},{28,12},{1,9},{5... | collective-permute-start | bytes 1572872 | tf_op jit(solution)/shard_map/ppermute | solution.py:403
  66.1 4.3 %collective-permute-start.23 = (bf16[256,1024]{1,0:T(8,128)(2,1)S(1)}, bf16[256,1024]{1,0:T(8,128)(2,1)S(1)}, u32[]{:S(2)}, u32[]{:S(2)}) collective-permute-start(bf16[256,1024]{1,0:T(8,128)(2,1)S(1)} %get-tuple-element.130.refs_15_.refs_16_.refs_12_.refs_8_), channel_id=1, source_target_pairs={{0,4},{4,0},{8,12},{12,8},{16,20},{20,16},{24,28},{28,24},{1,5},{5... | collective-permute-start | bytes 1572872 | tf_op jit(solution)/shard_map/ppermute | solution.py:406
  66.3 9.0 %collective-permute-start.20 = (bf16[2,512,256]{2,1,0:T(8,128)(2,1)S(1)}, bf16[2,512,256]{2,1,0:T(8,128)(2,1)S(1)}, u32[]{:S(2)}, u32[]{:S(2)}) collective-permute-start(bf16[2,512,256]{2,1,0:T(8,128)(2,1)S(1)} %copy-done.8), channel_id=1, source_target_pairs={{0,4},{4,0},{8,12},{12,8},{16,20},{20,16},{24,28},{28,24},{1,5},{5... | collective-permute-start | bytes 1572872 | tf_op jit(solution)/shard_map/ppermute | solution.py:406
  66.7 9.2 %collective-permute-start.19 = (bf16[2,512,256]{2,1,0:T(8,128)(2,1)S(1)}, bf16[2,512,256]{2,1,0:T(8,128)(2,1)S(1)}, u32[]{:S(2)}, u32[]{:S(2)}) collective-permute-start(bf16[2,512,256]{2,1,0:T(8,128)(2,1)S(1)} %get-tuple-element.124.refs_13_.refs_8_.refs_3_.refs_2_), channel_id=1, source_target_pairs={{0,8},{4,20},{8,24},{12,4},{16,0},{20,28},{24,16},{28,12},{1,9},{5... | collective-permute-start | bytes 1572872 | tf_op jit(solution)/shard_map/ppermute | solution.py:403
  68.4 10.6 %collective-permute-start.28 = (bf16[2,512,256]{2,1,0:T(8,128)(2,1)S(1)}, bf16[2,512,256]{2,1,0:T(8,128)(2,1)S(1)}, u32[]{:S(2)}, u32[]{:S(2)}) collective-permute-start(bf16[2,512,256]{2,1,0:T(8,128)(2,1)S(1)} %copy-done.7), channel_id=1, source_target_pairs={{0,4},{4,0},{8,12},{12,8},{16,20},{20,16},{24,28},{28,24},{1,5},{5... | collective-permute-start | bytes 1572872 | tf_op jit(solution)/shard_map/ppermute | solution.py:406
  69.2 12.3 %collective-permute-start.27 = (bf16[2,512,256]{2,1,0:T(8,128)(2,1)S(1)}, bf16[2,512,256]{2,1,0:T(8,128)(2,1)S(1)}, u32[]{:S(2)}, u32[]{:S(2)}) collective-permute-start(bf16[2,512,256]{2,1,0:T(8,128)(2,1)S(1)} %get-tuple-element.135.refs_5_.refs_12_.refs_7_.refs_6_), channel_id=1, source_target_pairs={{0,8},{4,20},{8,24},{12,4},{16,0},{20,28},{24,16},{28,12},{1,9},{5... | collective-permute-start | bytes 1572872 | tf_op jit(solution)/shard_map/ppermute | solution.py:403
  70.4 19.5 %collective-permute-start.26 = (bf16[2,512,256]{2,1,0:T(8,128)(2,1)S(1)}, bf16[2,512,256]{2,1,0:T(8,128)(2,1)S(1)}, u32[]{:S(2)}, u32[]{:S(2)}) collective-permute-start(bf16[2,512,256]{2,1,0:T(8,128)(2,1)S(1)} %copy-done.6), channel_id=1, source_target_pairs={{0,4},{4,0},{8,12},{12,8},{16,20},{20,16},{24,28},{28,24},{1,5},{5... | collective-permute-start | bytes 1572872 | tf_op jit(solution)/shard_map/ppermute | solution.py:406
  76.6 13.3 %collective-permute-start.25 = (bf16[2,512,256]{2,1,0:T(8,128)(2,1)S(1)}, bf16[2,512,256]{2,1,0:T(8,128)(2,1)S(1)}, u32[]{:S(2)}, u32[]{:S(2)}) collective-permute-start(bf16[2,512,256]{2,1,0:T(8,128)(2,1)S(1)} %get-tuple-element.133.refs_9_.refs_4_.refs_3_.refs_2_), channel_id=1, source_target_pairs={{0,8},{4,20},{8,24},{12,4},{16,0},{20,28},{24,16},{28,12},{1,9},{5... | collective-permute-start | bytes 1572872 | tf_op jit(solution)/shard_map/ppermute | solution.py:403
  79.0 5.6 %collective-permute-start.29 = (bf16[256,256]{1,0:T(8,128)(2,1)S(1)}, bf16[256,256]{1,0:T(8,128)(2,1)S(1)}, u32[]{:S(2)}, u32[]{:S(2)}) collective-permute-start(bf16[256,256]{1,0:T(8,128)(2,1)S(1)} %get-tuple-element.143), channel_id=1, source_target_pairs={{0,4},{4,0},{8,12},{12,8},{16,20},{20,16},{24,28},{28,24},{1,5},{5... | collective-permute-start | bytes 393224 | tf_op jit(solution)/shard_map/ppermute | solution.py:406
  82.2 10.9 %collective-permute-start.31 = (bf16[2,512,256]{2,1,0:T(8,128)(2,1)S(1)}, bf16[2,512,256]{2,1,0:T(8,128)(2,1)S(1)}, u32[]{:S(2)}, u32[]{:S(2)}) collective-permute-start(bf16[2,512,256]{2,1,0:T(8,128)(2,1)S(1)} %get-tuple-element.138.refs_13_.refs_8_.refs_7_.refs_6_), channel_id=1, source_target_pairs={{0,8},{4,20},{8,24},{12,4},{16,0},{20,28},{24,16},{28,12},{1,9},{5... | collective-permute-start | bytes 1572872 | tf_op jit(solution)/shard_map/ppermute | solution.py:403
  90.7 9.4 %collective-permute-start.30 = (bf16[2,512,256]{2,1,0:T(8,128)(2,1)S(1)}, bf16[2,512,256]{2,1,0:T(8,128)(2,1)S(1)}, u32[]{:S(2)}, u32[]{:S(2)}) collective-permute-start(bf16[2,512,256]{2,1,0:T(8,128)(2,1)S(1)} %get-tuple-element.145.refs_5_.refs_4_.refs_3_.refs_2_), channel_id=1, source_target_pairs={{0,8},{4,20},{8,24},{12,4},{16,0},{20,28},{24,16},{28,12},{1,9},{5... | collective-permute-start | bytes 1572872 | tf_op jit(solution)/shard_map/ppermute | solution.py:403
  93.8 11.9 %collective-permute-start.36 = (bf16[2,512,256]{2,1,0:T(8,128)(2,1)S(1)}, bf16[2,512,256]{2,1,0:T(8,128)(2,1)S(1)}, u32[]{:S(2)}, u32[]{:S(2)}) collective-permute-start(bf16[2,512,256]{2,1,0:T(8,128)(2,1)S(1)} %get-tuple-element.147.refs_9_.refs_8_.refs_7_), channel_id=1, source_target_pairs={{0,8},{4,20},{8,24},{12,4},{16,0},{20,28},{24,16},{28,12},{1,9},{5... | collective-permute-start | bytes 1572872 | tf_op jit(solution)/shard_map/ppermute | solution.py:403
  100.7 10.8 %collective-permute-start.35 = (bf16[2,512,256]{2,1,0:T(8,128)(2,1)S(1)}, bf16[2,512,256]{2,1,0:T(8,128)(2,1)S(1)}, u32[]{:S(2)}, u32[]{:S(2)}) collective-permute-start(bf16[2,512,256]{2,1,0:T(8,128)(2,1)S(1)} %get-tuple-element.156.refs_5_.refs_4_.refs_3_), channel_id=1, source_target_pairs={{0,8},{4,20},{8,24},{12,4},{16,0},{20,28},{24,16},{28,12},{1,9},{5... | collective-permute-start | bytes 1572872 | tf_op jit(solution)/shard_map/ppermute | solution.py:403
  102.5 5.6 %collective-permute-start.37 = (bf16[256,256]{1,0:T(8,128)(2,1)S(1)}, bf16[256,256]{1,0:T(8,128)(2,1)S(1)}, u32[]{:S(2)}, u32[]{:S(2)}) collective-permute-start(bf16[256,256]{1,0:T(8,128)(2,1)S(1)} %get-tuple-element.163), channel_id=1, source_target_pairs={{0,4},{4,0},{8,12},{12,8},{16,20},{20,16},{24,28},{28,24},{1,5},{5... | collective-permute-start | bytes 393224 | tf_op jit(solution)/shard_map/ppermute | solution.py:406
  102.5 5.6 %collective-permute-start.38 = (bf16[256,256]{1,0:T(8,128)(2,1)S(1)}, bf16[256,256]{1,0:T(8,128)(2,1)S(1)}, u32[]{:S(2)}, u32[]{:S(2)}) collective-permute-start(bf16[256,256]{1,0:T(8,128)(2,1)S(1)} %get-tuple-element.164), channel_id=1, source_target_pairs={{0,4},{4,0},{8,12},{12,8},{16,20},{20,16},{24,28},{28,24},{1,5},{5... | collective-permute-start | bytes 393224 | tf_op jit(solution)/shard_map/ppermute | solution.py:406
  106.4 10.6 %collective-permute-start.39 = (bf16[2,512,256]{2,1,0:T(8,128)(2,1)S(1)}, bf16[2,512,256]{2,1,0:T(8,128)(2,1)S(1)}, u32[]{:S(2)}, u32[]{:S(2)}) collective-permute-start(bf16[2,512,256]{2,1,0:T(8,128)(2,1)S(1)} %get-tuple-element.158.refs_9_.refs_8_), channel_id=1, source_target_pairs={{0,8},{4,20},{8,24},{12,4},{16,0},{20,28},{24,16},{28,12},{1,9},{5... | collective-permute-start | bytes 1572872 | tf_op jit(solution)/shard_map/ppermute | solution.py:403
  112.2 10.3 %collective-permute-start.44 = (bf16[2,512,256]{2,1,0:T(8,128)(2,1)S(1)}, bf16[2,512,256]{2,1,0:T(8,128)(2,1)S(1)}, u32[]{:S(2)}, u32[]{:S(2)}) collective-permute-start(bf16[2,512,256]{2,1,0:T(8,128)(2,1)S(1)} %get-tuple-element.166.refs_5_.refs_4_), channel_id=1, source_target_pairs={{0,8},{4,20},{8,24},{12,4},{16,0},{20,28},{24,16},{28,12},{1,9},{5... | collective-permute-start | bytes 1572872 | tf_op jit(solution)/shard_map/ppermute | solution.py:403
  114.3 6.1 %collective-permute-start.45 = (bf16[256,256]{1,0:T(8,128)(2,1)S(1)}, bf16[256,256]{1,0:T(8,128)(2,1)S(1)}, u32[]{:S(2)}, u32[]{:S(2)}) collective-permute-start(bf16[256,256]{1,0:T(8,128)(2,1)S(1)} %get-tuple-element.179), channel_id=1, source_target_pairs={{0,4},{4,0},{8,12},{12,8},{16,20},{20,16},{24,28},{28,24},{1,5},{5... | collective-permute-start | bytes 393224 | tf_op jit(solution)/shard_map/ppermute | solution.py:406
  115.1 5.3 %collective-permute-start.46 = (bf16[256,256]{1,0:T(8,128)(2,1)S(1)}, bf16[256,256]{1,0:T(8,128)(2,1)S(1)}, u32[]{:S(2)}, u32[]{:S(2)}) collective-permute-start(bf16[256,256]{1,0:T(8,128)(2,1)S(1)} %get-tuple-element.180), channel_id=1, source_target_pairs={{0,4},{4,0},{8,12},{12,8},{16,20},{20,16},{24,28},{28,24},{1,5},{5... | collective-permute-start | bytes 393224 | tf_op jit(solution)/shard_map/ppermute | solution.py:406
  127.4 6.8 %collective-permute-start.49 = (f32[64,256]{1,0:T(8,128)S(1)}, f32[64,256]{1,0:T(8,128)S(1)}, u32[]{:S(2)}, u32[]{:S(2)}) collective-permute-start(f32[64,256]{1,0:T(8,128)S(1)} %get-tuple-element.189), channel_id=1, source_target_pairs={{0,1},{1,2},{2,3},{3,0},{4,5},{5,6},{6,7},{7,4},{8,9},{9,10},{10,1... | collective-permute-start | bytes 196616 | tf_op jit(solution)/shard_map/ppermute | solution.py:621
  127.5 8.6 %collective-permute-start.50 = (f32[64,256]{1,0:T(8,128)S(1)}, f32[64,256]{1,0:T(8,128)S(1)}, u32[]{:S(2)}, u32[]{:S(2)}) collective-permute-start(f32[64,256]{1,0:T(8,128)S(1)} %get-tuple-element.191), channel_id=1, source_target_pairs={{0,2},{1,3},{2,0},{3,1},{4,6},{5,7},{6,4},{7,5},{8,10},{9,11},{10,... | collective-permute-start | bytes 196616 | tf_op jit(solution)/shard_map/ppermute | solution.py:621
  130.5 5.6 %collective-permute-start.51 = (f32[64,256]{1,0:T(8,128)S(1)}, f32[64,256]{1,0:T(8,128)S(1)}, u32[]{:S(2)}, u32[]{:S(2)}) collective-permute-start(f32[64,256]{1,0:T(8,128)S(1)} %get-tuple-element.190), channel_id=1, source_target_pairs={{0,3},{1,0},{2,1},{3,2},{4,7},{5,4},{6,5},{7,6},{8,11},{9,8},{10,9... | collective-permute-start | bytes 196616 | tf_op jit(solution)/shard_map/ppermute | solution.py:621
  131.4 6.2 %collective-permute-start.42 = (bf16[256,256]{1,0:T(8,128)(2,1)S(1)}, bf16[256,256]{1,0:T(8,128)(2,1)S(1)}, u32[]{:S(2)}, u32[]{:S(2)}) collective-permute-start(bf16[256,256]{1,0:T(8,128)(2,1)S(1)} %get-tuple-element.173), channel_id=1, source_target_pairs={{0,4},{4,0},{8,12},{12,8},{16,20},{20,16},{24,28},{28,24},{1,5},{5... | collective-permute-start | bytes 393224 | tf_op jit(solution)/shard_map/ppermute | solution.py:406
  131.4 6.2 %collective-permute-start.43 = (bf16[256,256]{1,0:T(8,128)(2,1)S(1)}, bf16[256,256]{1,0:T(8,128)(2,1)S(1)}, u32[]{:S(2)}, u32[]{:S(2)}) collective-permute-start(bf16[256,256]{1,0:T(8,128)(2,1)S(1)} %get-tuple-element.174), channel_id=1, source_target_pairs={{0,4},{4,0},{8,12},{12,8},{16,20},{20,16},{24,28},{28,24},{1,5},{5... | collective-permute-start | bytes 393224 | tf_op jit(solution)/shard_map/ppermute | solution.py:406
  136.2 7.0 %collective-permute-start.52 = (f32[64,256]{1,0:T(8,128)S(1)}, f32[64,256]{1,0:T(8,128)S(1)}, u32[]{:S(2)}, u32[]{:S(2)}) collective-permute-start(f32[64,256]{1,0:T(8,128)S(1)} %get-tuple-element.186), channel_id=1, source_target_pairs={{0,1},{1,2},{2,3},{3,0},{4,5},{5,6},{6,7},{7,4},{8,9},{9,10},{10,1... | collective-permute-start | bytes 196616 | tf_op jit(solution)/shard_map/ppermute | solution.py:626
  139.0 6.4 %collective-permute-start.53 = (f32[64,256]{1,0:T(8,128)S(1)}, f32[64,256]{1,0:T(8,128)S(1)}, u32[]{:S(2)}, u32[]{:S(2)}) collective-permute-start(f32[64,256]{1,0:T(8,128)S(1)} %get-tuple-element.186), channel_id=1, source_target_pairs={{0,2},{1,3},{2,0},{3,1},{4,6},{5,7},{6,4},{7,5},{8,10},{9,11},{10,... | collective-permute-start | bytes 196616 | tf_op jit(solution)/shard_map/ppermute | solution.py:626
  141.0 4.8 %collective-permute-start.54 = (f32[64,256]{1,0:T(8,128)S(1)}, f32[64,256]{1,0:T(8,128)S(1)}, u32[]{:S(2)}, u32[]{:S(2)}) collective-permute-start(f32[64,256]{1,0:T(8,128)S(1)} %get-tuple-element.186), channel_id=1, source_target_pairs={{0,3},{1,0},{2,1},{3,2},{4,7},{5,4},{6,5},{7,6},{8,11},{9,8},{10,9... | collective-permute-start | bytes 196616 | tf_op jit(solution)/shard_map/ppermute | solution.py:626
  (23 other events, 84.9 us)

commit v3 on v2

--- a/solution.py
+++ b/solution.py
@@ -12,9 +12,9 @@
 CORES = 2
 LANES = 128
 WIDTHS = (256, 256)
-C_MOST = 3
+C_MOST = 4
 HOPS = (1, 0), (2, 1), (4, 0)
-PARTS = 2
+PARTS = 1
 
 ANY = pl.BlockSpec(memory_space=pl.ANY)
 SMEM = pl.BlockSpec(memory_space=pltpu.SMEM)
@@ -73,7 +73,7 @@
     return b_ref.at[rows, pl.ds(aligned(core * half + start, LANES), width)]
 
 
-def prologue_kernel(n_row, half, chunks, ids, b_ref, a_ref, scal, cand, tok_out, *rest):
+def prologue_kernel(n_row, half, chunks, ids, b_ref, a_ref, scal, cand, *rest):
     n = len(chunks)
     outs, (a_buf, bufs, a_sem, load_sem, store_sem) = rest[:n], rest[n:]
     n_chips = n_row // CORES
@@ -167,7 +167,7 @@
                 store().wait()
 
 
-def inject_kernel(n_col, half, chunk, first, hop, scal, *refs):
+def inject_kernel(n_col, half, chunk, first, alone, hop, scal, *refs):
     refs = list(refs)
     take = lambda n: [refs.pop(0) for _ in range(n)]
     if not first:
@@ -176,7 +176,9 @@
         b_ref, sib = take(2)
     if hop is not None:
         came, held_in = take(2)
-    tok_in, out, tok_out = take(3)
+    if not first or not alone:
+        take(1)
+    out, tok_out = take(2)
     if hop is not None:
         (held,) = take(1)
     buf, load_sem, store_sem, a_buf, a_sem = refs
@@ -421,16 +423,15 @@
     )
     flat = [chains[c][j] for j, c in order_of]
     widest = max(WIDTHS)
-    scal, cand, tok, *others = call(
+    scal, cand, *others = call(
         functools.partial(prologue_kernel, n_row, half, flat),
         out_shape=(
             like((CORE + 1,), jnp.int32),
             like((rows, STEPS * PANEL)),
-            like((8, LANES)),
         )
         + tuple(like((STEPS, PANEL, width)) for _, width in flat),
         in_specs=[SMEM, ANY, ANY],
-        out_specs=(SMEM,) + (ANY,) * (2 + len(flat)),
+        out_specs=(SMEM,) + (ANY,) * (1 + len(flat)),
         scratch_shapes=[
             pltpu.VMEM((rows, STEPS * PANEL), jnp.bfloat16),
             pltpu.VMEM((len(flat), STEPS, PANEL, widest), jnp.bfloat16),
@@ -454,14 +455,15 @@
         aliases = {} if first else {1: 0}
         if chunk is not None:
             args += [b_tile, sibs[c, t]]
-        outs = [like((STEPS, PANEL, WIDTHS[c])), like(tok.shape, tok.dtype)]
+        outs = [like((STEPS, PANEL, WIDTHS[c])), like((8, LANES))]
         if hop is not None:
             aliases[len(args) + 1] = 2
             args += [lax.ppermute(cand, "col", hops[hop]), cand]
             outs.append(like(cand.shape))
-        args.append(tok)
+        if tok is not None:
+            args.append(tok)
         return call(
-            functools.partial(inject_kernel, n_col, half, chunk, first, hop),
+            functools.partial(inject_kernel, n_col, half, chunk, first, tok is None, hop),
             out_shape=tuple(outs),
             in_specs=[SMEM] + [ANY] * (len(args) - 1),
             out_specs=(ANY,) * len(outs),
@@ -477,6 +479,7 @@
         )(*args)
 
     sends = [[] for _ in chains]
+    tok = None
     flying = [None] * n_chains
     for c in range(n_chains):
         sent, tok = inject(tok, c, 0, None)

time: 147 us -> 145 us (0.986)
  starting transfers between devices: 61.3 us -> 29.8 us
  waiting for transfers between devices: 39.9 us -> 56.1 us
  Pallas kernels: 41.8 us -> 55.3 us
    ppermute x17, starting transfers between devices: 40.3 us -> 4.13 us  [spread(): return lax.ppermute(x, 'row', around)]
    ppermute x17, waiting for transfers between devices: 16.4 us -> 32.9 us  [spread(): return lax.ppermute(x, 'row', around)]
    pallas_call x17, Pallas kernels: 12.3 us -> 24.2 us  [inject(): call(functools.partial(inject_kernel, n_col, half, chunk, first, tok is N...]
    ppermute x3, starting transfers between devices: 4 us -> 7.59 us  [ring_form(): part = part + lax.ppermute(cut(z + k), 'col', shift(k))]
    ppermute x3, waiting for transfers between devices: 4.18 us -> 2.41 us  [ring_form(): part = part + lax.ppermute(cut(z + k), 'col', shift(k))]
    pallas_call x1, Pallas kernels: 3.54 us -> 5.29 us  [ring_form(): call(functools.partial(prologue_kernel, n_row, half, flat), out_shape=(li...]
    ppermute x3, waiting for transfers between devices: 12.7 us -> 14.2 us  [inject(): args += [lax.ppermute(cand, 'col', hops[hop]), cand]]
  transfers between devices with their start and end apart: 55 -> 55, of which waited for: 20 -> 21; matrix products, arithmetic and copies ran while one was open for 0% -> 0% of each run, Pallas kernels for 24% -> 32%
where the time goes in v3:
time: 145 us; the launch traced here: 144 us
  waiting for transfers between devices  56.1 us (39%)
  Pallas kernels  55.3 us (38%)
  starting transfers between devices  29.8 us (21%)
  local copies, waits for them, and re-layouts  1.49 us (1%)
    ppermute x17, waiting for transfers between devices, spread(): return lax.ppermute(x, 'row', around)  32.9 us
    pallas_call x17, Pallas kernels, inject(): call(functools.partial(inject_kernel, n_col, half, chunk, first, tok is N...  24.2 us
    pallas_call x6, Pallas kernels, work(): call(functools.partial(work_kernel, plan, n_chips, half), out_shape=tuple...  23.5 us
    ppermute x3, waiting for transfers between devices, inject(): args += [lax.ppermute(cand, 'col', hops[hop]), cand]  14.2 us
    ppermute x3, starting transfers between devices, ring_form(): part = part + lax.ppermute(cut(z + k), 'col', shift(k))  7.59 us
    ppermute x29, starting transfers between devices, exchange(): return lax.ppermute(x, 'row', swap)  6.98 us
    ppermute x3, starting transfers between devices, inject(): args += [lax.ppermute(cand, 'col', hops[hop]), cand]  6.9 us
    pallas_call x1, Pallas kernels, ring_form(): call(functools.partial(prologue_kernel, n_row, half, flat), out_shape=(li...  5.29 us
  transfers between devices with their start and end apart: 55, of which 21 were waited for; matrix products, arithmetic and copies ran while one was open for 0% of the time, Pallas kernels for 32%

profile of v3, /device:TPU:0, one launch (start us, length us, event | category | flops | bytes accessed | tf_op | source)
XLA Modules:
  0.0 144.1 jit_solution(15440876846300841367)
XLA Ops:
  0.6 5.3 %shard_map.76 = (s32[11]{0:T(128)}, bf16[256,1024]{1,0:T(8,128)(2,1)}, bf16[2,512,256]{2,1,0:T(8,128)(2,1)}, bf16[2,512,256]{2,1,0:T(8,128)(2,1)}, bf16[2,512,25...) custom-call(s32[2]{0:T(128)} %ids.1, ...), custom_call_target="tpu_custom_call" | custom-call | flops 1 | bytes 1 | tf_op jit(solution)/shard_map/pallas_call | solution.py:426
  6.5 4.9 %collective-permute-start.3 = (bf16[256,1024]{1,0:T(8,128)(2,1)}, bf16[256,1024]{1,0:T(8,128)(2,1)S(1)}, u32[]{:S(2)}, u32[]{:S(2)}) collective-permute-start(bf16[256,1024]{1,0:T(8,128)(2,1)} %get-tuple-element.97.refs_4_), channel_id=1, source_target_pairs={{0,1},{3,2},{4,5},{7,6},{8,9},{11,10},{12,13},{15,14},{16,17},{19,... | collective-permute-start | bytes 1572872 | tf_op jit(solution)/shard_map/ppermute | solution.py:461
  12.2 1.6 %shard_map.77 = (bf16[2,512,256]{2,1,0:T(8,128)(2,1)S(1)}, bf16[8,128]{1,0:T(8,128)(2,1)S(1)}) custom-call(s32[11]{0:T(128)S(1)} %copy-done.3, bf16[2048,6656]{1,0:T(8,128)(2,1)} %refs_1_.29, bf16[2,512,256]{2,1,0:T(8,128)(2,1)S(1)} %collective-permute-done.refs_1_), custom_call_target="tpu_custom_call" | custom-call | flops 1 | bytes 1 | tf_op jit(solution)/shard_map/pallas_call | solution.py:465
  14.5 1.9 %shard_map.78 = (bf16[2,512,256]{2,1,0:T(8,128)(2,1)S(1)}, bf16[8,128]{1,0:T(8,128)(2,1)S(1)}) custom-call(s32[11]{0:T(128)S(1)} %copy-done.4, bf16[2048,6656]{1,0:T(8,128)(2,1)} %refs_1_.29, bf16[2,512,256]{2,1,0:T(8,128)(2,1)S(1)} %collective-permute-done.4.refs_1_, bf16[8,128]{1,0:T(8,128)(2,1)S(1)} %get-tuple-element.99.refs_2_), custom_call_target="tpu_custom_call" | custom-call | flops 1 | bytes 1 | tf_op jit(solution)/shard_map/pallas_call | solution.py:465
  16.9 1.0 shard_map.79
  17.9 5.3 %collective-permute-done.3.refs_3_ = bf16[256,1024]{1,0:T(8,128)(2,1)S(1)} collective-permute-done((bf16[256,1024]{1,0:T(8,128)(2,1)}, bf16[256,1024]{1,0:T(8,128)(2,1)S(1)}, u32[]{:S(2)}, u32[]{:S(2)}) %collective-permute-start.3) | collective-permute-done | bytes 524320 | tf_op jit(solution)/shard_map/ppermute | solution.py:461
  23.2 1.7 %shard_map.80 = (bf16[2,512,256]{2,1,0:T(8,128)(2,1)S(1)}, bf16[8,128]{1,0:T(8,128)(2,1)S(1)}, bf16[256,1024]{1,0:T(8,128)(2,1)S(1)}) custom-call(s32[11]{0:T(128)S(1)} %copy-done.4, bf16[2,512,256]{2,1,0:T(8,128)(2,1)S(1)} %collective-permute-done.1.refs_0_, bf16[2048,6656]{1,0:T(8,128)(2,1)} %refs_1_.29, ...), custom_call_target="tpu_custom_call", output_to_operand_aliasing={{0}: (1, {}), {2}: (5, {})} | custom-call | flops 1 | bytes 1 | tf_op jit(solution)/shard_map/pallas_call | solution.py:465
  25.5 3.2 %collective-permute-done.7.refs_0_ = bf16[2,512,256]{2,1,0:T(8,128)(2,1)S(1)} collective-permute-done((bf16[2,512,256]{2,1,0:T(8,128)(2,1)S(1)}, bf16[2,512,256]{2,1,0:T(8,128)(2,1)S(1)}, u32[]{:S(2)}, u32[]{:S(2)}) %collective-permute-start.7) | collective-permute-done | bytes 524320 | tf_op jit(solution)/shard_map/ppermute | solution.py:405
  28.7 1.6 %shard_map.81 = (bf16[2,512,256]{2,1,0:T(8,128)(2,1)S(1)}, bf16[8,128]{1,0:T(8,128)(2,1)S(1)}) custom-call(s32[11]{0:T(128)S(1)} %copy-done.4, bf16[2,512,256]{2,1,0:T(8,128)(2,1)S(1)} %collective-permute-done.7.refs_0_, bf16[2048,6656]{1,0:T(8,128)(2,1)} %refs_1_.29, ...), custom_call_target="tpu_custom_call", output_to_operand_aliasing={{0}: (1, {})} | custom-call | flops 1 | bytes 1 | tf_op jit(solution)/shard_map/pallas_call | solution.py:465
  31.2 3.1 %collective-permute-done.5.refs_0_ = bf16[2,512,256]{2,1,0:T(8,128)(2,1)S(1)} collective-permute-done((bf16[2,512,256]{2,1,0:T(8,128)(2,1)S(1)}, bf16[2,512,256]{2,1,0:T(8,128)(2,1)S(1)}, u32[]{:S(2)}, u32[]{:S(2)}) %collective-permute-start.5) | collective-permute-done | bytes 524320 | tf_op jit(solution)/shard_map/ppermute | solution.py:405
  34.3 1.6 %shard_map.82 = (bf16[2,512,256]{2,1,0:T(8,128)(2,1)S(1)}, bf16[8,128]{1,0:T(8,128)(2,1)S(1)}) custom-call(s32[11]{0:T(128)S(1)} %copy-done.4, bf16[2,512,256]{2,1,0:T(8,128)(2,1)S(1)} %collective-permute-done.5.refs_0_, bf16[2048,6656]{1,0:T(8,128)(2,1)} %refs_1_.29, ...), custom_call_target="tpu_custom_call", output_to_operand_aliasing={{0}: (1, {})} | custom-call | flops 1 | bytes 1 | tf_op jit(solution)/shard_map/pallas_call | solution.py:465
  36.1 3.9 %collective-permute-done.11.refs_0_ = bf16[2,512,256]{2,1,0:T(8,128)(2,1)S(1)} collective-permute-done((bf16[2,512,256]{2,1,0:T(8,128)(2,1)S(1)}, bf16[2,512,256]{2,1,0:T(8,128)(2,1)S(1)}, u32[]{:S(2)}, u32[]{:S(2)}) %collective-permute-start.11) | collective-permute-done | bytes 524320 | tf_op jit(solution)/shard_map/ppermute | solution.py:405
  40.0 1.7 %shard_map.83 = (bf16[2,512,256]{2,1,0:T(8,128)(2,1)S(1)}, bf16[8,128]{1,0:T(8,128)(2,1)S(1)}, bf16[256,1024]{1,0:T(8,128)(2,1)S(1)}) custom-call(s32[11]{0:T(128)S(1)} %copy-done.4, bf16[2,512,256]{2,1,0:T(8,128)(2,1)S(1)} %collective-permute-done.11.refs_0_, bf16[2048,6656]{1,0:T(8,128)(2,1)} %refs_1_.29, ...), custom_call_target="tpu_custom_call", output_to_operand_aliasing={{0}: (1, {}), {2}: (5, {})} | custom-call | flops 1 | bytes 1 | tf_op jit(solution)/shard_map/pallas_call | solution.py:465
  42.3 3.2 %collective-permute-done.9.refs_0_ = bf16[2,512,256]{2,1,0:T(8,128)(2,1)S(1)} collective-permute-done((bf16[2,512,256]{2,1,0:T(8,128)(2,1)S(1)}, bf16[2,512,256]{2,1,0:T(8,128)(2,1)S(1)}, u32[]{:S(2)}, u32[]{:S(2)}) %collective-permute-start.9) | collective-permute-done | bytes 524320 | tf_op jit(solution)/shard_map/ppermute | solution.py:405
  45.6 1.3 collective-permute-start.16
  46.9 1.6 %shard_map.84 = (bf16[2,512,256]{2,1,0:T(8,128)(2,1)S(1)}, bf16[8,128]{1,0:T(8,128)(2,1)S(1)}) custom-call(s32[11]{0:T(128)S(1)} %copy-done.4, bf16[2,512,256]{2,1,0:T(8,128)(2,1)S(1)} %collective-permute-done.9.refs_0_, bf16[2048,6656]{1,0:T(8,128)(2,1)} %refs_1_.29, ...), custom_call_target="tpu_custom_call", output_to_operand_aliasing={{0}: (1, {})} | custom-call | flops 1 | bytes 1 | tf_op jit(solution)/shard_map/pallas_call | solution.py:465
  48.6 2.6 %collective-permute-done.17.refs_0_ = bf16[2,512,256]{2,1,0:T(8,128)(2,1)S(1)} collective-permute-done((bf16[2,512,256]{2,1,0:T(8,128)(2,1)S(1)}, bf16[2,512,256]{2,1,0:T(8,128)(2,1)S(1)}, u32[]{:S(2)}, u32[]{:S(2)}) %collective-permute-start.17) | collective-permute-done | bytes 524320 | tf_op jit(solution)/shard_map/ppermute | solution.py:405
  51.2 1.6 %shard_map.85 = (bf16[2,512,256]{2,1,0:T(8,128)(2,1)S(1)}, bf16[8,128]{1,0:T(8,128)(2,1)S(1)}) custom-call(s32[11]{0:T(128)S(1)} %copy-done.4, bf16[2,512,256]{2,1,0:T(8,128)(2,1)S(1)} %collective-permute-done.17.refs_0_, bf16[2048,6656]{1,0:T(8,128)(2,1)} %refs_1_.29, ...), custom_call_target="tpu_custom_call", output_to_operand_aliasing={{0}: (1, {})} | custom-call | flops 1 | bytes 1 | tf_op jit(solution)/shard_map/pallas_call | solution.py:465
  52.9 8.9 %collective-permute-done.16.refs_3_ = bf16[256,1024]{1,0:T(8,128)(2,1)S(1)} collective-permute-done((bf16[256,1024]{1,0:T(8,128)(2,1)S(1)}, bf16[256,1024]{1,0:T(8,128)(2,1)S(1)}, u32[]{:S(2)}, u32[]{:S(2)}) %collective-permute-start.16) | collective-permute-done | bytes 524320 | tf_op jit(solution)/shard_map/ppermute | solution.py:461
  61.8 1.7 %shard_map.86 = (bf16[2,512,256]{2,1,0:T(8,128)(2,1)S(1)}, bf16[8,128]{1,0:T(8,128)(2,1)S(1)}, bf16[256,1024]{1,0:T(8,128)(2,1)S(1)}) custom-call(s32[11]{0:T(128)S(1)} %copy-done.4, bf16[2,512,256]{2,1,0:T(8,128)(2,1)S(1)} %collective-permute-done.14.refs_0_, bf16[2048,6656]{1,0:T(8,128)(2,1)} %refs_1_.29, ...), custom_call_target="tpu_custom_call", output_to_operand_aliasing={{0}: (1, {}), {2}: (5, {})} | custom-call | flops 1 | bytes 1 | tf_op jit(solution)/shard_map/pallas_call | solution.py:465
  64.1 0.9 collective-permute-start.28
  65.0 1.8 %shard_map.87 = (bf16[2,512,256]{2,1,0:T(8,128)(2,1)S(1)}, bf16[8,128]{1,0:T(8,128)(2,1)S(1)}) custom-call(s32[11]{0:T(128)S(1)} %copy-done.4, bf16[2,512,256]{2,1,0:T(8,128)(2,1)S(1)} %collective-permute-done.21.refs_0_, bf16[2048,6656]{1,0:T(8,128)(2,1)} %refs_1_.29, ...), custom_call_target="tpu_custom_call", output_to_operand_aliasing={{0}: (1, {})} | custom-call | flops 1 | bytes 1 | tf_op jit(solution)/shard_map/pallas_call | solution.py:465
  67.1 6.5 %shard_map.88 = (bf16[8,128]{1,0:T(8,128)(2,1)S(1)}, f32[1024,128]{1,0:T(8,128)S(1)}, f32[512,128]{1,0:T(8,128)S(1)}, bf16[256,6656]{1,0:T(8,128)(2,1)}, bf16[25...) custom-call(s32[11]{0:T(128)S(1)} %copy-done.4, ...), custom_call_target="tpu_custom_call" | custom-call | flops 1 | bytes 1 | tf_op jit(solution)/shard_map/pallas_call | solution.py:550
  73.6 1.6 %shard_map.89 = (bf16[2,512,256]{2,1,0:T(8,128)(2,1)S(1)}, bf16[8,128]{1,0:T(8,128)(2,1)S(1)}) custom-call(s32[11]{0:T(128)S(1)} %copy-done.4, bf16[2,512,256]{2,1,0:T(8,128)(2,1)S(1)} %collective-permute-done.19.refs_0_, bf16[2048,6656]{1,0:T(8,128)(2,1)} %refs_1_.29, ...), custom_call_target="tpu_custom_call", output_to_operand_aliasing={{0}: (1, {})} | custom-call | flops 1 | bytes 1 | tf_op jit(solution)/shard_map/pallas_call | solution.py:465
  76.4 2.5 %collective-permute-done.27.refs_0_ = bf16[2,512,256]{2,1,0:T(8,128)(2,1)S(1)} collective-permute-done((bf16[2,512,256]{2,1,0:T(8,128)(2,1)S(1)}, bf16[2,512,256]{2,1,0:T(8,128)(2,1)S(1)}, u32[]{:S(2)}, u32[]{:S(2)}) %collective-permute-start.27) | collective-permute-done | bytes 524320 | tf_op jit(solution)/shard_map/ppermute | solution.py:405
  78.9 1.6 %shard_map.90 = (bf16[2,512,256]{2,1,0:T(8,128)(2,1)S(1)}, bf16[8,128]{1,0:T(8,128)(2,1)S(1)}) custom-call(s32[11]{0:T(128)S(1)} %copy-done.4, bf16[2,512,256]{2,1,0:T(8,128)(2,1)S(1)} %collective-permute-done.27.refs_0_, bf16[2048,6656]{1,0:T(8,128)(2,1)} %refs_1_.29, ...), custom_call_target="tpu_custom_call", output_to_operand_aliasing={{0}: (1, {})} | custom-call | flops 1 | bytes 1 | tf_op jit(solution)/shard_map/pallas_call | solution.py:465
  80.6 3.6 %shard_map.91 = (bf16[8,128]{1,0:T(8,128)(2,1)S(1)}, f32[1024,128]{1,0:T(8,128)S(1)}, f32[512,128]{1,0:T(8,128)S(1)}, bf16[256,6656]{1,0:T(8,128)(2,1)}, bf16[25...) custom-call(s32[11]{0:T(128)S(1)} %copy-done.4, ...), custom_call_target="tpu_custom_call", output_to_operand_aliasing={{1}: (11, {}), {2}: (16, {}), {3}: (17, {})} | custom-call | flops 1 | bytes 1 | tf_op jit(solution)/shard_map/pallas_call | solution.py:550
  84.5 1.6 %shard_map.92 = (bf16[2,512,256]{2,1,0:T(8,128)(2,1)S(1)}, bf16[8,128]{1,0:T(8,128)(2,1)S(1)}) custom-call(s32[11]{0:T(128)S(1)} %copy-done.4, bf16[2,512,256]{2,1,0:T(8,128)(2,1)S(1)} %collective-permute-done.25.refs_0_, bf16[2048,6656]{1,0:T(8,128)(2,1)} %refs_1_.29, ...), custom_call_target="tpu_custom_call", output_to_operand_aliasing={{0}: (1, {})} | custom-call | flops 1 | bytes 1 | tf_op jit(solution)/shard_map/pallas_call | solution.py:465
  86.8 3.3 %collective-permute-done.32.refs_0_ = bf16[2,512,256]{2,1,0:T(8,128)(2,1)S(1)} collective-permute-done((bf16[2,512,256]{2,1,0:T(8,128)(2,1)S(1)}, bf16[2,512,256]{2,1,0:T(8,128)(2,1)S(1)}, u32[]{:S(2)}, u32[]{:S(2)}) %collective-permute-start.32) | collective-permute-done | bytes 524320 | tf_op jit(solution)/shard_map/ppermute | solution.py:405
  91.3 3.4 %shard_map.94 = (bf16[8,128]{1,0:T(8,128)(2,1)S(1)}, f32[1024,128]{1,0:T(8,128)S(1)}, f32[512,128]{1,0:T(8,128)S(1)}, bf16[256,6656]{1,0:T(8,128)(2,1)}, bf16[25...) custom-call(s32[11]{0:T(128)S(1)} %copy-done.4, ...), custom_call_target="tpu_custom_call", output_to_operand_aliasing={{1}: (11, {}), {2}: (16, {}), {3}: (17, {})} | custom-call | flops 1 | bytes 1 | tf_op jit(solution)/shard_map/pallas_call | solution.py:550
  94.8 1.0 collective-permute-done.31.refs_0_
  97.5 3.9 %collective-permute-done.36.refs_0_ = bf16[2,512,256]{2,1,0:T(8,128)(2,1)S(1)} collective-permute-done((bf16[2,512,256]{2,1,0:T(8,128)(2,1)S(1)}, bf16[2,512,256]{2,1,0:T(8,128)(2,1)S(1)}, u32[]{:S(2)}, u32[]{:S(2)}) %collective-permute-start.36) | collective-permute-done | bytes 524320 | tf_op jit(solution)/shard_map/ppermute | solution.py:405
  102.6 3.4 %shard_map.97 = (bf16[8,128]{1,0:T(8,128)(2,1)S(1)}, f32[1024,128]{1,0:T(8,128)S(1)}, f32[512,128]{1,0:T(8,128)S(1)}, bf16[256,6656]{1,0:T(8,128)(2,1)}, bf16[25...) custom-call(s32[11]{0:T(128)S(1)} %copy-done.4, ...), custom_call_target="tpu_custom_call", output_to_operand_aliasing={{1}: (11, {}), {2}: (16, {}), {3}: (17, {})} | custom-call | flops 1 | bytes 1 | tf_op jit(solution)/shard_map/pallas_call | solution.py:550
  106.0 1.0 collective-permute-done.35.refs_0_
  108.7 0.8 collective-permute-done.40.refs_18_
  109.7 2.8 %collective-permute-done.39.refs_9_ = bf16[2,512,256]{2,1,0:T(8,128)(2,1)S(1)} collective-permute-done((bf16[2,512,256]{2,1,0:T(8,128)(2,1)S(1)}, bf16[2,512,256]{2,1,0:T(8,128)(2,1)S(1)}, u32[]{:S(2)}, u32[]{:S(2)}) %collective-permute-start.39) | collective-permute-done | bytes 524320 | tf_op jit(solution)/shard_map/ppermute | solution.py:405
  112.6 3.4 %shard_map.99 = (bf16[8,128]{1,0:T(8,128)(2,1)S(1)}, f32[1024,128]{1,0:T(8,128)S(1)}, f32[512,128]{1,0:T(8,128)S(1)}, bf16[256,6656]{1,0:T(8,128)(2,1)}, bf16[25...) custom-call(s32[11]{0:T(128)S(1)} %copy-done.4, ...), custom_call_target="tpu_custom_call", output_to_operand_aliasing={{1}: (11, {}), {2}: (16, {}), {3}: (17, {})} | custom-call | flops 1 | bytes 1 | tf_op jit(solution)/shard_map/pallas_call | solution.py:550
  116.0 2.2 %collective-permute-done.44.refs_5_ = bf16[2,512,256]{2,1,0:T(8,128)(2,1)S(1)} collective-permute-done((bf16[2,512,256]{2,1,0:T(8,128)(2,1)S(1)}, bf16[2,512,256]{2,1,0:T(8,128)(2,1)S(1)}, u32[]{:S(2)}, u32[]{:S(2)}) %collective-permute-start.44) | collective-permute-done | bytes 524320 | tf_op jit(solution)/shard_map/ppermute | solution.py:405
  118.2 3.2 %shard_map.100 = (bf16[8,128]{1,0:T(8,128)(2,1)}, f32[1024,128]{1,0:T(8,128)S(1)}, f32[512,128]{1,0:T(8,128)S(1)}, bf16[256,6656]{1,0:T(8,128)(2,1)}, bf16[256,2...) custom-call(s32[11]{0:T(128)S(1)} %copy-done.4, ...), custom_call_target="tpu_custom_call", output_to_operand_aliasing={{1}: (7, {}), {2}: (12, {}), {3}: (13, {})} | custom-call | flops 1 | bytes 1 | tf_op jit(solution)/shard_map/pallas_call | solution.py:550
  121.5 1.5 %collective-permute-done.48 = f32[256,256]{1,0:T(8,128)S(1)} collective-permute-done((f32[256,256]{1,0:T(8,128)S(1)}, f32[256,256]{1,0:T(8,128)S(1)}, u32[]{:S(2)}, u32[]{:S(2)}) %collective-permute-start.48) | collective-permute-done | bytes 262176 | tf_op jit(solution)/shard_map/ppermute | solution.py:408
  123.1 3.6 %collective-permute-start.49 = (f32[64,256]{1,0:T(8,128)S(1)}, f32[64,256]{1,0:T(8,128)S(1)}, u32[]{:S(2)}, u32[]{:S(2)}) collective-permute-start(f32[64,256]{1,0:T(8,128)S(1)} %get-tuple-element.187), channel_id=1, source_target_pairs={{0,1},{1,2},{2,3},{3,0},{4,5},{5,6},{6,7},{7,4},{8,9},{9,10},{10,1... | collective-permute-start | bytes 196616 | tf_op jit(solution)/shard_map/ppermute | solution.py:624
  126.7 1.1 collective-permute-start.50
  127.8 2.8 %collective-permute-start.51 = (f32[64,256]{1,0:T(8,128)S(1)}, f32[64,256]{1,0:T(8,128)S(1)}, u32[]{:S(2)}, u32[]{:S(2)}) collective-permute-start(f32[64,256]{1,0:T(8,128)S(1)} %get-tuple-element.188), channel_id=1, source_target_pairs={{0,3},{1,0},{2,1},{3,2},{4,7},{5,4},{6,5},{7,6},{8,11},{9,8},{10,9... | collective-permute-start | bytes 196616 | tf_op jit(solution)/shard_map/ppermute | solution.py:624
  131.2 2.4 %collective-permute-done.50 = f32[64,256]{1,0:T(8,128)S(1)} collective-permute-done((f32[64,256]{1,0:T(8,128)S(1)}, f32[64,256]{1,0:T(8,128)S(1)}, u32[]{:S(2)}, u32[]{:S(2)}) %collective-permute-start.50) | collective-permute-done | bytes 65568 | tf_op jit(solution)/shard_map/ppermute | solution.py:624
  133.6 1.3 collective-permute-start.52
  135.0 1.3 shard_map.101
  136.3 2.8 %collective-permute-start.53 = (f32[64,256]{1,0:T(8,128)S(1)}, f32[64,256]{1,0:T(8,128)S(1)}, u32[]{:S(2)}, u32[]{:S(2)}) collective-permute-start(f32[64,256]{1,0:T(8,128)S(1)} %get-tuple-element.184), channel_id=1, source_target_pairs={{0,2},{1,3},{2,0},{3,1},{4,6},{5,7},{6,4},{7,5},{8,10},{9,11},{10,... | collective-permute-start | bytes 196616 | tf_op jit(solution)/shard_map/ppermute | solution.py:629
  139.9 2.8 %collective-permute-done.53 = f32[64,256]{1,0:T(8,128)S(1)} collective-permute-done((f32[64,256]{1,0:T(8,128)S(1)}, f32[64,256]{1,0:T(8,128)S(1)}, u32[]{:S(2)}, u32[]{:S(2)}) %collective-permute-start.53) | collective-permute-done | bytes 65568 | tf_op jit(solution)/shard_map/ppermute | solution.py:629
  (126 shorter events, 16.8 us)
Async XLA Ops:
  5.9 5.6 %collective-permute-start = (bf16[2,512,256]{2,1,0:T(8,128)(2,1)}, bf16[2,512,256]{2,1,0:T(8,128)(2,1)S(1)}, u32[]{:S(2)}, u32[]{:S(2)}) collective-permute-start(bf16[2,512,256]{2,1,0:T(8,128)(2,1)} %get-tuple-element.94), channel_id=1, source_target_pairs={{0,4},{4,0},{8,12},{12,8},{16,20},{20,16},{24,28},{28,24},{1,5},{5... | collective-permute-start | bytes 1572872 | tf_op jit(solution)/shard_map/ppermute | solution.py:408
  6.4 8.0 %collective-permute-start.4 = (bf16[2,512,256]{2,1,0:T(8,128)(2,1)}, bf16[2,512,256]{2,1,0:T(8,128)(2,1)S(1)}, u32[]{:S(2)}, u32[]{:S(2)}) collective-permute-start(bf16[2,512,256]{2,1,0:T(8,128)(2,1)} %get-tuple-element.98), channel_id=1, source_target_pairs={{0,4},{4,0},{8,12},{12,8},{16,20},{20,16},{24,28},{28,24},{1,5},{5... | collective-permute-start | bytes 1572872 | tf_op jit(solution)/shard_map/ppermute | solution.py:408
  6.5 16.6 %collective-permute-start.3 = (bf16[256,1024]{1,0:T(8,128)(2,1)}, bf16[256,1024]{1,0:T(8,128)(2,1)S(1)}, u32[]{:S(2)}, u32[]{:S(2)}) collective-permute-start(bf16[256,1024]{1,0:T(8,128)(2,1)} %get-tuple-element.97.refs_4_), channel_id=1, source_target_pairs={{0,1},{3,2},{4,5},{7,6},{8,9},{11,10},{12,13},{15,14},{16,17},{19,... | collective-permute-start | bytes 1572872 | tf_op jit(solution)/shard_map/ppermute | solution.py:461
  11.5 11.7 %collective-permute-start.2 = (bf16[2,512,256]{2,1,0:T(8,128)(2,1)}, bf16[2,512,256]{2,1,0:T(8,128)(2,1)S(1)}, u32[]{:S(2)}, u32[]{:S(2)}) collective-permute-start(bf16[2,512,256]{2,1,0:T(8,128)(2,1)} %get-tuple-element.96), channel_id=1, source_target_pairs={{0,4},{4,0},{8,12},{12,8},{16,20},{20,16},{24,28},{28,24},{1,5},{5... | collective-permute-start | bytes 1572872 | tf_op jit(solution)/shard_map/ppermute | solution.py:408
  13.9 9.3 %collective-permute-start.1 = (bf16[2,512,256]{2,1,0:T(8,128)(2,1)S(1)}, bf16[2,512,256]{2,1,0:T(8,128)(2,1)S(1)}, u32[]{:S(2)}, u32[]{:S(2)}) collective-permute-start(bf16[2,512,256]{2,1,0:T(8,128)(2,1)S(1)} %get-tuple-element.95.refs_2_), channel_id=1, source_target_pairs={{0,8},{4,20},{8,24},{12,4},{16,0},{20,28},{24,16},{28,12},{1,9},{5... | collective-permute-start | bytes 1572872 | tf_op jit(solution)/shard_map/ppermute | solution.py:405
  13.9 11.6 %collective-permute-start.8 = (bf16[2,512,256]{2,1,0:T(8,128)(2,1)S(1)}, bf16[2,512,256]{2,1,0:T(8,128)(2,1)S(1)}, u32[]{:S(2)}, u32[]{:S(2)}) collective-permute-start(bf16[2,512,256]{2,1,0:T(8,128)(2,1)S(1)} %copy-done.14), channel_id=1, source_target_pairs={{0,4},{4,0},{8,12},{12,8},{16,20},{20,16},{24,28},{28,24},{1,5},{5... | collective-permute-start | bytes 1572872 | tf_op jit(solution)/shard_map/ppermute | solution.py:408
  16.4 12.3 %collective-permute-start.7 = (bf16[2,512,256]{2,1,0:T(8,128)(2,1)S(1)}, bf16[2,512,256]{2,1,0:T(8,128)(2,1)S(1)}, u32[]{:S(2)}, u32[]{:S(2)}) collective-permute-start(bf16[2,512,256]{2,1,0:T(8,128)(2,1)S(1)} %get-tuple-element.104.refs_6_), channel_id=1, source_target_pairs={{0,8},{4,20},{8,24},{12,4},{16,0},{20,28},{24,16},{28,12},{1,9},{5... | collective-permute-start | bytes 1572872 | tf_op jit(solution)/shard_map/ppermute | solution.py:405
  23.2 8.0 %collective-permute-start.6 = (bf16[2,512,256]{2,1,0:T(8,128)(2,1)S(1)}, bf16[2,512,256]{2,1,0:T(8,128)(2,1)S(1)}, u32[]{:S(2)}, u32[]{:S(2)}) collective-permute-start(bf16[2,512,256]{2,1,0:T(8,128)(2,1)S(1)} %copy-done.13), channel_id=1, source_target_pairs={{0,4},{4,0},{8,12},{12,8},{16,20},{20,16},{24,28},{28,24},{1,5},{5... | collective-permute-start | bytes 1572872 | tf_op jit(solution)/shard_map/ppermute | solution.py:408
  24.9 9.4 %collective-permute-start.5 = (bf16[2,512,256]{2,1,0:T(8,128)(2,1)S(1)}, bf16[2,512,256]{2,1,0:T(8,128)(2,1)S(1)}, u32[]{:S(2)}, u32[]{:S(2)}) collective-permute-start(bf16[2,512,256]{2,1,0:T(8,128)(2,1)S(1)} %get-tuple-element.102.refs_3_.refs_10_), channel_id=1, source_target_pairs={{0,8},{4,20},{8,24},{12,4},{16,0},{20,28},{24,16},{28,12},{1,9},{5... | collective-permute-start | bytes 1572872 | tf_op jit(solution)/shard_map/ppermute | solution.py:405
  25.0 11.0 %collective-permute-start.12 = (bf16[2,512,256]{2,1,0:T(8,128)(2,1)S(1)}, bf16[2,512,256]{2,1,0:T(8,128)(2,1)S(1)}, u32[]{:S(2)}, u32[]{:S(2)}) collective-permute-start(bf16[2,512,256]{2,1,0:T(8,128)(2,1)S(1)} %copy-done.12), channel_id=1, source_target_pairs={{0,4},{4,0},{8,12},{12,8},{16,20},{20,16},{24,28},{28,24},{1,5},{5... | collective-permute-start | bytes 1572872 | tf_op jit(solution)/shard_map/ppermute | solution.py:408
  30.3 9.6 %collective-permute-start.11 = (bf16[2,512,256]{2,1,0:T(8,128)(2,1)S(1)}, bf16[2,512,256]{2,1,0:T(8,128)(2,1)S(1)}, u32[]{:S(2)}, u32[]{:S(2)}) collective-permute-start(bf16[2,512,256]{2,1,0:T(8,128)(2,1)S(1)} %get-tuple-element.110.refs_7_.refs_14_), channel_id=1, source_target_pairs={{0,8},{4,20},{8,24},{12,4},{16,0},{20,28},{24,16},{28,12},{1,9},{5... | collective-permute-start | bytes 1572872 | tf_op jit(solution)/shard_map/ppermute | solution.py:405
  30.4 9.5 %collective-permute-start.13 = (bf16[256,1024]{1,0:T(8,128)(2,1)S(1)}, bf16[256,1024]{1,0:T(8,128)(2,1)S(1)}, u32[]{:S(2)}, u32[]{:S(2)}) collective-permute-start(bf16[256,1024]{1,0:T(8,128)(2,1)S(1)} %get-tuple-element.112.refs_4_), channel_id=1, source_target_pairs={{1,2},{2,1},{5,6},{6,5},{9,10},{10,9},{13,14},{14,13},{17,18},{18,... | collective-permute-start | bytes 1572872 | tf_op jit(solution)/shard_map/ppermute | solution.py:461
  31.1 35.7 %collective-permute-start.24 = (bf16[256,3328]{1,0:T(8,128)(2,1)S(1)}, bf16[256,3328]{1,0:T(8,128)(2,1)S(1)}, u32[]{:S(2)}, u32[]{:S(2)}) collective-permute-start(bf16[256,3328]{1,0:T(8,128)(2,1)S(1)} %get-tuple-element.130), channel_id=1, source_target_pairs={{0,4},{4,0},{8,12},{12,8},{16,20},{20,16},{24,28},{28,24},{1,5},{5... | collective-permute-start | bytes 5111816 | tf_op jit(solution)/shard_map/ppermute | solution.py:408
  34.3 7.4 %collective-permute-start.10 = (bf16[2,512,256]{2,1,0:T(8,128)(2,1)S(1)}, bf16[2,512,256]{2,1,0:T(8,128)(2,1)S(1)}, u32[]{:S(2)}, u32[]{:S(2)}) collective-permute-start(bf16[2,512,256]{2,1,0:T(8,128)(2,1)S(1)} %copy-done.11), channel_id=1, source_target_pairs={{0,4},{4,0},{8,12},{12,8},{16,20},{20,16},{24,28},{28,24},{1,5},{5... | collective-permute-start | bytes 1572872 | tf_op jit(solution)/shard_map/ppermute | solution.py:408
  36.0 9.6 %collective-permute-start.9 = (bf16[2,512,256]{2,1,0:T(8,128)(2,1)S(1)}, bf16[2,512,256]{2,1,0:T(8,128)(2,1)S(1)}, u32[]{:S(2)}, u32[]{:S(2)}) collective-permute-start(bf16[2,512,256]{2,1,0:T(8,128)(2,1)S(1)} %get-tuple-element.108.refs_4_.refs_11_.refs_2_), channel_id=1, source_target_pairs={{0,8},{4,20},{8,24},{12,4},{16,0},{20,28},{24,16},{28,12},{1,9},{5... | collective-permute-start | bytes 1572872 | tf_op jit(solution)/shard_map/ppermute | solution.py:405
  39.9 8.6 %collective-permute-start.18 = (bf16[2,512,256]{2,1,0:T(8,128)(2,1)S(1)}, bf16[2,512,256]{2,1,0:T(8,128)(2,1)S(1)}, u32[]{:S(2)}, u32[]{:S(2)}) collective-permute-start(bf16[2,512,256]{2,1,0:T(8,128)(2,1)S(1)} %copy-done.10), channel_id=1, source_target_pairs={{0,4},{4,0},{8,12},{12,8},{16,20},{20,16},{24,28},{28,24},{1,5},{5... | collective-permute-start | bytes 1572872 | tf_op jit(solution)/shard_map/ppermute | solution.py:408
  41.7 9.5 %collective-permute-start.17 = (bf16[2,512,256]{2,1,0:T(8,128)(2,1)S(1)}, bf16[2,512,256]{2,1,0:T(8,128)(2,1)S(1)}, u32[]{:S(2)}, u32[]{:S(2)}) collective-permute-start(bf16[2,512,256]{2,1,0:T(8,128)(2,1)S(1)} %get-tuple-element.118.refs_8_.refs_15_.refs_6_), channel_id=1, source_target_pairs={{0,8},{4,20},{8,24},{12,4},{16,0},{20,28},{24,16},{28,12},{1,9},{5... | collective-permute-start | bytes 1572872 | tf_op jit(solution)/shard_map/ppermute | solution.py:405
  41.7 11.1 %collective-permute-start.15 = (bf16[2,512,256]{2,1,0:T(8,128)(2,1)S(1)}, bf16[2,512,256]{2,1,0:T(8,128)(2,1)S(1)}, u32[]{:S(2)}, u32[]{:S(2)}) collective-permute-start(bf16[2,512,256]{2,1,0:T(8,128)(2,1)S(1)} %copy-done.9), channel_id=1, source_target_pairs={{0,4},{4,0},{8,12},{12,8},{16,20},{20,16},{24,28},{28,24},{1,5},{5... | collective-permute-start | bytes 1572872 | tf_op jit(solution)/shard_map/ppermute | solution.py:408
  45.6 16.2 %collective-permute-start.16 = (bf16[256,1024]{1,0:T(8,128)(2,1)S(1)}, bf16[256,1024]{1,0:T(8,128)(2,1)S(1)}, u32[]{:S(2)}, u32[]{:S(2)}) collective-permute-start(bf16[256,1024]{1,0:T(8,128)(2,1)S(1)} %get-tuple-element.117.refs_4_), channel_id=1, source_target_pairs={{1,0},{2,3},{5,4},{6,7},{9,8},{10,11},{13,12},{14,15},{17,16},{18,... | collective-permute-start | bytes 1572872 | tf_op jit(solution)/shard_map/ppermute | solution.py:461
  48.5 13.3 %collective-permute-start.14 = (bf16[2,512,256]{2,1,0:T(8,128)(2,1)S(1)}, bf16[2,512,256]{2,1,0:T(8,128)(2,1)S(1)}, u32[]{:S(2)}, u32[]{:S(2)}) collective-permute-start(bf16[2,512,256]{2,1,0:T(8,128)(2,1)S(1)} %get-tuple-element.115.refs_5_.refs_12_.refs_3_.refs_2_), channel_id=1, source_target_pairs={{0,8},{4,20},{8,24},{12,4},{16,0},{20,28},{24,16},{28,12},{1,9},{5... | collective-permute-start | bytes 1572872 | tf_op jit(solution)/shard_map/ppermute | solution.py:405
  51.2 12.9 %collective-permute-start.22 = (bf16[2,512,256]{2,1,0:T(8,128)(2,1)S(1)}, bf16[2,512,256]{2,1,0:T(8,128)(2,1)S(1)}, u32[]{:S(2)}, u32[]{:S(2)}) collective-permute-start(bf16[2,512,256]{2,1,0:T(8,128)(2,1)S(1)} %copy-done.8), channel_id=1, source_target_pairs={{0,4},{4,0},{8,12},{12,8},{16,20},{20,16},{24,28},{28,24},{1,5},{5... | collective-permute-start | bytes 1572872 | tf_op jit(solution)/shard_map/ppermute | solution.py:408
  52.8 11.2 %collective-permute-start.21 = (bf16[2,512,256]{2,1,0:T(8,128)(2,1)S(1)}, bf16[2,512,256]{2,1,0:T(8,128)(2,1)S(1)}, u32[]{:S(2)}, u32[]{:S(2)}) collective-permute-start(bf16[2,512,256]{2,1,0:T(8,128)(2,1)S(1)} %get-tuple-element.124.refs_9_.refs_16_.refs_7_.refs_6_), channel_id=1, source_target_pairs={{0,8},{4,20},{8,24},{12,4},{16,0},{20,28},{24,16},{28,12},{1,9},{5... | collective-permute-start | bytes 1572872 | tf_op jit(solution)/shard_map/ppermute | solution.py:405
  63.6 10.0 %collective-permute-start.20 = (bf16[2,512,256]{2,1,0:T(8,128)(2,1)S(1)}, bf16[2,512,256]{2,1,0:T(8,128)(2,1)S(1)}, u32[]{:S(2)}, u32[]{:S(2)}) collective-permute-start(bf16[2,512,256]{2,1,0:T(8,128)(2,1)S(1)} %copy-done.7), channel_id=1, source_target_pairs={{0,4},{4,0},{8,12},{12,8},{16,20},{20,16},{24,28},{28,24},{1,5},{5... | collective-permute-start | bytes 1572872 | tf_op jit(solution)/shard_map/ppermute | solution.py:408
  64.1 9.5 %collective-permute-start.19 = (bf16[2,512,256]{2,1,0:T(8,128)(2,1)S(1)}, bf16[2,512,256]{2,1,0:T(8,128)(2,1)S(1)}, u32[]{:S(2)}, u32[]{:S(2)}) collective-permute-start(bf16[2,512,256]{2,1,0:T(8,128)(2,1)S(1)} %get-tuple-element.122.refs_13_.refs_4_.refs_3_.refs_2_), channel_id=1, source_target_pairs={{0,8},{4,20},{8,24},{12,4},{16,0},{20,28},{24,16},{28,12},{1,9},{5... | collective-permute-start | bytes 1572872 | tf_op jit(solution)/shard_map/ppermute | solution.py:405
  64.1 12.3 %collective-permute-start.28 = (bf16[2,512,256]{2,1,0:T(8,128)(2,1)S(1)}, bf16[2,512,256]{2,1,0:T(8,128)(2,1)S(1)}, u32[]{:S(2)}, u32[]{:S(2)}) collective-permute-start(bf16[2,512,256]{2,1,0:T(8,128)(2,1)S(1)} %copy-done.6), channel_id=1, source_target_pairs={{0,4},{4,0},{8,12},{12,8},{16,20},{20,16},{24,28},{28,24},{1,5},{5... | collective-permute-start | bytes 1572872 | tf_op jit(solution)/shard_map/ppermute | solution.py:408
  66.8 12.1 %collective-permute-start.27 = (bf16[2,512,256]{2,1,0:T(8,128)(2,1)S(1)}, bf16[2,512,256]{2,1,0:T(8,128)(2,1)S(1)}, u32[]{:S(2)}, u32[]{:S(2)}) collective-permute-start(bf16[2,512,256]{2,1,0:T(8,128)(2,1)S(1)} %get-tuple-element.127.refs_17_.refs_8_.refs_7_.refs_6_), channel_id=1, source_target_pairs={{0,8},{4,20},{8,24},{12,4},{16,0},{20,28},{24,16},{28,12},{1,9},{5... | collective-permute-start | bytes 1572872 | tf_op jit(solution)/shard_map/ppermute | solution.py:405
  66.9 17.3 %collective-permute-start.26 = (bf16[2,512,256]{2,1,0:T(8,128)(2,1)S(1)}, bf16[2,512,256]{2,1,0:T(8,128)(2,1)S(1)}, u32[]{:S(2)}, u32[]{:S(2)}) collective-permute-start(bf16[2,512,256]{2,1,0:T(8,128)(2,1)S(1)} %copy-done.5), channel_id=1, source_target_pairs={{0,4},{4,0},{8,12},{12,8},{16,20},{20,16},{24,28},{28,24},{1,5},{5... | collective-permute-start | bytes 1572872 | tf_op jit(solution)/shard_map/ppermute | solution.py:408
  75.3 9.2 %collective-permute-start.25 = (bf16[2,512,256]{2,1,0:T(8,128)(2,1)S(1)}, bf16[2,512,256]{2,1,0:T(8,128)(2,1)S(1)}, u32[]{:S(2)}, u32[]{:S(2)}) collective-permute-start(bf16[2,512,256]{2,1,0:T(8,128)(2,1)S(1)} %get-tuple-element.132.refs_5_.refs_4_.refs_3_.refs_2_), channel_id=1, source_target_pairs={{0,8},{4,20},{8,24},{12,4},{16,0},{20,28},{24,16},{28,12},{1,9},{5... | collective-permute-start | bytes 1572872 | tf_op jit(solution)/shard_map/ppermute | solution.py:405
  75.9 4.7 %collective-permute-start.29 = (bf16[256,256]{1,0:T(8,128)(2,1)S(1)}, bf16[256,256]{1,0:T(8,128)(2,1)S(1)}, u32[]{:S(2)}, u32[]{:S(2)}) collective-permute-start(bf16[256,256]{1,0:T(8,128)(2,1)S(1)} %get-tuple-element.141), channel_id=1, source_target_pairs={{0,4},{4,0},{8,12},{12,8},{16,20},{20,16},{24,28},{28,24},{1,5},{5... | collective-permute-start | bytes 393224 | tf_op jit(solution)/shard_map/ppermute | solution.py:408
  80.5 9.6 %collective-permute-start.32 = (bf16[2,512,256]{2,1,0:T(8,128)(2,1)S(1)}, bf16[2,512,256]{2,1,0:T(8,128)(2,1)S(1)}, u32[]{:S(2)}, u32[]{:S(2)}) collective-permute-start(bf16[2,512,256]{2,1,0:T(8,128)(2,1)S(1)} %get-tuple-element.136.refs_9_.refs_8_.refs_7_.refs_6_), channel_id=1, source_target_pairs={{0,8},{4,20},{8,24},{12,4},{16,0},{20,28},{24,16},{28,12},{1,9},{5... | collective-permute-start | bytes 1572872 | tf_op jit(solution)/shard_map/ppermute | solution.py:405
  86.1 9.6 %collective-permute-start.31 = (bf16[2,512,256]{2,1,0:T(8,128)(2,1)S(1)}, bf16[2,512,256]{2,1,0:T(8,128)(2,1)S(1)}, u32[]{:S(2)}, u32[]{:S(2)}) collective-permute-start(bf16[2,512,256]{2,1,0:T(8,128)(2,1)S(1)} %get-tuple-element.144.refs_5_.refs_4_.refs_3_.refs_2_), channel_id=1, source_target_pairs={{0,8},{4,20},{8,24},{12,4},{16,0},{20,28},{24,16},{28,12},{1,9},{5... | collective-permute-start | bytes 1572872 | tf_op jit(solution)/shard_map/ppermute | solution.py:405
  86.2 5.1 %collective-permute-start.33 = (bf16[256,256]{1,0:T(8,128)(2,1)S(1)}, bf16[256,256]{1,0:T(8,128)(2,1)S(1)}, u32[]{:S(2)}, u32[]{:S(2)}) collective-permute-start(bf16[256,256]{1,0:T(8,128)(2,1)S(1)} %get-tuple-element.151), channel_id=1, source_target_pairs={{0,4},{4,0},{8,12},{12,8},{16,20},{20,16},{24,28},{28,24},{1,5},{5... | collective-permute-start | bytes 393224 | tf_op jit(solution)/shard_map/ppermute | solution.py:408
  86.3 5.1 %collective-permute-start.34 = (bf16[256,256]{1,0:T(8,128)(2,1)S(1)}, bf16[256,256]{1,0:T(8,128)(2,1)S(1)}, u32[]{:S(2)}, u32[]{:S(2)}) collective-permute-start(bf16[256,256]{1,0:T(8,128)(2,1)S(1)} %get-tuple-element.152), channel_id=1, source_target_pairs={{0,4},{4,0},{8,12},{12,8},{16,20},{20,16},{24,28},{28,24},{1,5},{5... | collective-permute-start | bytes 393224 | tf_op jit(solution)/shard_map/ppermute | solution.py:408
  90.7 10.6 %collective-permute-start.36 = (bf16[2,512,256]{2,1,0:T(8,128)(2,1)S(1)}, bf16[2,512,256]{2,1,0:T(8,128)(2,1)S(1)}, u32[]{:S(2)}, u32[]{:S(2)}) collective-permute-start(bf16[2,512,256]{2,1,0:T(8,128)(2,1)S(1)} %get-tuple-element.146.refs_9_.refs_8_.refs_7_), channel_id=1, source_target_pairs={{0,8},{4,20},{8,24},{12,4},{16,0},{20,28},{24,16},{28,12},{1,9},{5... | collective-permute-start | bytes 1572872 | tf_op jit(solution)/shard_map/ppermute | solution.py:405
  96.3 10.6 %collective-permute-start.35 = (bf16[2,512,256]{2,1,0:T(8,128)(2,1)S(1)}, bf16[2,512,256]{2,1,0:T(8,128)(2,1)S(1)}, u32[]{:S(2)}, u32[]{:S(2)}) collective-permute-start(bf16[2,512,256]{2,1,0:T(8,128)(2,1)S(1)} %get-tuple-element.154.refs_5_.refs_4_.refs_3_), channel_id=1, source_target_pairs={{0,8},{4,20},{8,24},{12,4},{16,0},{20,28},{24,16},{28,12},{1,9},{5... | collective-permute-start | bytes 1572872 | tf_op jit(solution)/shard_map/ppermute | solution.py:405
  97.0 5.6 %collective-permute-start.37 = (bf16[256,256]{1,0:T(8,128)(2,1)S(1)}, bf16[256,256]{1,0:T(8,128)(2,1)S(1)}, u32[]{:S(2)}, u32[]{:S(2)}) collective-permute-start(bf16[256,256]{1,0:T(8,128)(2,1)S(1)} %get-tuple-element.161), channel_id=1, source_target_pairs={{0,4},{4,0},{8,12},{12,8},{16,20},{20,16},{24,28},{28,24},{1,5},{5... | collective-permute-start | bytes 393224 | tf_op jit(solution)/shard_map/ppermute | solution.py:408
  97.0 5.6 %collective-permute-start.38 = (bf16[256,256]{1,0:T(8,128)(2,1)S(1)}, bf16[256,256]{1,0:T(8,128)(2,1)S(1)}, u32[]{:S(2)}, u32[]{:S(2)}) collective-permute-start(bf16[256,256]{1,0:T(8,128)(2,1)S(1)} %get-tuple-element.162), channel_id=1, source_target_pairs={{0,4},{4,0},{8,12},{12,8},{16,20},{20,16},{24,28},{28,24},{1,5},{5... | collective-permute-start | bytes 393224 | tf_op jit(solution)/shard_map/ppermute | solution.py:408
  102.0 10.6 %collective-permute-start.39 = (bf16[2,512,256]{2,1,0:T(8,128)(2,1)S(1)}, bf16[2,512,256]{2,1,0:T(8,128)(2,1)S(1)}, u32[]{:S(2)}, u32[]{:S(2)}) collective-permute-start(bf16[2,512,256]{2,1,0:T(8,128)(2,1)S(1)} %get-tuple-element.156.refs_9_.refs_8_), channel_id=1, source_target_pairs={{0,8},{4,20},{8,24},{12,4},{16,0},{20,28},{24,16},{28,12},{1,9},{5... | collective-permute-start | bytes 1572872 | tf_op jit(solution)/shard_map/ppermute | solution.py:405
  107.6 10.6 %collective-permute-start.44 = (bf16[2,512,256]{2,1,0:T(8,128)(2,1)S(1)}, bf16[2,512,256]{2,1,0:T(8,128)(2,1)S(1)}, u32[]{:S(2)}, u32[]{:S(2)}) collective-permute-start(bf16[2,512,256]{2,1,0:T(8,128)(2,1)S(1)} %get-tuple-element.164.refs_5_.refs_4_), channel_id=1, source_target_pairs={{0,8},{4,20},{8,24},{12,4},{16,0},{20,28},{24,16},{28,12},{1,9},{5... | collective-permute-start | bytes 1572872 | tf_op jit(solution)/shard_map/ppermute | solution.py:405
  108.7 7.3 %collective-permute-start.45 = (bf16[256,256]{1,0:T(8,128)(2,1)S(1)}, bf16[256,256]{1,0:T(8,128)(2,1)S(1)}, u32[]{:S(2)}, u32[]{:S(2)}) collective-permute-start(bf16[256,256]{1,0:T(8,128)(2,1)S(1)} %get-tuple-element.177), channel_id=1, source_target_pairs={{0,4},{4,0},{8,12},{12,8},{16,20},{20,16},{24,28},{28,24},{1,5},{5... | collective-permute-start | bytes 393224 | tf_op jit(solution)/shard_map/ppermute | solution.py:408
  109.5 6.5 %collective-permute-start.46 = (bf16[256,256]{1,0:T(8,128)(2,1)S(1)}, bf16[256,256]{1,0:T(8,128)(2,1)S(1)}, u32[]{:S(2)}, u32[]{:S(2)}) collective-permute-start(bf16[256,256]{1,0:T(8,128)(2,1)S(1)} %get-tuple-element.178), channel_id=1, source_target_pairs={{0,4},{4,0},{8,12},{12,8},{16,20},{20,16},{24,28},{28,24},{1,5},{5... | collective-permute-start | bytes 393224 | tf_op jit(solution)/shard_map/ppermute | solution.py:408
  123.1 8.1 %collective-permute-start.49 = (f32[64,256]{1,0:T(8,128)S(1)}, f32[64,256]{1,0:T(8,128)S(1)}, u32[]{:S(2)}, u32[]{:S(2)}) collective-permute-start(f32[64,256]{1,0:T(8,128)S(1)} %get-tuple-element.187), channel_id=1, source_target_pairs={{0,1},{1,2},{2,3},{3,0},{4,5},{5,6},{6,7},{7,4},{8,9},{9,10},{10,1... | collective-permute-start | bytes 196616 | tf_op jit(solution)/shard_map/ppermute | solution.py:624
  126.7 6.9 %collective-permute-start.50 = (f32[64,256]{1,0:T(8,128)S(1)}, f32[64,256]{1,0:T(8,128)S(1)}, u32[]{:S(2)}, u32[]{:S(2)}) collective-permute-start(f32[64,256]{1,0:T(8,128)S(1)} %get-tuple-element.189), channel_id=1, source_target_pairs={{0,2},{1,3},{2,0},{3,1},{4,6},{5,7},{6,4},{7,5},{8,10},{9,11},{10,... | collective-permute-start | bytes 196616 | tf_op jit(solution)/shard_map/ppermute | solution.py:624
  127.8 5.8 %collective-permute-start.51 = (f32[64,256]{1,0:T(8,128)S(1)}, f32[64,256]{1,0:T(8,128)S(1)}, u32[]{:S(2)}, u32[]{:S(2)}) collective-permute-start(f32[64,256]{1,0:T(8,128)S(1)} %get-tuple-element.188), channel_id=1, source_target_pairs={{0,3},{1,0},{2,1},{3,2},{4,7},{5,4},{6,5},{7,6},{8,11},{9,8},{10,9... | collective-permute-start | bytes 196616 | tf_op jit(solution)/shard_map/ppermute | solution.py:624
  130.7 4.3 %collective-permute-start.42 = (bf16[256,256]{1,0:T(8,128)(2,1)S(1)}, bf16[256,256]{1,0:T(8,128)(2,1)S(1)}, u32[]{:S(2)}, u32[]{:S(2)}) collective-permute-start(bf16[256,256]{1,0:T(8,128)(2,1)S(1)} %get-tuple-element.171), channel_id=1, source_target_pairs={{0,4},{4,0},{8,12},{12,8},{16,20},{20,16},{24,28},{28,24},{1,5},{5... | collective-permute-start | bytes 393224 | tf_op jit(solution)/shard_map/ppermute | solution.py:408
  130.7 4.3 %collective-permute-start.43 = (bf16[256,256]{1,0:T(8,128)(2,1)S(1)}, bf16[256,256]{1,0:T(8,128)(2,1)S(1)}, u32[]{:S(2)}, u32[]{:S(2)}) collective-permute-start(bf16[256,256]{1,0:T(8,128)(2,1)S(1)} %get-tuple-element.172), channel_id=1, source_target_pairs={{0,4},{4,0},{8,12},{12,8},{16,20},{20,16},{24,28},{28,24},{1,5},{5... | collective-permute-start | bytes 393224 | tf_op jit(solution)/shard_map/ppermute | solution.py:408
  133.6 6.2 %collective-permute-start.52 = (f32[64,256]{1,0:T(8,128)S(1)}, f32[64,256]{1,0:T(8,128)S(1)}, u32[]{:S(2)}, u32[]{:S(2)}) collective-permute-start(f32[64,256]{1,0:T(8,128)S(1)} %get-tuple-element.184), channel_id=1, source_target_pairs={{0,1},{1,2},{2,3},{3,0},{4,5},{5,6},{6,7},{7,4},{8,9},{9,10},{10,1... | collective-permute-start | bytes 196616 | tf_op jit(solution)/shard_map/ppermute | solution.py:629
  136.3 6.3 %collective-permute-start.53 = (f32[64,256]{1,0:T(8,128)S(1)}, f32[64,256]{1,0:T(8,128)S(1)}, u32[]{:S(2)}, u32[]{:S(2)}) collective-permute-start(f32[64,256]{1,0:T(8,128)S(1)} %get-tuple-element.184), channel_id=1, source_target_pairs={{0,2},{1,3},{2,0},{3,1},{4,6},{5,7},{6,4},{7,5},{8,10},{9,11},{10,... | collective-permute-start | bytes 196616 | tf_op jit(solution)/shard_map/ppermute | solution.py:629
  (22 other events, 67.8 us)
